TPU v7x, 256 devices: a whole 4x4x8 slice. The times are simulated.
256 devices in a mesh: section: 2 (over y_lo), ctx: 64 (over z, x, y_hi), mp: 2 (over core).
Axes of the slice: x: 4, y: 4 (y_hi: 2, y_lo: 2; y = y_hi * 2 + y_lo), z: 8, core: 2. Of those that a mesh axis runs over, the one named last changes fastest.
Arguments:
- depth_logits: float32 [2, 32768, 41], P('section', ('ctx', 'mp')), may hold values from -20 to 320
- features: bfloat16 [2, 32768, 64], P('section', ('ctx', 'mp')), may hold values from -6 to 6
- cell_index: int32 [2, 32768, 41], P('section', ('ctx', 'mp')), may hold values from 0 to 511
- embed: bfloat16 [32768, 8192], P('ctx', ('section', 'mp')), may hold values from -6 to 6
- w_visual: bfloat16 [64, 8192], P(None, ('section', 'mp')), may hold values from -0.75 to 0.75
- w_gate: bfloat16 [64, 8192], P(None, ('section', 'mp')), may hold values from -0.75 to 0.75
- input_map: bfloat16 [32768, 128], P('ctx'), may hold values from -0.5 to 0.5
- output_map: bfloat16 [32768, 128], P('ctx'), may hold values from -0.5 to 0.5
- forget: float32 [32768, 64], P('ctx', ('section', 'mp')), may hold values from 0 to 1
- skip: float32 [64], P(('section', 'mp')), may hold values from 0.5 to 6
- frame_ids: int32 [32768], P('ctx'), may hold values from 0 to 681, never falling along the last dimension, each value on 1 to 96 neighbouring positions
- norm_gain: float32 [8192], P(('section', 'mp')), may hold values from 0.1 to 1.9
Outputs:
- layer_out: bfloat16 [32768, 8192], P('ctx', ('section', 'mp'))
Inputs may be any that keep to these rules, and one draw needn't show every extreme that they name: `frame_ids`: frame numbers never fall along the sequence; a frame holds at most 96 tokens.
All inputs are finite; a program needn't handle non-finite values.
Results may differ from a plain program's by a relative error of at most 0.0033.
The roundings to bfloat16 on the way count: a program that leaves them out, or rounds other values in their place, can miss the bound.
Values sent between devices are 32-bit elements; how exact they have to be, the bound alone decides.
No kernel may reach another device: no remote copies, remote signals or barrier semaphores. Data moves between devices by JAX's collectives and lax.ppermute only.
A program may use at most 192 MiB of HBM per device.

v0:
```python
import jax
import jax.numpy as jnp
from jax import lax
from jax.sharding import PartitionSpec as P

P_SIZE = 128
N = 128
BLK = 256
CF = 64
DI = 8192


EPSILON = 1e-05


def entering_2(value, axis, combine, identity):
    count, here = (lax.axis_size(axis), lax.axis_index(axis))
    everything = jax.tree.map(lambda part: lax.all_gather(part, axis), value)
    start = jax.tree.map(
        lambda part, zero: jnp.broadcast_to(jnp.asarray(zero, part.dtype), part.shape),
        value,
        identity,
    )

    def step(k, before):
        reached = k < here
        new = combine(before, jax.tree.map(lambda part: part[k], everything))
        return jax.tree.map(lambda a, b: jnp.where(reached, a, b), new, before)

    return lax.fori_loop(0, count, step, start)


def link_states(earlier, later):
    decay_early, state_early = earlier
    decay_late, state_late = later
    return (decay_early * decay_late, decay_late[:, None, None] * state_early + state_late)


def local_chain(keys_scaled, streams, block_ends):
    block_state = jnp.einsum(
        "bshn,bshp->bhnp", keys_scaled, streams, preferred_element_type=jnp.float32
    )
    running = jnp.zeros(block_state.shape[1:], jnp.float32)
    starts = []
    for token_position in range(block_state.shape[0]):
        starts.append(running)
        running = (
            jnp.exp(-block_ends[token_position])[:, None, None] * running
            + block_state[token_position]
        )
    return (jnp.stack(starts), running)


def body(
    depth_logits,
    features,
    cell_index,
    embed,
    w_visual,
    w_gate,
    input_map,
    output_map,
    forget,
    skip,
    frame_ids,
    norm_gain,
):
    tok_rows = embed.shape[0]
    head_count = forget.shape[1]
    blocks = tok_rows // BLK
    highest = lax.Precision.HIGHEST
    probability = jax.nn.softmax(depth_logits[0], axis=-1)
    lifted = probability[:, :, None] * features[0][:, None, :].astype(jnp.float32)
    partial_sum = jax.ops.segment_sum(
        lifted.reshape(-1, CF), cell_index[0].reshape(-1), num_segments=tok_rows
    )
    pooled = lax.psum(partial_sum, ("section", "mp"))
    visual_part = jnp.dot(pooled, w_visual.astype(jnp.float32), precision=highest)
    stream = (embed.astype(jnp.float32) + visual_part).astype(jnp.bfloat16)
    gate_act = jnp.dot(pooled, w_gate.astype(jnp.float32), precision=highest)
    streams = stream.reshape(blocks, BLK, head_count, P_SIZE)
    cumulative = jnp.cumsum(forget.reshape(blocks, BLK, head_count), axis=1)
    block_ends = cumulative[:, -1, :]
    read_rows = output_map.reshape(blocks, BLK, N)
    writes = input_map.reshape(blocks, BLK, N)
    frames = frame_ids.reshape(blocks, BLK)
    scores = jnp.einsum("btn,bsn->bts", read_rows, writes, preferred_element_type=jnp.float32)
    row_order = lax.broadcasted_iota(jnp.int32, (BLK, BLK), 0)
    col_order = lax.broadcasted_iota(jnp.int32, (BLK, BLK), 1)
    visible = (col_order <= row_order)[None] | (frames[:, :, None] == frames[:, None, :])
    distance = jnp.abs(cumulative[:, :, None, :] - cumulative[:, None, :, :])
    weights = jnp.where(visible[..., None], scores[..., None] * jnp.exp(-distance), 0.0).astype(
        jnp.bfloat16
    )
    within = jnp.einsum("btsh,bshp->bthp", weights, streams, preferred_element_type=jnp.float32)
    keys_scaled = (
        jnp.exp(cumulative - block_ends[:, None, :])[..., None]
        * writes.astype(jnp.float32)[:, :, None, :]
    ).astype(jnp.bfloat16)
    reads_scaled = read_rows.astype(jnp.float32)[:, :, None, :] * jnp.exp(-cumulative)[..., None]
    shard_decay = jnp.exp(-jnp.sum(block_ends, axis=0))
    before = jnp.exp(block_ends - jnp.cumsum(block_ends, axis=0))
    starts, running = local_chain(keys_scaled, streams, block_ends)
    incoming = entering_2(
        (shard_decay, running),
        "ctx",
        link_states,
        (jnp.ones_like(shard_decay), jnp.zeros_like(running)),
    )[1]
    entering = starts + before[:, :, None, None] * incoming[None]
    carried = jnp.einsum("bthn,bhnp->bthp", reads_scaled, entering, precision=highest)
    mixed = within + carried + skip[None, None, :, None] * streams.astype(jnp.float32)
    gated_out = mixed.reshape(tok_rows, head_count * P_SIZE) * jax.nn.silu(gate_act)
    energy = lax.psum(jnp.sum(gated_out * gated_out, axis=1), ("section", "mp"))
    inverse = lax.rsqrt(energy / DI + EPSILON)
    return (gated_out * inverse[:, None] * norm_gain[None, :]).astype(jnp.bfloat16)


def solution(mesh):
    return jax.shard_map(
        body,
        mesh=mesh,
        in_specs=(
            P("section", ("ctx", "mp"), None),
            P("section", ("ctx", "mp"), None),
            P("section", ("ctx", "mp"), None),
            P("ctx", ("section", "mp")),
            P(None, ("section", "mp")),
            P(None, ("section", "mp")),
            P("ctx", None),
            P("ctx", None),
            P("ctx", ("section", "mp")),
            P(("section", "mp")),
            P("ctx"),
            P(("section", "mp")),
        ),
        out_specs=P("ctx", ("section", "mp")),
        check_vma=False,
    )
```

profile of v0, /device:TPU:1, one launch (start us, length us, event | category | flops | bytes accessed | tf_op | source)
XLA Modules:
  0.0 893.5 jit_solution(2292289003036691882)
XLA Ops:
  10.7 4.5 mul.143
  15.2 6.2 mul.144
  21.4 1.7 broadcast_multiply_fusion
  23.2 5.4 copy.51
  28.9 58.7 %scatter_custom_fusion = f32[512,64]{1,0:T(8,128)} fusion(s32[10496]{0:T(1024)S(1)} %reshape.157, f32[10496,64]{1,0:T(8,128)} %copy.51, f32[]{:T(128)} %constant.44.clone.1), kind=kCustom, calls=%fused_computation.35 | custom fusion | flops 671744 | bytes 131584 | tf_op jit(solution)/shard_map/scatter-add | solution.py:74
  90.9 42.3 %all-reduce.4.cloned.1.call-done = f32[512,64]{1,0:T(8,128)} async-done(((f32[512,64]{1,0:T(8,128)}), f32[512,64]{1,0:T(8,128)}) %all-reduce.4.cloned.1.call-update) | async-done | bytes 131088 | tf_op jit(solution)/shard_map/psum | solution.py:77
  133.3 2.8 fusion.19
  136.1 2.0 copy.66
  138.1 3.0 copy.55
  141.8 1.6 slice_add_fusion
  145.5 158.7 %all-reduce.1 = f32[1024]{0:T(1024)S(1)} all-reduce(f32[1024]{0:T(1024)S(1)} %exponential_dynamic-update-slice_fusion), channel_id=2, replica_groups=mesh['section'=2,'ctx'=64,'mp'=2] {'ctx'}, use_global_device_ids=true, to_apply=%add.1 | all-reduce | flops 1024 | bytes 8192
  307.6 5.2 fusion.1
  312.8 404.0 %all-gather.3.cloned.1.call-done = f32[64,16,128,128]{3,2,1,0:T(8,128)} async-done(((f32[1,16,128,128]{3,2,1,0:T(8,128)}), f32[64,16,128,128]{3,2,1,0:T(8,128)}) %all-gather.3.cloned.1.call-update) | async-done | bytes 67108880 | tf_op jit(solution)/shard_map/all_gather | solution.py:18
  716.7 138.1 %while.14 = (s32[]{:T(128)}, f32[16,128,128]{2,1,0:T(8,128)S(1)}, s32[]{:T(128)}, f32[64,16]{1,0:T(8,128)}, f32[64,16,128,128]{3,2,1,0:T(8,128)}, /*index=5*/s32[]{:T(128)}, s32[]{:T(128)}) while((s32[]{:T(128)}, f32[16,128,128]{2,1,0:T(8,128)S(1)}, s32[]{:T(128)}, f32[64,16]{1,0:T(8,128)}, f32[64,16,128,128]{3,2,1,0:T(8,128)}, ...), condition=%wide.region_9.10_spmd.clone, body=%wide.region_8.9_spmd.clone.sunk | while | flops 1048580 | bytes 3146025 | solution.py:30
  752.0 1.5 fusion.43
  754.1 1.5 fusion.43
  775.7 1.5 fusion.43
  793.0 1.5 fusion.43
  797.3 1.5 fusion.43
  854.9 8.8 bitcast_add_fusion.1
  863.7 5.5 copy.60
  869.2 7.5 multiply_reduce_fusion
  876.7 6.1 psum.15
  882.8 3.9 multiply_convert_fusion
  (189 shorter events, 143.1 us)
Async XLA Ops:
  6.5 862.6 %copy-start = (bf16[64,2048]{1,0:T(8,128)(2,1)S(1)}, bf16[64,2048]{1,0:T(8,128)(2,1)}, u32[]{:S(2)}) copy-start(bf16[64,2048]{1,0:T(8,128)(2,1)} %param.19) | copy-start | bytes 786436
  6.5 126.7 %all-reduce.4.cloned.1.call-start = ((), (), s32[]{:S(2)}) async-start(), calls=%async_computation | async-start | bytes 524288 | tf_op jit(solution)/shard_map/psum | solution.py:77
  23.1 5.4 copy-start.8
  23.2 64.5 %copy-start.9 = (f32[512,16]{0,1:T(8,128)S(1)}, f32[512,16]{0,1:T(8,128)}, u32[]{:S(2)}) copy-start(f32[512,16]{0,1:T(8,128)} %param.22) | copy-start | bytes 98308
  23.2 67.5 %copy-start.3 = (bf16[512,128]{1,0:T(8,128)(2,1)S(1)}, bf16[512,128]{1,0:T(8,128)(2,1)}, u32[]{:S(2)}) copy-start(bf16[512,128]{1,0:T(8,128)(2,1)} %param.20) | copy-start | bytes 393220
  23.2 110.1 %copy-start.1 = (bf16[512,2048]{1,0:T(8,128)(2,1)S(1)}, bf16[512,2048]{1,0:T(8,128)(2,1)}, u32[]{:S(2)}) copy-start(bf16[512,2048]{1,0:T(8,128)(2,1)} %param.17) | copy-start | bytes 6291460
  23.2 110.1 %copy-start.4 = (bf16[64,2048]{1,0:T(8,128)(2,1)S(1)}, bf16[64,2048]{1,0:T(8,128)(2,1)}, u32[]{:S(2)}) copy-start(bf16[64,2048]{1,0:T(8,128)(2,1)} %param.18) | copy-start | bytes 786436
  87.6 629.1 %all-gather.3.cloned.1.call-start = ((), (), s32[]{:S(2)}) async-start(), calls=%async_computation.1 | async-start | bytes 68157440 | tf_op jit(solution)/shard_map/all_gather | solution.py:18
  89.2 48.9 %copy-start.7 = (f32[2,256,16]{1,2,0:T(8,128)}, f32[2,256,16]{1,2,0:T(8,128)S(1)}, u32[]{:S(2)}) copy-start(f32[2,256,16]{1,2,0:T(8,128)S(1)} %bitcast_bitcast_fusion) | copy-start | bytes 98308
  141.1 2.4 copy-start.12
  141.1 164.4 %copy-start.2 = (bf16[512,128]{1,0:T(8,128)(2,1)S(1)}, bf16[512,128]{1,0:T(8,128)(2,1)}, u32[]{:S(2)}) copy-start(bf16[512,128]{1,0:T(8,128)(2,1)} %param.21) | copy-start | bytes 393220
  716.7 138.2 %copy-start.6 = (f32[2,256,16]{1,2,0:T(8,128)S(1)}, f32[2,256,16]{1,2,0:T(8,128)}, u32[]{:S(2)}) copy-start(f32[2,256,16]{1,2,0:T(8,128)} %get-tuple-element.135) | copy-start | bytes 98308
  716.7 138.2 %copy-start.11 = (f32[16]{0:T(128)S(1)}, f32[16]{0:T(128)}, u32[]{:S(2)}) copy-start(f32[16]{0:T(128)} %param.23) | copy-start | bytes 196
  863.7 5.5 copy-start.5
  869.2 13.6 %copy-start.10 = (f32[2048]{0:T(1024)S(1)}, f32[2048]{0:T(1024)}, u32[]{:S(2)}) copy-start(f32[2048]{0:T(1024)} %param.25) | copy-start | bytes 24580
Sparse Core Ops, SparseCore 0:
  87.8 45.4 all-reduce.3
  143.5 573.1 all-gather.2
where the time goes:
time: 899 us; the launch traced here: 894 us
  waiting for transfers between devices  446 us (50%)
  other arithmetic  166 us (18%)
  blocking collectives  165 us (18%)
  local copies, waits for them, and re-layouts  74.8 us (8%)
  matrix products  26.1 us (3%)
  between operations  14.2 us (2%)
    all_gather x1, waiting for transfers between devices, entering_2(): everything = jax.tree.map(lambda part: lax.all_gather(part, axis), value)  404 us
    unnamed x1, blocking collectives  159 us
    select_n x64, other arithmetic, step(): return jax.tree.map(lambda a, b: jnp.where(reached, a, b), new, before)  93 us
    scatter-add x1, other arithmetic, body(): jax.ops.segment_sum(lifted.reshape(-1, CF), cell_index[0].reshape(-1), nu...  58.7 us
    mul x64, local copies, waits for them, and re-layouts, link_states(): decay_late[:, None, None] * state_early + state_late  43.9 us
    psum x1, waiting for transfers between devices, body(): pooled = lax.psum(partial_sum, ('section', 'mp'))  42.3 us
  transfers between devices with their start and end apart: 2, of which 2 were waited for; matrix products, arithmetic and copies ran while one was open for 1% of the time, Pallas kernels for 0%

commit v1 on v0

v1 whole, which is shorter than its diff:
```python
import functools
import math

import jax
import jax.numpy as jnp
from jax import lax
from jax.experimental import pallas as pl
from jax.experimental.pallas import tpu as pltpu
from jax.sharding import PartitionSpec as P

P_SIZE = 128
N = 128
BLK = 256
CF = 64
DI = 8192
EPSILON = 1e-05
LOG2E = math.log2(math.e)
CHUNK = 64
EXTRA = 8

f32 = jnp.float32
bf16 = jnp.bfloat16

VMEM = pl.BlockSpec(memory_space=pltpu.VMEM)
SMEM = pl.BlockSpec(memory_space=pltpu.SMEM)
PARAMS = pltpu.CompilerParams(vmem_limit_bytes=48 * 1024 * 1024)


def terms(x, count):
    parts = []
    for _ in range(count - 1):
        part = x.astype(bf16)
        parts.append(part)
        x = x - part.astype(f32)
    parts.append(x.astype(bf16))
    return parts


def dot(a, b):
    return jnp.dot(a, b, preferred_element_type=f32)


def pool_kernel(logits_ref, cells_ref, feats_ref, out_ref, wide, prob, cell, hits):
    rows, bins = logits_ref.shape
    wide[:, :bins] = logits_ref[...]
    logits = wide[...].T[:bins]
    raised = jnp.exp(logits - jnp.max(logits, axis=0, keepdims=True))
    prob[...] = raised / jnp.sum(raised, axis=0, keepdims=True)
    wide[:, :bins] = cells_ref[...].astype(f32)
    cell[...] = wide[...].T[:bins]

    def chunk(k, carry):
        first = pl.multiple_of(k * CHUNK, CHUNK)
        ids = (lax.broadcasted_iota(jnp.int32, (CHUNK, rows), 0) + first).astype(f32)
        acc = jnp.zeros((CHUNK, rows), f32)
        for d in range(bins):
            acc = acc + jnp.where(cell[d : d + 1, :] == ids, prob[d : d + 1, :], 0.0)
        high, low = terms(acc, 2)
        hits[pl.ds(first, CHUNK), :rows] = high
        hits[pl.ds(first, CHUNK), rows:] = low
        return carry

    lax.fori_loop(0, hits.shape[0] // CHUNK, chunk, 0)
    feats = feats_ref[...]
    pooled = dot(hits[...], jnp.concatenate([feats, feats], axis=0))
    half = pooled.shape[0] // 2
    out_ref[...] = jnp.concatenate([pooled[:half], pooled[half:]], axis=1)


def mask_kernel(
    forget_ref, in_ref, read_ref, frames_ref, weights_ref, keys_ref, ends_ref, decay_ref, wide, cum_t
):
    heads = forget_ref.shape[1]
    blocks = weights_ref.shape[0]
    row_order = lax.broadcasted_iota(jnp.int32, (BLK, BLK), 0)
    col_order = lax.broadcasted_iota(jnp.int32, (BLK, BLK), 1)
    causal = col_order <= row_order
    lower = jnp.where(causal, 1.0, 0.0).astype(bf16)
    before = jnp.zeros((1, heads), f32)
    for b in range(blocks):
        rows = slice(b * BLK, (b + 1) * BLK)
        cum = sum(dot(lower, part) for part in terms(forget_ref[rows, :], 3))
        wide[rows, :heads] = cum
        decay = terms(jnp.exp(-(cum + before)), 3)
        own = terms(jnp.exp(-cum), 3)
        decay_ref[0, rows, :] = jnp.concatenate(decay, axis=1)
        decay_ref[1, rows, :] = jnp.concatenate(own, axis=1)
        before = before + cum[BLK - 1 :, :]
    turned = wide[...].T
    cum_t[...] = turned[:heads]

    def block(b, carry):
        rows = pl.ds(pl.multiple_of(b * BLK, BLK), BLK)
        scores = lax.dot_general(
            read_ref[rows, :], in_ref[rows, :], (((1,), (1,)), ((), ())), preferred_element_type=f32
        )
        frame_row = frames_ref[:, rows].astype(f32)
        frame_col = jnp.broadcast_to(frame_row, (128, BLK)).T
        same = jnp.concatenate([frame_col, frame_col], axis=1) == frame_row
        scored = jnp.where(causal | same, scores, 0.0)
        write_t = in_ref[rows, :].astype(f32).T
        cum_b = cum_t[:, rows]
        end = cum_b[:, BLK - 1 :]
        rise = jnp.exp(cum_b - end)
        ends_ref[b] = jnp.broadcast_to(end, (heads, 128))
        scaled_rows = cum_b * LOG2E
        scaled_cols = wide[rows, :] * LOG2E
        for h in range(heads):
            distance = jnp.abs(scaled_cols[:, h : h + 1] - scaled_rows[h : h + 1, :])
            weights_ref[b, h] = (scored * jnp.exp2(-distance)).astype(bf16)
            keys_ref[b, h] = (write_t * rise[h : h + 1, :]).astype(bf16)
        return carry

    lax.fori_loop(0, blocks, block, 0)


def stream_kernel(
    mine_ref, other_ref, w_ref, embed_ref, keys_ref, ends_ref, stream_ref, pay_ref, first_ref, pooled_ref
):
    packed = mine_ref[...] + other_ref[...]
    pooled = jnp.concatenate([packed[:, :CF], packed[:, CF:]], axis=0)
    pooled_ref[...] = jnp.concatenate(terms(pooled, 3), axis=1)
    heads = first_ref.shape[0]

    def pair(q, carry):
        lanes = pl.ds(pl.multiple_of(q * 256, 256), 256)
        w = w_ref[:, lanes]
        visual = dot(pooled_ref[...], jnp.concatenate([w, w, w], axis=0))
        stream = (embed_ref[:, lanes].astype(f32) + visual).astype(bf16)
        stream_ref[:, lanes] = stream
        for j in range(2):
            h = 2 * q + j
            part = stream[:, j * P_SIZE : (j + 1) * P_SIZE]
            early = dot(keys_ref[0, h], part[:BLK])
            late = dot(keys_ref[1, h], part[BLK:])
            end_early = ends_ref[0, pl.ds(h, 1), :]
            end_late = ends_ref[1, pl.ds(h, 1), :]
            first_ref[h] = early
            pay_ref[h, :N, :] = jnp.exp(-end_late) * early + late
            pay_ref[h, N:, :] = jnp.broadcast_to(end_early + end_late, (EXTRA, P_SIZE))
        return carry

    lax.fori_loop(0, heads // 2, pair, 0)


def pick(heads, h):
    row = lax.broadcasted_iota(jnp.int32, (3 * heads, P_SIZE), 0)
    hit = (row == h) | (row == h + heads) | (row == h + 2 * heads)
    return jnp.where(hit, 1.0, 0.0).astype(bf16)


def within_kernel(
    weights_ref, stream_ref, pooled_ref, w_ref, skip_ref, first_ref, read_ref, decay_ref, base_ref, gain_ref
):
    heads = first_ref.shape[0]
    read = read_ref[BLK:, :]
    read_twice = jnp.concatenate([read, read], axis=1)

    def head(h, carry):
        lanes = pl.ds(pl.multiple_of(h * P_SIZE, P_SIZE), P_SIZE)
        w = w_ref[:, lanes]
        gate = dot(pooled_ref[...], jnp.concatenate([w, w, w], axis=0))
        silu = gate / (1.0 + jnp.exp(-gate))
        chosen = pick(heads, h)
        gain_ref[:, lanes] = silu * dot(decay_ref[0], chosen)
        stream = stream_ref[:, lanes]
        direct = skip_ref[0, h] * stream.astype(f32)
        early = dot(weights_ref[0, h], stream[:BLK])
        late = dot(weights_ref[1, h], stream[BLK:])
        state = jnp.concatenate(terms(first_ref[h], 2), axis=0)
        late = late + dot(decay_ref[1, BLK:, :], chosen) * dot(read_twice, state)
        base_ref[:BLK, lanes] = (early + direct[:BLK]) * silu[:BLK]
        base_ref[BLK:, lanes] = (late + direct[BLK:]) * silu[BLK:]
        return carry

    lax.fori_loop(0, heads, head, 0)


def total_kernel(got_ref, total_ref):
    state = got_ref[0, :N, :]
    log = got_ref[0, N:, :]
    for i in range(1, got_ref.shape[0]):
        gone = got_ref[i, N:, :]
        state = jnp.exp(-gone[:1]) * state + got_ref[i, :N, :]
        log = log + gone
    total_ref[:N, :] = state
    total_ref[N:, :] = log


def join_kernel(total_ref, near_ref, out_ref):
    out_ref[...] = total_ref[:N, :] + jnp.exp(-total_ref[N : N + 1, :]) * near_ref[:N, :]


def spread_kernel(got_ref, near_ref, far_ref, out_ref):
    state = near_ref[:N, :] + jnp.exp(-near_ref[N : N + 1, :]) * far_ref[...]
    for i in range(got_ref.shape[0]):
        out_ref[i] = state
        state = jnp.exp(-got_ref[i, N : N + 1, :]) * state + got_ref[i, :N, :]


def carry_kernel(state_ref, read_ref, base_ref, gain_ref, gated_ref, energy_ref, acc):
    heads = state_ref.shape[0]
    read = read_ref[...]
    read_twice = jnp.concatenate([read, read], axis=1)
    acc[...] = jnp.zeros_like(acc)

    def head(h, carry):
        lanes = pl.ds(pl.multiple_of(h * P_SIZE, P_SIZE), P_SIZE)
        state = jnp.concatenate(terms(state_ref[h], 2), axis=0)
        gated = base_ref[:, lanes] + gain_ref[:, lanes] * dot(read_twice, state)
        gated_ref[:, lanes] = gated
        acc[...] += gated * gated
        return carry

    lax.fori_loop(0, heads, head, 0)
    energy_ref[...] = jnp.sum(acc[...].T, axis=0, keepdims=True)


def norm_kernel(gated_ref, mine_ref, other_ref, gain_ref, out_ref):
    inverse = lax.rsqrt((mine_ref[...] + other_ref[...]) / DI + EPSILON)
    column = jnp.broadcast_to(inverse, (P_SIZE, inverse.shape[1])).T

    def head(h, carry):
        lanes = pl.ds(pl.multiple_of(h * P_SIZE, P_SIZE), P_SIZE)
        out_ref[:, lanes] = (gated_ref[:, lanes] * column * gain_ref[:, lanes]).astype(bf16)
        return carry

    lax.fori_loop(0, gated_ref.shape[1] // P_SIZE, head, 0)


def call(kernel, ins, outs, scratch=(), specs=None):
    return pl.pallas_call(
        kernel,
        out_shape=[jax.ShapeDtypeStruct(shape, dtype) for shape, dtype in outs],
        in_specs=specs or [VMEM] * len(ins),
        out_specs=[VMEM] * len(outs),
        scratch_shapes=list(scratch),
        compiler_params=PARAMS,
    )(*ins)


def swap(value, axis):
    return lax.ppermute(value, axis, [(0, 1), (1, 0)])


def body(
    depth_logits,
    features,
    cell_index,
    embed,
    w_visual,
    w_gate,
    input_map,
    output_map,
    forget,
    skip,
    frame_ids,
    norm_gain,
):
    tokens, width = embed.shape
    heads = forget.shape[1]
    blocks = tokens // BLK
    pixels, bins = depth_logits.shape[1:]
    shards = lax.axis_size("ctx")
    groups = [list(range(g, g + heads)) for g in range(0, shards, heads)]

    (partial_sum,) = call(
        pool_kernel,
        (depth_logits[0], cell_index[0], features[0]),
        [((tokens // 2, 2 * CF), f32)],
        [
            pltpu.VMEM((pixels, 128), f32),
            pltpu.VMEM((bins, pixels), f32),
            pltpu.VMEM((bins, pixels), f32),
            pltpu.VMEM((tokens, 2 * pixels), bf16),
        ],
    )
    chip_sum = partial_sum + swap(partial_sum, "mp")
    other_sum = swap(chip_sum, "section")

    weights, keys, ends, decay = call(
        mask_kernel,
        (forget, input_map, output_map, frame_ids.reshape(1, tokens)),
        [
            ((blocks, heads, BLK, BLK), bf16),
            ((blocks, heads, N, BLK), bf16),
            ((blocks, heads, 128), f32),
            ((2, tokens, 3 * heads), bf16),
        ],
        [pltpu.VMEM((tokens, 128), f32), pltpu.VMEM((heads, tokens), f32)],
    )

    stream, pay, first, pooled = call(
        stream_kernel,
        (chip_sum, other_sum, w_visual, embed, keys, ends),
        [
            ((tokens, width), bf16),
            ((heads, N + EXTRA, P_SIZE), f32),
            ((heads, N, P_SIZE), f32),
            ((tokens, 3 * CF), bf16),
        ],
    )
    got = lax.all_to_all(pay, "ctx", 0, 0, axis_index_groups=groups, tiled=True)

    base, gain = call(
        within_kernel,
        (weights, stream, pooled, w_gate, skip.reshape(1, heads), first, output_map, decay),
        [((tokens, width), f32), ((tokens, width), f32)],
        specs=[VMEM] * 4 + [SMEM] + [VMEM] * 3,
    )

    (total,) = call(total_kernel, (got,), [((N + EXTRA, P_SIZE), f32)])
    near = lax.ppermute(total, "ctx", [(i, i + heads) for i in range(shards - heads)])
    (joined,) = call(join_kernel, (total, near), [((N, P_SIZE), f32)])
    far = lax.ppermute(joined, "ctx", [(i, i + 2 * heads) for i in range(shards - 2 * heads)])
    (sent,) = call(spread_kernel, (got, near, far), [((heads, N, P_SIZE), f32)])
    incoming = lax.all_to_all(sent, "ctx", 0, 0, axis_index_groups=groups, tiled=True)

    gated, energy = call(
        carry_kernel,
        (incoming, output_map, base, gain),
        [((tokens, width), f32), ((1, tokens), f32)],
        [pltpu.VMEM((tokens, P_SIZE), f32)],
    )
    chip_energy = energy + swap(energy, "mp")
    other_energy = swap(chip_energy, "section")
    (out,) = call(
        norm_kernel,
        (gated, chip_energy, other_energy, norm_gain.reshape(1, width)),
        [((tokens, width), bf16)],
    )
    return out


def solution(mesh):
    return jax.shard_map(
        body,
        mesh=mesh,
        in_specs=(
            P("section", ("ctx", "mp"), None),
            P("section", ("ctx", "mp"), None),
            P("section", ("ctx", "mp"), None),
            P("ctx", ("section", "mp")),
            P(None, ("section", "mp")),
            P(None, ("section", "mp")),
            P("ctx", None),
            P("ctx", None),
            P("ctx", ("section", "mp")),
            P(("section", "mp")),
            P("ctx"),
            P(("section", "mp")),
        ),
        out_specs=P("ctx", ("section", "mp")),
        check_vma=False,
    )
```

time: 899 us -> 108 us (0.12)
  waiting for transfers between devices: 446 us -> 6.9 us
  other arithmetic: 166 us -> 0.02 us
  blocking collectives: 165 us -> 25.1 us
  local copies, waits for them, and re-layouts: 74.8 us -> 12.2 us
  Pallas kernels: 0 us -> 36.3 us
  starting transfers between devices: 0.04 us -> 26.3 us
  matrix products: 26.1 us -> 0 us
  between operations: 14.2 us -> 0.17 us
    all_gather x1 -> x0, waiting for transfers between devices: 404 us -> none  [entering_2(): everything = jax.tree.map(lambda part: lax.all_gather(part, axis), value)]
    unnamed x1 -> x0, blocking collectives: 159 us -> none
    select_n x64 -> x0, other arithmetic: 93 us -> none  [step(): return jax.tree.map(lambda a, b: jnp.where(reached, a, b), new, before)]
    mul x67 -> x0, local copies, waits for them, and re-layouts: 60 us -> none  [the longest x64 43.9 us: link_states(): decay_late[:, None, None] * state_early + state_late]
    scatter-add x1 -> x0, other arithmetic: 58.7 us -> none  [body(): jax.ops.segment_sum(lifted.reshape(-1, CF), cell_index[0].reshape(-1), nu...]
    psum x1 -> x0, waiting for transfers between devices: 42.3 us -> none  [body(): pooled = lax.psum(partial_sum, ('section', 'mp'))]
    pallas_call x0 -> x9, Pallas kernels: none -> 36.3 us  [call(): pl.pallas_call(kernel, out_shape=[jax.ShapeDtypeStruct(shape, dtype) for...]
    dot_general x6 -> x0, matrix products: 26.1 us -> none  [the longest x1 8.77 us: body(): jnp.einsum('bthn,bhnp->bthp', reads_scaled, entering, precision=highest)]
  transfers between devices with their start and end apart: 2 -> 7, of which waited for: 2 -> 5; matrix products, arithmetic and copies ran while one was open for 1% -> 1% of each run, Pallas kernels for 0% -> 15%
where the time goes in v1:
time: 108 us; the launch traced here: 107 us
  Pallas kernels  36.3 us (34%)
  starting transfers between devices  26.3 us (24%)
  blocking collectives  25.1 us (23%)
  local copies, waits for them, and re-layouts  12.2 us (11%)
  waiting for transfers between devices  6.9 us (6%)
    pallas_call x9, Pallas kernels, call(): pl.pallas_call(kernel, out_shape=[jax.ShapeDtypeStruct(shape, dtype) for...  36.3 us
    all_to_all x1, blocking collectives, body(): got = lax.all_to_all(pay, 'ctx', 0, 0, axis_index_groups=groups, tiled=True)  25.1 us
    unnamed x34, local copies, waits for them, and re-layouts  12.2 us
    ppermute x1, starting transfers between devices, body(): lax.ppermute(joined, 'ctx', [(i, i + 2 * heads) for i in range(shards - 2...  9.72 us
    ppermute x4, starting transfers between devices, swap(): return lax.ppermute(value, axis, [(0, 1), (1, 0)])  8.04 us
    ppermute x1, starting transfers between devices, body(): lax.ppermute(total, 'ctx', [(i, i + heads) for i in range(shards - heads)])  4.89 us
    ppermute x4, waiting for transfers between devices, swap(): return lax.ppermute(value, axis, [(0, 1), (1, 0)])  4.24 us
    all_to_all x1, starting transfers between devices, body(): lax.all_to_all(sent, 'ctx', 0, 0, axis_index_groups=groups, tiled=True)  3.66 us
  transfers between devices with their start and end apart: 7, of which 5 were waited for; matrix products, arithmetic and copies ran while one was open for 1% of the time, Pallas kernels for 15%

profile of v1, /device:TPU:1, one launch (start us, length us, event | category | flops | bytes accessed | tf_op | source)
XLA Modules:
  0.0 107.1 jit_solution(1618488068992789308)
XLA Ops:
  0.0 0.9 copy.15
  2.7 3.0 %shard_map.118 = f32[256,128]{1,0:T(8,128)S(1)} custom-call(f32[256,41]{1,0:T(8,128)S(1)} %bitcast.6, s32[256,41]{1,0:T(8,128)S(1)} %bitcast.7, bf16[256,64]{1,0:T(8,128)(2,1)S(1)} %bitcast.8), custom_call_target="tpu_custom_call" | custom-call | tf_op jit(solution)/shard_map/pallas_call | solution.py:232
  5.7 3.3 %collective-permute-start = (f32[256,128]{1,0:T(8,128)S(1)}, f32[256,128]{1,0:T(8,128)S(1)}, u32[]{:S(2)}, u32[]{:S(2)}) collective-permute-start(f32[256,128]{1,0:T(8,128)S(1)} %shard_map.118), channel_id=1, source_target_pairs={{0,1},{1,0},{2,3},{3,2},{4,5},{5,4},{6,7},{7,6},{8,9},{9,8},{10,11... | collective-permute-start | bytes 393224 | tf_op jit(solution)/shard_map/ppermute | solution.py:243
  9.0 1.0 collective-permute-done
  11.9 0.9 copy-done.11
  13.5 4.6 %shard_map.119 = (bf16[2,16,256,256]{3,2,1,0:T(8,128)(2,1)}, bf16[2,16,128,256]{3,2,1,0:T(8,128)(2,1)S(1)}, f32[2,16,128]{2,1,0:T(8,128)S(1)}, bf16[2,512,48]{2,1,0:T(8,128)(2,1)S(1)}) custom-call(f32[512,16]{1,0:T(8,128)S(1)} %copy.16.forget_ref, bf16[512,128]{1,0:T(8,128)(2,1)S(1)} %copy-done.11, bf16[512,128]{1,0:T(8,128)(2,1)S(1)} %copy-done.1, ...), custom_call_target="tpu_custom_call" | custom-call | tf_op jit(solution)/shard_map/pallas_call | solution.py:232
  18.1 1.3 %copy-done = bf16[2,16,128,256]{3,2,1,0:T(8,128)(2,1)} copy-done((bf16[2,16,128,256]{3,2,1,0:T(8,128)(2,1)}, bf16[2,16,128,256]{3,2,1,0:T(8,128)(2,1)S(1)}, u32[]{:S(2)}) %copy-start) | copy-done | bytes 2097176
  20.1 6.4 %shard_map.120 = (bf16[512,2048]{1,0:T(8,128)(2,1)S(1)}, f32[16,136,128]{2,1,0:T(8,128)S(1)}, f32[16,128,128]{2,1,0:T(8,128)S(1)}, bf16[512,192]{1,0:T(8,128)(2,1)S(1)}) custom-call(f32[256,128]{1,0:T(8,128)S(1)} %add.6.mine_ref, f32[256,128]{1,0:T(8,128)S(1)} %collective-permute-done.1.other_ref, bf16[64,2048]{1,0:T(8,128)(2,1)S(1)} %copy-done.5, ...), custom_call_target="tpu_custom_call" | custom-call | tf_op jit(solution)/shard_map/pallas_call | solution.py:232
  26.6 1.0 copy-done.3
  27.6 25.1 %all_to_all.10.got_ref = f32[16,136,128]{2,1,0:T(8,128)S(1)} all-to-all(f32[16,136,128]{2,1,0:T(8,128)S(1)} %get-tuple-element.19), channel_id=1, replica_groups={{0,2,4,6,8,10,12,14,16,18,20,22,24,26,28,30},{32,34,36,38,40,42,44,46,4..., dimensions={0} | all-to-all | bytes 2228224 | tf_op jit(solution)/shard_map/all_to_all | solution.py:303
  52.8 4.9 %collective-permute-start.2 = (f32[136,128]{1,0:T(8,128)S(1)}, f32[136,128]{1,0:T(8,128)S(1)}, u32[]{:S(2)}, u32[]{:S(2)}) collective-permute-start(f32[136,128]{1,0:T(8,128)S(1)} %shard_map.121.total_ref), channel_id=1, source_target_pairs={{0,32},{2,34},{4,36},{6,38},{8,40},{10,42},{12,44},{14,46},{16,48}... | collective-permute-start | bytes 208904 | tf_op jit(solution)/shard_map/ppermute | solution.py:313
  57.7 1.3 %collective-permute-done.2.near_ref = f32[136,128]{1,0:T(8,128)S(1)} collective-permute-done((f32[136,128]{1,0:T(8,128)S(1)}, f32[136,128]{1,0:T(8,128)S(1)}, u32[]{:S(2)}, u32[]{:S(2)}) %collective-permute-start.2) | collective-permute-done | bytes 69664 | tf_op jit(solution)/shard_map/ppermute | solution.py:313
  59.1 9.7 %collective-permute-start.3 = (f32[128,128]{1,0:T(8,128)S(1)}, f32[128,128]{1,0:T(8,128)S(1)}, u32[]{:S(2)}, u32[]{:S(2)}) collective-permute-start(f32[128,128]{1,0:T(8,128)S(1)} %shard_map.122), channel_id=1, source_target_pairs={{0,64},{2,66},{4,68},{6,70},{8,72},{10,74},{12,76},{14,78},{16,80}... | collective-permute-start | bytes 196616 | tf_op jit(solution)/shard_map/ppermute | solution.py:315
  68.8 1.3 %collective-permute-done.3.far_ref = f32[128,128]{1,0:T(8,128)S(1)} collective-permute-done((f32[128,128]{1,0:T(8,128)S(1)}, f32[128,128]{1,0:T(8,128)S(1)}, u32[]{:S(2)}, u32[]{:S(2)}) %collective-permute-start.3) | collective-permute-done | bytes 65568 | tf_op jit(solution)/shard_map/ppermute | solution.py:315
  70.1 1.1 shard_map.123
  71.2 3.7 %all-to-all-start.1 = ((f32[16,128,128]{2,1,0:T(8,128)}), f32[16,128,128]{2,1,0:T(8,128)S(1)}, u32[]{:S(2)}, u32[]{:S(2)}) async-start(f32[16,128,128]{2,1,0:T(8,128)} %shard_map.123), calls=%async_computation.1 | async-start | bytes 2097152 | tf_op jit(solution)/shard_map/all_to_all | solution.py:317
  74.9 1.2 %copy-done.4 = f32[16,128,128]{2,1,0:T(8,128)S(1)} copy-done((f32[16,128,128]{2,1,0:T(8,128)S(1)}, f32[16,128,128]{2,1,0:T(8,128)}, u32[]{:S(2)}) %copy-start.4) | copy-done | bytes 1048600
  76.1 0.9 copy-done.8
  77.1 0.9 copy-done.10
  78.0 11.4 %shard_map.124 = (f32[512,2048]{1,0:T(8,128)}, f32[512,2048]{1,0:T(8,128)}) custom-call(bf16[2,16,256,256]{3,2,1,0:T(8,128)(2,1)} %get-tuple-element.20.weights_ref, bf16[512,2048]{1,0:T(8,128)(2,1)S(1)} %get-tuple-element.21.stream_ref, bf16[512,192]{1,0:T(8,128)(2,1)S(1)} %copy-done.10, bf16[64,2048]{1,0:T(8,128)(2,1)S(1)} %copy-done.6, ...), custom_call_target="tpu_custom_call" | custom-call | tf_op jit(solution)/shard_map/pallas_call | solution.py:232
  89.5 7.5 %shard_map.125 = (f32[512,2048]{1,0:T(8,128)S(1)}, f32[1,512]{1,0:T(1,128)S(1)}) custom-call(f32[16,128,128]{2,1,0:T(8,128)S(1)} %all-to-all-done.1.state_ref, bf16[512,128]{1,0:T(8,128)(2,1)S(1)} %copy-done.2, f32[512,2048]{1,0:T(8,128)} %get-tuple-element.25.base_ref, f32[512,2048]{1,0:T(8,128)} %get-tuple-element.26.gain_ref), custom_call_target="tpu_custom_call" | custom-call | tf_op jit(solution)/shard_map/pallas_call | solution.py:232
  97.0 4.6 %collective-permute-start.4 = (f32[1,512]{1,0:T(1,128)S(1)}, f32[1,512]{1,0:T(1,128)S(1)}, u32[]{:S(2)}, u32[]{:S(2)}) collective-permute-start(f32[1,512]{1,0:T(1,128)S(1)} %get-tuple-element.28), channel_id=1, source_target_pairs={{0,1},{1,0},{2,3},{3,2},{4,5},{5,4},{6,7},{7,6},{8,9},{9,8},{10,11... | collective-permute-start | bytes 6152 | tf_op jit(solution)/shard_map/ppermute | solution.py:243
  102.4 2.4 %collective-permute-done.5.other_ref = f32[1,512]{1,0:T(1,128)S(1)} collective-permute-done((f32[1,512]{1,0:T(1,128)S(1)}, f32[1,512]{1,0:T(1,128)S(1)}, u32[]{:S(2)}, u32[]{:S(2)}) %collective-permute-start.5) | collective-permute-done | bytes 2080 | tf_op jit(solution)/shard_map/ppermute | solution.py:243
  104.8 2.2 %shard_map.126 = bf16[512,2048]{1,0:T(8,128)(2,1)} custom-call(f32[512,2048]{1,0:T(8,128)S(1)} %get-tuple-element.27.gated_ref, f32[1,512]{1,0:T(1,128)S(1)} %add.7.mine_ref, f32[1,512]{1,0:T(1,128)S(1)} %collective-permute-done.5.other_ref, f32[1,2048]{1,0:T(1,128)S(1)} %bitcast.9), custom_call_target="tpu_custom_call" | custom-call | tf_op jit(solution)/shard_map/pallas_call | solution.py:232
  (36 shorter events, 6.0 us)
Async XLA Ops:
  0.0 20.1 %copy-start.5 = (bf16[64,2048]{1,0:T(8,128)(2,1)S(1)}, bf16[64,2048]{1,0:T(8,128)(2,1)}, u32[]{:S(2)}) copy-start(bf16[64,2048]{1,0:T(8,128)(2,1)} %w_ref.2) | copy-start | bytes 786436
  5.7 4.3 %collective-permute-start = (f32[256,128]{1,0:T(8,128)S(1)}, f32[256,128]{1,0:T(8,128)S(1)}, u32[]{:S(2)}, u32[]{:S(2)}) collective-permute-start(f32[256,128]{1,0:T(8,128)S(1)} %shard_map.118), channel_id=1, source_target_pairs={{0,1},{1,0},{2,3},{3,2},{4,5},{5,4},{6,7},{7,6},{8,9},{9,8},{10,11... | collective-permute-start | bytes 393224 | tf_op jit(solution)/shard_map/ppermute | solution.py:243
  10.0 10.1 %collective-permute-start.1 = (f32[256,128]{1,0:T(8,128)S(1)}, f32[256,128]{1,0:T(8,128)S(1)}, u32[]{:S(2)}, u32[]{:S(2)}) collective-permute-start(f32[256,128]{1,0:T(8,128)S(1)} %add.6.mine_ref), channel_id=1, source_target_pairs={{0,128},{128,0},{1,129},{129,1},{2,130},{130,2},{3,131},{131,3},{4... | collective-permute-start | bytes 393224 | tf_op jit(solution)/shard_map/ppermute | solution.py:243
  11.0 0.9 copy-start.1
  11.9 0.9 copy-start.11
  12.8 0.7 copy-start.13
  18.1 1.3 %copy-start = (bf16[2,16,128,256]{3,2,1,0:T(8,128)(2,1)}, bf16[2,16,128,256]{3,2,1,0:T(8,128)(2,1)S(1)}, u32[]{:S(2)}) copy-start(bf16[2,16,128,256]{3,2,1,0:T(8,128)(2,1)S(1)} %get-tuple-element.17.keys_ref) | copy-start | bytes 6291460
  19.4 0.7 copy-start.7
  26.5 1.0 copy-start.3
  27.6 31.5 %copy-start.9 = (bf16[512,192]{1,0:T(8,128)(2,1)}, bf16[512,192]{1,0:T(8,128)(2,1)S(1)}, u32[]{:S(2)}) copy-start(bf16[512,192]{1,0:T(8,128)(2,1)S(1)} %get-tuple-element.22.pooled_ref) | copy-start | bytes 589828
  52.8 6.2 %collective-permute-start.2 = (f32[136,128]{1,0:T(8,128)S(1)}, f32[136,128]{1,0:T(8,128)S(1)}, u32[]{:S(2)}, u32[]{:S(2)}) collective-permute-start(f32[136,128]{1,0:T(8,128)S(1)} %shard_map.121.total_ref), channel_id=1, source_target_pairs={{0,32},{2,34},{4,36},{6,38},{8,40},{10,42},{12,44},{14,46},{16,48}... | collective-permute-start | bytes 208904 | tf_op jit(solution)/shard_map/ppermute | solution.py:313
  59.1 15.8 %copy-start.2 = (bf16[512,128]{1,0:T(8,128)(2,1)S(1)}, bf16[512,128]{1,0:T(8,128)(2,1)}, u32[]{:S(2)}) copy-start(bf16[512,128]{1,0:T(8,128)(2,1)} %read_ref.5) | copy-start | bytes 393220
  59.1 15.8 %copy-start.6 = (bf16[64,2048]{1,0:T(8,128)(2,1)S(1)}, bf16[64,2048]{1,0:T(8,128)(2,1)}, u32[]{:S(2)}) copy-start(bf16[64,2048]{1,0:T(8,128)(2,1)} %w_ref.3) | copy-start | bytes 786436
  59.1 15.8 %copy-start.14 = (f32[16]{0:T(128)S(1)}, f32[16]{0:T(128)}, u32[]{:S(2)}) copy-start(f32[16]{0:T(128)} %param.21) | copy-start | bytes 196
  59.1 11.0 %collective-permute-start.3 = (f32[128,128]{1,0:T(8,128)S(1)}, f32[128,128]{1,0:T(8,128)S(1)}, u32[]{:S(2)}, u32[]{:S(2)}) collective-permute-start(f32[128,128]{1,0:T(8,128)S(1)} %shard_map.122), channel_id=1, source_target_pairs={{0,64},{2,66},{4,68},{6,70},{8,72},{10,74},{12,76},{14,78},{16,80}... | collective-permute-start | bytes 196616 | tf_op jit(solution)/shard_map/ppermute | solution.py:315
  71.2 18.3 %all-to-all-start.1 = ((f32[16,128,128]{2,1,0:T(8,128)}), f32[16,128,128]{2,1,0:T(8,128)S(1)}, u32[]{:S(2)}, u32[]{:S(2)}) async-start(f32[16,128,128]{2,1,0:T(8,128)} %shard_map.123), calls=%async_computation.1 | async-start | bytes 2097152 | tf_op jit(solution)/shard_map/all_to_all | solution.py:317
  74.9 1.2 %copy-start.4 = (f32[16,128,128]{2,1,0:T(8,128)S(1)}, f32[16,128,128]{2,1,0:T(8,128)}, u32[]{:S(2)}) copy-start(f32[16,128,128]{2,1,0:T(8,128)} %copy-done.3) | copy-start | bytes 3145732
  76.1 0.9 copy-start.8
  77.1 0.9 copy-start.10
  89.5 15.4 %copy-start.12 = (f32[2048]{0:T(1024)S(1)}, f32[2048]{0:T(1024)}, u32[]{:S(2)}) copy-start(f32[2048]{0:T(1024)} %param.23) | copy-start | bytes 24580
  97.0 5.4 %collective-permute-start.4 = (f32[1,512]{1,0:T(1,128)S(1)}, f32[1,512]{1,0:T(1,128)S(1)}, u32[]{:S(2)}, u32[]{:S(2)}) collective-permute-start(f32[1,512]{1,0:T(1,128)S(1)} %get-tuple-element.28), channel_id=1, source_target_pairs={{0,1},{1,0},{2,3},{3,2},{4,5},{5,4},{6,7},{7,6},{8,9},{9,8},{10,11... | collective-permute-start | bytes 6152 | tf_op jit(solution)/shard_map/ppermute | solution.py:243
  102.4 2.4 %collective-permute-start.5 = (f32[1,512]{1,0:T(1,128)S(1)}, f32[1,512]{1,0:T(1,128)S(1)}, u32[]{:S(2)}, u32[]{:S(2)}) collective-permute-start(f32[1,512]{1,0:T(1,128)S(1)} %add.7.mine_ref), channel_id=1, source_target_pairs={{0,128},{128,0},{1,129},{129,1},{2,130},{130,2},{3,131},{131,3},{4... | collective-permute-start | bytes 6152 | tf_op jit(solution)/shard_map/ppermute | solution.py:243

commit v2 on v1

--- a/solution.py
+++ b/solution.py
@@ -1,4 +1,3 @@
-import functools
 import math
 
 import jax
@@ -23,7 +22,8 @@
 
 VMEM = pl.BlockSpec(memory_space=pltpu.VMEM)
 SMEM = pl.BlockSpec(memory_space=pltpu.SMEM)
-PARAMS = pltpu.CompilerParams(vmem_limit_bytes=48 * 1024 * 1024)
+HBM = pl.BlockSpec(memory_space=pltpu.HBM)
+PARAMS = pltpu.CompilerParams(vmem_limit_bytes=24 * 1024 * 1024)
 
 
 def terms(x, count):
@@ -40,21 +40,27 @@
     return jnp.dot(a, b, preferred_element_type=f32)
 
 
-def pool_kernel(logits_ref, cells_ref, feats_ref, out_ref, wide, prob, cell, hits):
-    rows, bins = logits_ref.shape
-    wide[:, :bins] = logits_ref[...]
-    logits = wide[...].T[:bins]
+def pool_kernel(*refs):
+    count = (len(refs) - 4) // 2
+    far, out_ref, near = refs[:count], refs[count], refs[count + 1 : 2 * count - 2]
+    logits_ref, cells_ref, feats_ref, prob, hits, sems = refs[2 * count - 2 :]
+    near = (logits_ref, cells_ref, feats_ref) + tuple(near)
+    copies = [pltpu.make_async_copy(far[i], near[i], sems.at[i]) for i in range(count)]
+    for copy in copies:
+        copy.start()
+    for copy in copies[:3]:
+        copy.wait()
+    bins, _, rows = logits_ref.shape
+    logits = logits_ref[...]
     raised = jnp.exp(logits - jnp.max(logits, axis=0, keepdims=True))
     prob[...] = raised / jnp.sum(raised, axis=0, keepdims=True)
-    wide[:, :bins] = cells_ref[...].astype(f32)
-    cell[...] = wide[...].T[:bins]
 
     def chunk(k, carry):
         first = pl.multiple_of(k * CHUNK, CHUNK)
-        ids = (lax.broadcasted_iota(jnp.int32, (CHUNK, rows), 0) + first).astype(f32)
+        ids = lax.broadcasted_iota(jnp.int32, (CHUNK, rows), 0) + first
         acc = jnp.zeros((CHUNK, rows), f32)
         for d in range(bins):
-            acc = acc + jnp.where(cell[d : d + 1, :] == ids, prob[d : d + 1, :], 0.0)
+            acc = acc + jnp.where(cells_ref[d] == ids, prob[d], 0.0)
         high, low = terms(acc, 2)
         hits[pl.ds(first, CHUNK), :rows] = high
         hits[pl.ds(first, CHUNK), rows:] = low
@@ -62,32 +68,39 @@
 
     lax.fori_loop(0, hits.shape[0] // CHUNK, chunk, 0)
     feats = feats_ref[...]
-    pooled = dot(hits[...], jnp.concatenate([feats, feats], axis=0))
+    pooled = lax.dot_general(
+        hits[...],
+        jnp.concatenate([feats, feats], axis=1),
+        (((1,), (1,)), ((), ())),
+        preferred_element_type=f32,
+    )
     half = pooled.shape[0] // 2
     out_ref[...] = jnp.concatenate([pooled[:half], pooled[half:]], axis=1)
+    for copy in copies[3:]:
+        copy.wait()
 
 
 def mask_kernel(
-    forget_ref, in_ref, read_ref, frames_ref, weights_ref, keys_ref, ends_ref, decay_ref, wide, cum_t
+    forget_ref, in_ref, read_ref, frames_ref, weights_ref, keys_ref, ends_ref, decay_ref, wide, turned, cum_t
 ):
-    heads = forget_ref.shape[1]
+    heads = forget_ref.shape[0]
     blocks = weights_ref.shape[0]
     row_order = lax.broadcasted_iota(jnp.int32, (BLK, BLK), 0)
     col_order = lax.broadcasted_iota(jnp.int32, (BLK, BLK), 1)
     causal = col_order <= row_order
-    lower = jnp.where(causal, 1.0, 0.0).astype(bf16)
+    upper = jnp.where(row_order <= col_order, 1.0, 0.0).astype(bf16)
+    for b in range(blocks):
+        lanes = slice(b * BLK, (b + 1) * BLK)
+        cum_t[:, lanes] = sum(dot(part, upper) for part in terms(forget_ref[:, lanes], 3))
+    turned[:heads, :] = cum_t[...]
+    wide[...] = turned[...].T
     before = jnp.zeros((1, heads), f32)
     for b in range(blocks):
         rows = slice(b * BLK, (b + 1) * BLK)
-        cum = sum(dot(lower, part) for part in terms(forget_ref[rows, :], 3))
-        wide[rows, :heads] = cum
-        decay = terms(jnp.exp(-(cum + before)), 3)
-        own = terms(jnp.exp(-cum), 3)
-        decay_ref[0, rows, :] = jnp.concatenate(decay, axis=1)
-        decay_ref[1, rows, :] = jnp.concatenate(own, axis=1)
+        cum = wide[rows, :heads]
+        decay_ref[0, rows, :] = jnp.concatenate(terms(jnp.exp(-(cum + before)), 3), axis=1)
+        decay_ref[1, rows, :] = jnp.concatenate(terms(jnp.exp(-cum), 3), axis=1)
         before = before + cum[BLK - 1 :, :]
-    turned = wide[...].T
-    cum_t[...] = turned[:heads]
 
     def block(b, carry):
         rows = pl.ds(pl.multiple_of(b * BLK, BLK), BLK)
@@ -140,13 +153,20 @@
             pay_ref[h, N:, :] = jnp.broadcast_to(end_early + end_late, (EXTRA, P_SIZE))
         return carry
 
-    lax.fori_loop(0, heads // 2, pair, 0)
-
-
-def pick(heads, h):
-    row = lax.broadcasted_iota(jnp.int32, (3 * heads, P_SIZE), 0)
+    lax.fori_loop(0, heads // 2, pair, 0, unroll=2)
+
+
+def pick(heads, q):
+    row = lax.broadcasted_iota(jnp.int32, (3 * heads, 2 * P_SIZE), 0)
+    lane = lax.broadcasted_iota(jnp.int32, (3 * heads, 2 * P_SIZE), 1)
+    h = 2 * q + jnp.where(lane < P_SIZE, 0, 1)
     hit = (row == h) | (row == h + heads) | (row == h + 2 * heads)
     return jnp.where(hit, 1.0, 0.0).astype(bf16)
+
+
+def side_by_side(ref, q):
+    parts = [jnp.concatenate(terms(ref[2 * q + j], 2), axis=0) for j in range(2)]
+    return jnp.concatenate(parts, axis=1)
 
 
 def within_kernel(
@@ -156,24 +176,27 @@
     read = read_ref[BLK:, :]
     read_twice = jnp.concatenate([read, read], axis=1)
 
-    def head(h, carry):
-        lanes = pl.ds(pl.multiple_of(h * P_SIZE, P_SIZE), P_SIZE)
+    def pair(q, carry):
+        lanes = pl.ds(pl.multiple_of(q * 2 * P_SIZE, 2 * P_SIZE), 2 * P_SIZE)
         w = w_ref[:, lanes]
         gate = dot(pooled_ref[...], jnp.concatenate([w, w, w], axis=0))
         silu = gate / (1.0 + jnp.exp(-gate))
-        chosen = pick(heads, h)
+        chosen = pick(heads, q)
         gain_ref[:, lanes] = silu * dot(decay_ref[0], chosen)
         stream = stream_ref[:, lanes]
-        direct = skip_ref[0, h] * stream.astype(f32)
-        early = dot(weights_ref[0, h], stream[:BLK])
-        late = dot(weights_ref[1, h], stream[BLK:])
-        state = jnp.concatenate(terms(first_ref[h], 2), axis=0)
-        late = late + dot(decay_ref[1, BLK:, :], chosen) * dot(read_twice, state)
-        base_ref[:BLK, lanes] = (early + direct[:BLK]) * silu[:BLK]
-        base_ref[BLK:, lanes] = (late + direct[BLK:]) * silu[BLK:]
+        early, late = [], []
+        for j in range(2):
+            h = 2 * q + j
+            part = stream[:, j * P_SIZE : (j + 1) * P_SIZE]
+            direct = skip_ref[0, h] * part.astype(f32)
+            early.append(dot(weights_ref[0, h], part[:BLK]) + direct[:BLK])
+            late.append(dot(weights_ref[1, h], part[BLK:]) + direct[BLK:])
+        carried = dot(decay_ref[1, BLK:, :], chosen) * dot(read_twice, side_by_side(first_ref, q))
+        base_ref[:BLK, lanes] = jnp.concatenate(early, axis=1) * silu[:BLK]
+        base_ref[BLK:, lanes] = (jnp.concatenate(late, axis=1) + carried) * silu[BLK:]
         return carry
 
-    lax.fori_loop(0, heads, head, 0)
+    lax.fori_loop(0, heads // 2, pair, 0)
 
 
 def total_kernel(got_ref, total_ref):
@@ -183,16 +206,17 @@
         gone = got_ref[i, N:, :]
         state = jnp.exp(-gone[:1]) * state + got_ref[i, :N, :]
         log = log + gone
-    total_ref[:N, :] = state
-    total_ref[N:, :] = log
-
-
-def join_kernel(total_ref, near_ref, out_ref):
-    out_ref[...] = total_ref[:N, :] + jnp.exp(-total_ref[N : N + 1, :]) * near_ref[:N, :]
-
-
-def spread_kernel(got_ref, near_ref, far_ref, out_ref):
-    state = near_ref[:N, :] + jnp.exp(-near_ref[N : N + 1, :]) * far_ref[...]
+    for k in range(total_ref.shape[0]):
+        total_ref[k, :N, :] = state
+        total_ref[k, N:, :] = log
+
+
+def spread_kernel(got_ref, totals_ref, place_ref, out_ref):
+    place = place_ref[0]
+    state = jnp.zeros(out_ref.shape[1:], f32)
+    for k in range(totals_ref.shape[0] - 1):
+        later = jnp.exp(-totals_ref[k, N : N + 1, :]) * state + totals_ref[k, :N, :]
+        state = jnp.where(k < place, later, state)
     for i in range(got_ref.shape[0]):
         out_ref[i] = state
         state = jnp.exp(-got_ref[i, N : N + 1, :]) * state + got_ref[i, :N, :]
@@ -204,36 +228,43 @@
     read_twice = jnp.concatenate([read, read], axis=1)
     acc[...] = jnp.zeros_like(acc)
 
-    def head(h, carry):
-        lanes = pl.ds(pl.multiple_of(h * P_SIZE, P_SIZE), P_SIZE)
-        state = jnp.concatenate(terms(state_ref[h], 2), axis=0)
-        gated = base_ref[:, lanes] + gain_ref[:, lanes] * dot(read_twice, state)
+    def pair(q, carry):
+        lanes = pl.ds(pl.multiple_of(q * 2 * P_SIZE, 2 * P_SIZE), 2 * P_SIZE)
+        gated = base_ref[:, lanes] + gain_ref[:, lanes] * dot(read_twice, side_by_side(state_ref, q))
         gated_ref[:, lanes] = gated
-        acc[...] += gated * gated
+        squares = gated * gated
+        acc[...] += squares[:, :P_SIZE] + squares[:, P_SIZE:]
         return carry
 
-    lax.fori_loop(0, heads, head, 0)
+    lax.fori_loop(0, heads // 2, pair, 0, unroll=2)
     energy_ref[...] = jnp.sum(acc[...].T, axis=0, keepdims=True)
 
 
-def norm_kernel(gated_ref, mine_ref, other_ref, gain_ref, out_ref):
+def norm_kernel(gated_ref, mine_ref, other_ref, gain_ref, out_ref, held, sems):
     inverse = lax.rsqrt((mine_ref[...] + other_ref[...]) / DI + EPSILON)
-    column = jnp.broadcast_to(inverse, (P_SIZE, inverse.shape[1])).T
-
-    def head(h, carry):
-        lanes = pl.ds(pl.multiple_of(h * P_SIZE, P_SIZE), P_SIZE)
-        out_ref[:, lanes] = (gated_ref[:, lanes] * column * gain_ref[:, lanes]).astype(bf16)
-        return carry
-
-    lax.fori_loop(0, gated_ref.shape[1] // P_SIZE, head, 0)
-
-
-def call(kernel, ins, outs, scratch=(), specs=None):
+    copies = []
+    for k in range(held.shape[0] // P_SIZE):
+        rows = slice(k * P_SIZE, (k + 1) * P_SIZE)
+        column = jnp.broadcast_to(inverse[:, rows], (P_SIZE, P_SIZE)).T
+
+        def head(h, carry):
+            lanes = pl.ds(pl.multiple_of(h * P_SIZE, P_SIZE), P_SIZE)
+            held[rows, lanes] = (gated_ref[rows, lanes] * column * gain_ref[:, lanes]).astype(bf16)
+            return carry
+
+        lax.fori_loop(0, held.shape[1] // P_SIZE, head, 0, unroll=4)
+        copies.append(pltpu.make_async_copy(held.at[rows], out_ref.at[rows], sems.at[k]))
+        copies[-1].start()
+    for copy in copies:
+        copy.wait()
+
+
+def call(kernel, ins, outs, scratch=(), specs=None, out_specs=None):
     return pl.pallas_call(
         kernel,
         out_shape=[jax.ShapeDtypeStruct(shape, dtype) for shape, dtype in outs],
         in_specs=specs or [VMEM] * len(ins),
-        out_specs=[VMEM] * len(outs),
+        out_specs=out_specs or [VMEM] * len(outs),
         scratch_shapes=list(scratch),
         compiler_params=PARAMS,
     )(*ins)
@@ -263,31 +294,43 @@
     pixels, bins = depth_logits.shape[1:]
     shards = lax.axis_size("ctx")
     groups = [list(range(g, g + heads)) for g in range(0, shards, heads)]
-
-    (partial_sum,) = call(
+    peers = [list(range(g, shards, heads)) for g in range(heads)]
+    place = (lax.axis_index("ctx") // heads).astype(jnp.int32).reshape(1)
+
+    near = (depth_logits.transpose(2, 0, 1), cell_index.transpose(2, 0, 1), features[0].T)
+    far = (forget.T, input_map, output_map, frame_ids.reshape(1, tokens))
+    far += (w_visual, embed, w_gate, norm_gain.reshape(1, width))
+    partial_sum, forget, input_map, output_map, frames, w_visual, embed, w_gate, norm_gain = call(
         pool_kernel,
-        (depth_logits[0], cell_index[0], features[0]),
-        [((tokens // 2, 2 * CF), f32)],
+        tuple(pltpu.with_memory_space_constraint(array, pltpu.HBM) for array in near + far),
+        [((tokens // 2, 2 * CF), f32)] + [(array.shape, array.dtype) for array in far],
         [
-            pltpu.VMEM((pixels, 128), f32),
-            pltpu.VMEM((bins, pixels), f32),
-            pltpu.VMEM((bins, pixels), f32),
+            pltpu.VMEM((bins, 1, pixels), f32),
+            pltpu.VMEM((bins, 1, pixels), jnp.int32),
+            pltpu.VMEM((CF, pixels), bf16),
+            pltpu.VMEM((bins, 1, pixels), f32),
             pltpu.VMEM((tokens, 2 * pixels), bf16),
+            pltpu.SemaphoreType.DMA((3 + len(far),)),
         ],
+        specs=[HBM] * (3 + len(far)),
     )
     chip_sum = partial_sum + swap(partial_sum, "mp")
     other_sum = swap(chip_sum, "section")
 
     weights, keys, ends, decay = call(
         mask_kernel,
-        (forget, input_map, output_map, frame_ids.reshape(1, tokens)),
+        (forget, input_map, output_map, frames),
         [
             ((blocks, heads, BLK, BLK), bf16),
             ((blocks, heads, N, BLK), bf16),
             ((blocks, heads, 128), f32),
             ((2, tokens, 3 * heads), bf16),
         ],
-        [pltpu.VMEM((tokens, 128), f32), pltpu.VMEM((heads, tokens), f32)],
+        [
+            pltpu.VMEM((tokens, 128), f32),
+            pltpu.VMEM((128, tokens), f32),
+            pltpu.VMEM((heads, tokens), f32),
+        ],
     )
 
     stream, pay, first, pooled = call(
@@ -309,11 +352,11 @@
         specs=[VMEM] * 4 + [SMEM] + [VMEM] * 3,
     )
 
-    (total,) = call(total_kernel, (got,), [((N + EXTRA, P_SIZE), f32)])
-    near = lax.ppermute(total, "ctx", [(i, i + heads) for i in range(shards - heads)])
-    (joined,) = call(join_kernel, (total, near), [((N, P_SIZE), f32)])
-    far = lax.ppermute(joined, "ctx", [(i, i + 2 * heads) for i in range(shards - 2 * heads)])
-    (sent,) = call(spread_kernel, (got, near, far), [((heads, N, P_SIZE), f32)])
+    (total,) = call(total_kernel, (got,), [((shards // heads, N + EXTRA, P_SIZE), f32)])
+    totals = lax.all_to_all(total, "ctx", 0, 0, axis_index_groups=peers, tiled=True)
+    (sent,) = call(
+        spread_kernel, (got, totals, place), [((heads, N, P_SIZE), f32)], specs=[VMEM, VMEM, SMEM]
+    )
     incoming = lax.all_to_all(sent, "ctx", 0, 0, axis_index_groups=groups, tiled=True)
 
     gated, energy = call(
@@ -326,8 +369,10 @@
     other_energy = swap(chip_energy, "section")
     (out,) = call(
         norm_kernel,
-        (gated, chip_energy, other_energy, norm_gain.reshape(1, width)),
+        (gated, chip_energy, other_energy, norm_gain),
         [((tokens, width), bf16)],
+        [pltpu.VMEM((tokens, width), bf16), pltpu.SemaphoreType.DMA((tokens // P_SIZE,))],
+        out_specs=[HBM],
     )
     return out
 

time: 108 us -> 95.1 us (0.88)
  Pallas kernels: 36.3 us -> 20.9 us
  starting transfers between devices: 26.3 us -> 19.6 us
  waiting for transfers between devices: 6.9 us -> 12.5 us
  local copies, waits for them, and re-layouts: 12.2 us -> 16.3 us
    pallas_call x9 -> x8, Pallas kernels: 36.3 us -> 20.9 us  [call(): pl.pallas_call(kernel, out_shape=[jax.ShapeDtypeStruct(shape, dtype) for...]
    ppermute x2 -> x0, starting transfers between devices: 14.6 us -> none  [the longest x1 9.72 us: body(): lax.ppermute(joined, 'ctx', [(i, i + 2 * heads) for i in range(shards - 2...]
    all_to_all x0 -> x1, waiting for transfers between devices: none -> 8.19 us  [body(): lax.all_to_all(total, 'ctx', 0, 0, axis_index_groups=peers, tiled=True)]
    all_to_all x0 -> x1, starting transfers between devices: none -> 7.28 us  [body(): lax.all_to_all(total, 'ctx', 0, 0, axis_index_groups=peers, tiled=True)]
    unnamed x34 -> x32, local copies, waits for them, and re-layouts: 12.2 us -> 16.3 us
    ppermute x2 -> x0, waiting for transfers between devices: 2.66 us -> none  [the longest x1 1.35 us: body(): lax.ppermute(total, 'ctx', [(i, i + heads) for i in range(shards - heads)])]
  transfers between devices with their start and end apart: 7 -> 6, of which waited for: 5 -> 5; matrix products, arithmetic and copies ran while one was open for 1% -> 0% of each run, Pallas kernels for 15% -> 8%
where the time goes in v2:
time: 95.1 us; the launch traced here: 94.6 us
  blocking collectives  25.1 us (26%)
  Pallas kernels  20.9 us (22%)
  starting transfers between devices  19.6 us (21%)
  local copies, waits for them, and re-layouts  16.3 us (17%)
  waiting for transfers between devices  12.5 us (13%)
    all_to_all x1, blocking collectives, body(): got = lax.all_to_all(pay, 'ctx', 0, 0, axis_index_groups=groups, tiled=True)  25.1 us
    pallas_call x8, Pallas kernels, call(): pl.pallas_call(kernel, out_shape=[jax.ShapeDtypeStruct(shape, dtype) for...  20.9 us
    unnamed x32, local copies, waits for them, and re-layouts  16.3 us
    ppermute x4, starting transfers between devices, swap(): return lax.ppermute(value, axis, [(0, 1), (1, 0)])  8.53 us
    all_to_all x1, waiting for transfers between devices, body(): lax.all_to_all(total, 'ctx', 0, 0, axis_index_groups=peers, tiled=True)  8.19 us
    all_to_all x1, starting transfers between devices, body(): lax.all_to_all(total, 'ctx', 0, 0, axis_index_groups=peers, tiled=True)  7.28 us
    ppermute x4, waiting for transfers between devices, swap(): return lax.ppermute(value, axis, [(0, 1), (1, 0)])  4.32 us
    all_to_all x1, starting transfers between devices, body(): lax.all_to_all(sent, 'ctx', 0, 0, axis_index_groups=groups, tiled=True)  3.79 us
  transfers between devices with their start and end apart: 6, of which 5 were waited for; matrix products, arithmetic and copies ran while one was open for 0% of the time, Pallas kernels for 8%

profile of v2, /device:TPU:1, one launch (start us, length us, event | category | flops | bytes accessed | tf_op | source)
XLA Modules:
  0.0 94.6 jit_solution(2423307359216750775)
XLA Ops:
  0.0 3.9 %shard_map.118 = (f32[256,128]{1,0:T(8,128)S(1)}, f32[16,512]{1,0:T(8,128)S(1)}, bf16[512,128]{1,0:T(8,128)(2,1)S(1)}, bf16[512,128]{1,0:T(8,128)(2,1)S(1)}, s32...) custom-call(f32[41,1,256]{2,1,0:T(1,128)} %bitcast.11, ...), custom_call_target="tpu_custom_call" | custom-call | tf_op jit(solution)/shard_map/pallas_call | solution.py:263
  3.9 3.3 %collective-permute-start = (f32[256,128]{1,0:T(8,128)S(1)}, f32[256,128]{1,0:T(8,128)S(1)}, u32[]{:S(2)}, u32[]{:S(2)}) collective-permute-start(f32[256,128]{1,0:T(8,128)S(1)} %get-tuple-element.26), channel_id=1, source_target_pairs={{0,1},{1,0},{2,3},{3,2},{4,5},{5,4},{6,7},{7,6},{8,9},{9,8},{10,11... | collective-permute-start | bytes 393224 | tf_op jit(solution)/shard_map/ppermute | solution.py:274
  7.2 1.0 %collective-permute-done = f32[256,128]{1,0:T(8,128)S(1)} collective-permute-done((f32[256,128]{1,0:T(8,128)S(1)}, f32[256,128]{1,0:T(8,128)S(1)}, u32[]{:S(2)}, u32[]{:S(2)}) %collective-permute-start) | collective-permute-done | bytes 131104 | tf_op jit(solution)/shard_map/ppermute | solution.py:274
  8.3 2.7 %shard_map.119 = (bf16[2,16,256,256]{3,2,1,0:T(8,128)(2,1)S(1)}, bf16[2,16,128,256]{3,2,1,0:T(8,128)(2,1)S(1)}, f32[2,16,128]{2,1,0:T(8,128)S(1)}, bf16[2,512,48]{2,1,0:T(8,128)(2,1)S(1)}) custom-call(f32[16,512]{1,0:T(8,128)S(1)} %get-tuple-element.29.forget_ref, bf16[512,128]{1,0:T(8,128)(2,1)S(1)} %get-tuple-element.30.in_ref, ...), custom_call_target="tpu_custom_call" | custom-call | tf_op jit(solution)/shard_map/pallas_call | solution.py:263
  11.0 1.9 %copy-done.4 = bf16[2,16,256,256]{3,2,1,0:T(8,128)(2,1)} copy-done((bf16[2,16,256,256]{3,2,1,0:T(8,128)(2,1)}, bf16[2,16,256,256]{3,2,1,0:T(8,128)(2,1)S(1)}, u32[]{:S(2)}) %copy-start.4) | copy-done | bytes 4194328
  13.0 3.6 %shard_map.120 = (bf16[512,2048]{1,0:T(8,128)(2,1)S(1)}, f32[16,136,128]{2,1,0:T(8,128)S(1)}, f32[16,128,128]{2,1,0:T(8,128)S(1)}, bf16[512,192]{1,0:T(8,128)(2,1)S(1)}) custom-call(f32[256,128]{1,0:T(8,128)S(1)} %add.7.mine_ref, f32[256,128]{1,0:T(8,128)S(1)} %collective-permute-done.1.other_ref, bf16[64,2048]{1,0:T(8,128)(2,1)S(1)} %get-tuple-element.27.w_ref, ...), custom_call_target="tpu_custom_call" | custom-call | tf_op jit(solution)/shard_map/pallas_call | solution.py:263
  16.7 25.1 %all_to_all.15.got_ref = f32[16,136,128]{2,1,0:T(8,128)S(1)} all-to-all(f32[16,136,128]{2,1,0:T(8,128)S(1)} %get-tuple-element.35), channel_id=1, replica_groups={{0,2,4,6,8,10,12,14,16,18,20,22,24,26,28,30},{32,34,36,38,40,42,44,46,4..., dimensions={0} | all-to-all | bytes 2228224 | tf_op jit(solution)/shard_map/all_to_all | solution.py:346
  42.6 7.3 %all-to-all-start.1 = ((f32[4,136,128]{2,1,0:T(8,128)}), f32[4,136,128]{2,1,0:T(8,128)}, u32[]{:S(2)}, u32[]{:S(2)}) async-start(f32[4,136,128]{2,1,0:T(8,128)} %copy-done.6), calls=%async_computation.1 | async-start | bytes 557056 | tf_op jit(solution)/shard_map/all_to_all | solution.py:356
  49.8 8.2 %all-to-all-done.1.totals_ref = f32[4,136,128]{2,1,0:T(8,128)} async-done(((f32[4,136,128]{2,1,0:T(8,128)}), f32[4,136,128]{2,1,0:T(8,128)}, u32[]{:S(2)}, u32[]{:S(2)}) %all-to-all-start.1) | async-done | bytes 278560 | tf_op jit(solution)/shard_map/all_to_all | solution.py:356
  58.0 2.1 %shard_map.122 = f32[16,128,128]{2,1,0:T(8,128)} custom-call(f32[16,136,128]{2,1,0:T(8,128)S(1)} %all_to_all.15.got_ref, f32[4,136,128]{2,1,0:T(8,128)} %all-to-all-done.1.totals_ref, s32[1]{0:T(128)} %bitcast.7.place_ref), custom_call_target="tpu_custom_call" | custom-call | tf_op jit(solution)/shard_map/pallas_call | solution.py:263
  60.1 3.8 %all-to-all-start.2 = ((f32[16,128,128]{2,1,0:T(8,128)}), f32[16,128,128]{2,1,0:T(8,128)S(1)}, u32[]{:S(2)}, u32[]{:S(2)}) async-start(f32[16,128,128]{2,1,0:T(8,128)} %shard_map.122), calls=%async_computation.2 | async-start | bytes 2097152 | tf_op jit(solution)/shard_map/all_to_all | solution.py:360
  63.9 2.2 %copy-done.5 = bf16[2,16,256,256]{3,2,1,0:T(8,128)(2,1)S(1)} copy-done((bf16[2,16,256,256]{3,2,1,0:T(8,128)(2,1)S(1)}, bf16[2,16,256,256]{3,2,1,0:T(8,128)(2,1)}, u32[]{:S(2)}) %copy-start.5) | copy-done | bytes 4194328
  66.1 1.2 %copy-done.8 = f32[16,128,128]{2,1,0:T(8,128)S(1)} copy-done((f32[16,128,128]{2,1,0:T(8,128)S(1)}, f32[16,128,128]{2,1,0:T(8,128)}, u32[]{:S(2)}) %copy-start.8) | copy-done | bytes 1048600
  67.3 0.9 %copy-done.12 = bf16[2,512,48]{2,1,0:T(8,128)(2,1)S(1)} copy-done((bf16[2,512,48]{2,1,0:T(8,128)(2,1)S(1)}, bf16[2,512,48]{2,1,0:T(8,128)(2,1)}, u32[]{:S(2)}) %copy-start.12) | copy-done | bytes 98328
  68.3 0.9 %copy-done.14 = bf16[512,192]{1,0:T(8,128)(2,1)S(1)} copy-done((bf16[512,192]{1,0:T(8,128)(2,1)S(1)}, bf16[512,192]{1,0:T(8,128)(2,1)}, u32[]{:S(2)}) %copy-start.14) | copy-done | bytes 196632
  69.2 4.8 %shard_map.123 = (f32[512,2048]{1,0:T(8,128)S(1)}, f32[512,2048]{1,0:T(8,128)S(1)}) custom-call(bf16[2,16,256,256]{3,2,1,0:T(8,128)(2,1)S(1)} %copy-done.5, bf16[512,2048]{1,0:T(8,128)(2,1)S(1)} %get-tuple-element.37.stream_ref, bf16[512,192]{1,0:T(8,128)(2,1)S(1)} %copy-done.14, bf16[64,2048]{1,0:T(8,128)(2,1)S(1)} %copy-done.10, f32[1,16]{1,0:T(1,128)S(1)} %bitcast.10, ...), custom_call_target="tpu_custom_call" | custom-call | tf_op jit(solution)/shard_map/pallas_call | solution.py:263
  74.0 1.9 %copy-done = f32[512,2048]{1,0:T(8,128)} copy-done((f32[512,2048]{1,0:T(8,128)}, f32[512,2048]{1,0:T(8,128)S(1)}, u32[]{:S(2)}) %copy-start) | copy-done | bytes 4194328
  76.0 2.0 %copy-done.2 = f32[512,2048]{1,0:T(8,128)} copy-done((f32[512,2048]{1,0:T(8,128)}, f32[512,2048]{1,0:T(8,128)S(1)}, u32[]{:S(2)}) %copy-start.2) | copy-done | bytes 4194328
  78.0 2.2 %copy-done.1 = f32[512,2048]{1,0:T(8,128)S(1)} copy-done((f32[512,2048]{1,0:T(8,128)S(1)}, f32[512,2048]{1,0:T(8,128)}, u32[]{:S(2)}) %copy-start.1) | copy-done | bytes 4194328
  80.2 2.2 %copy-done.3 = f32[512,2048]{1,0:T(8,128)S(1)} copy-done((f32[512,2048]{1,0:T(8,128)S(1)}, f32[512,2048]{1,0:T(8,128)}, u32[]{:S(2)}) %copy-start.3) | copy-done | bytes 4194328
  82.4 1.6 %shard_map.124 = (f32[512,2048]{1,0:T(8,128)S(1)}, f32[1,512]{1,0:T(1,128)S(1)}) custom-call(f32[16,128,128]{2,1,0:T(8,128)S(1)} %all-to-all-done.2.state_ref, bf16[512,128]{1,0:T(8,128)(2,1)S(1)} %get-tuple-element.31.read_ref, f32[512,2048]{1,0:T(8,128)S(1)} %copy-done.1, f32[512,2048]{1,0:T(8,128)S(1)} %copy-done.3), custom_call_target="tpu_custom_call" | custom-call | tf_op jit(solution)/shard_map/pallas_call | solution.py:263
  84.0 5.1 %collective-permute-start.2 = (f32[1,512]{1,0:T(1,128)S(1)}, f32[1,512]{1,0:T(1,128)S(1)}, u32[]{:S(2)}, u32[]{:S(2)}) collective-permute-start(f32[1,512]{1,0:T(1,128)S(1)} %get-tuple-element.45), channel_id=1, source_target_pairs={{0,1},{1,0},{2,3},{3,2},{4,5},{5,4},{6,7},{7,6},{8,9},{9,8},{10,11... | collective-permute-start | bytes 6152 | tf_op jit(solution)/shard_map/ppermute | solution.py:274
  89.9 2.4 %collective-permute-done.3.other_ref = f32[1,512]{1,0:T(1,128)S(1)} collective-permute-done((f32[1,512]{1,0:T(1,128)S(1)}, f32[1,512]{1,0:T(1,128)S(1)}, u32[]{:S(2)}, u32[]{:S(2)}) %collective-permute-start.3) | collective-permute-done | bytes 2080 | tf_op jit(solution)/shard_map/ppermute | solution.py:274
  92.4 2.2 %shard_map.125 = bf16[512,2048]{1,0:T(8,128)(2,1)} custom-call(f32[512,2048]{1,0:T(8,128)S(1)} %get-tuple-element.44.gated_ref, f32[1,512]{1,0:T(1,128)S(1)} %add.8.mine_ref, f32[1,512]{1,0:T(1,128)S(1)} %collective-permute-done.3.other_ref, f32[1,2048]{1,0:T(1,128)S(1)} %get-tuple-element.46.gain_ref), custom_call_target="tpu_custom_call" | custom-call | tf_op jit(solution)/shard_map/pallas_call | solution.py:263
  (31 shorter events, 1.8 us)
Async XLA Ops:
  3.9 4.4 %copy-start.9 = (bf16[64,2048]{1,0:T(8,128)(2,1)}, bf16[64,2048]{1,0:T(8,128)(2,1)S(1)}, u32[]{:S(2)}) copy-start(bf16[64,2048]{1,0:T(8,128)(2,1)S(1)} %get-tuple-element.39.w_ref) | copy-start | bytes 786436
  3.9 4.3 %collective-permute-start = (f32[256,128]{1,0:T(8,128)S(1)}, f32[256,128]{1,0:T(8,128)S(1)}, u32[]{:S(2)}, u32[]{:S(2)}) collective-permute-start(f32[256,128]{1,0:T(8,128)S(1)} %get-tuple-element.26), channel_id=1, source_target_pairs={{0,1},{1,0},{2,3},{3,2},{4,5},{5,4},{6,7},{7,6},{8,9},{9,8},{10,11... | collective-permute-start | bytes 393224 | tf_op jit(solution)/shard_map/ppermute | solution.py:274
  8.2 4.8 %collective-permute-start.1 = (f32[256,128]{1,0:T(8,128)S(1)}, f32[256,128]{1,0:T(8,128)S(1)}, u32[]{:S(2)}, u32[]{:S(2)}) collective-permute-start(f32[256,128]{1,0:T(8,128)S(1)} %add.7.mine_ref), channel_id=1, source_target_pairs={{0,128},{128,0},{1,129},{129,1},{2,130},{130,2},{3,131},{131,3},{4... | collective-permute-start | bytes 393224 | tf_op jit(solution)/shard_map/ppermute | solution.py:274
  11.0 1.9 %copy-start.4 = (bf16[2,16,256,256]{3,2,1,0:T(8,128)(2,1)}, bf16[2,16,256,256]{3,2,1,0:T(8,128)(2,1)S(1)}, u32[]{:S(2)}) copy-start(bf16[2,16,256,256]{3,2,1,0:T(8,128)(2,1)S(1)} %get-tuple-element.36.weights_ref) | copy-start | bytes 12582916
  12.9 3.7 %copy-start.11 = (bf16[2,512,48]{2,1,0:T(8,128)(2,1)}, bf16[2,512,48]{2,1,0:T(8,128)(2,1)S(1)}, u32[]{:S(2)}) copy-start(bf16[2,512,48]{2,1,0:T(8,128)(2,1)S(1)} %get-tuple-element.41.decay_ref) | copy-start | bytes 294916
  16.7 25.1 %copy-start.7 = (f32[16,128,128]{2,1,0:T(8,128)}, f32[16,128,128]{2,1,0:T(8,128)S(1)}, u32[]{:S(2)}) copy-start(f32[16,128,128]{2,1,0:T(8,128)S(1)} %get-tuple-element.40.first_ref) | copy-start | bytes 3145732
  16.7 25.1 %copy-start.13 = (bf16[512,192]{1,0:T(8,128)(2,1)}, bf16[512,192]{1,0:T(8,128)(2,1)S(1)}, u32[]{:S(2)}) copy-start(bf16[512,192]{1,0:T(8,128)(2,1)S(1)} %get-tuple-element.38.pooled_ref) | copy-start | bytes 589828
  41.9 0.7 copy-start.6
  42.6 15.5 %all-to-all-start.1 = ((f32[4,136,128]{2,1,0:T(8,128)}), f32[4,136,128]{2,1,0:T(8,128)}, u32[]{:S(2)}, u32[]{:S(2)}) async-start(f32[4,136,128]{2,1,0:T(8,128)} %copy-done.6), calls=%async_computation.1 | async-start | bytes 557056 | tf_op jit(solution)/shard_map/all_to_all | solution.py:356
  58.0 5.9 %copy-start.15 = (f32[16]{0:T(128)S(1)}, f32[16]{0:T(128)}, u32[]{:S(2)}) copy-start(f32[16]{0:T(128)} %param.21) | copy-start | bytes 196
  60.1 3.8 %copy-start.10 = (bf16[64,2048]{1,0:T(8,128)(2,1)S(1)}, bf16[64,2048]{1,0:T(8,128)(2,1)}, u32[]{:S(2)}) copy-start(bf16[64,2048]{1,0:T(8,128)(2,1)} %copy-done.9) | copy-start | bytes 786436
  60.1 17.9 %all-to-all-start.2 = ((f32[16,128,128]{2,1,0:T(8,128)}), f32[16,128,128]{2,1,0:T(8,128)S(1)}, u32[]{:S(2)}, u32[]{:S(2)}) async-start(f32[16,128,128]{2,1,0:T(8,128)} %shard_map.122), calls=%async_computation.2 | async-start | bytes 2097152 | tf_op jit(solution)/shard_map/all_to_all | solution.py:360
  63.9 2.2 %copy-start.5 = (bf16[2,16,256,256]{3,2,1,0:T(8,128)(2,1)S(1)}, bf16[2,16,256,256]{3,2,1,0:T(8,128)(2,1)}, u32[]{:S(2)}) copy-start(bf16[2,16,256,256]{3,2,1,0:T(8,128)(2,1)} %copy-done.4) | copy-start | bytes 12582916
  66.1 1.2 %copy-start.8 = (f32[16,128,128]{2,1,0:T(8,128)S(1)}, f32[16,128,128]{2,1,0:T(8,128)}, u32[]{:S(2)}) copy-start(f32[16,128,128]{2,1,0:T(8,128)} %copy-done.7) | copy-start | bytes 3145732
  67.3 0.9 %copy-start.12 = (bf16[2,512,48]{2,1,0:T(8,128)(2,1)S(1)}, bf16[2,512,48]{2,1,0:T(8,128)(2,1)}, u32[]{:S(2)}) copy-start(bf16[2,512,48]{2,1,0:T(8,128)(2,1)} %copy-done.11) | copy-start | bytes 294916
  68.3 0.9 %copy-start.14 = (bf16[512,192]{1,0:T(8,128)(2,1)S(1)}, bf16[512,192]{1,0:T(8,128)(2,1)}, u32[]{:S(2)}) copy-start(bf16[512,192]{1,0:T(8,128)(2,1)} %copy-done.13) | copy-start | bytes 589828
  74.0 1.9 %copy-start = (f32[512,2048]{1,0:T(8,128)}, f32[512,2048]{1,0:T(8,128)S(1)}, u32[]{:S(2)}) copy-start(f32[512,2048]{1,0:T(8,128)S(1)} %get-tuple-element.42.base_ref) | copy-start | bytes 12582916
  76.0 2.0 %copy-start.2 = (f32[512,2048]{1,0:T(8,128)}, f32[512,2048]{1,0:T(8,128)S(1)}, u32[]{:S(2)}) copy-start(f32[512,2048]{1,0:T(8,128)S(1)} %get-tuple-element.43.gain_ref) | copy-start | bytes 12582916
  78.0 2.2 %copy-start.1 = (f32[512,2048]{1,0:T(8,128)S(1)}, f32[512,2048]{1,0:T(8,128)}, u32[]{:S(2)}) copy-start(f32[512,2048]{1,0:T(8,128)} %copy-done) | copy-start | bytes 12582916
  80.2 2.2 %copy-start.3 = (f32[512,2048]{1,0:T(8,128)S(1)}, f32[512,2048]{1,0:T(8,128)}, u32[]{:S(2)}) copy-start(f32[512,2048]{1,0:T(8,128)} %copy-done.2) | copy-start | bytes 12582916
  84.0 5.9 %collective-permute-start.2 = (f32[1,512]{1,0:T(1,128)S(1)}, f32[1,512]{1,0:T(1,128)S(1)}, u32[]{:S(2)}, u32[]{:S(2)}) collective-permute-start(f32[1,512]{1,0:T(1,128)S(1)} %get-tuple-element.45), channel_id=1, source_target_pairs={{0,1},{1,0},{2,3},{3,2},{4,5},{5,4},{6,7},{7,6},{8,9},{9,8},{10,11... | collective-permute-start | bytes 6152 | tf_op jit(solution)/shard_map/ppermute | solution.py:274
  89.9 2.4 %collective-permute-start.3 = (f32[1,512]{1,0:T(1,128)S(1)}, f32[1,512]{1,0:T(1,128)S(1)}, u32[]{:S(2)}, u32[]{:S(2)}) collective-permute-start(f32[1,512]{1,0:T(1,128)S(1)} %add.8.mine_ref), channel_id=1, source_target_pairs={{0,128},{128,0},{1,129},{129,1},{2,130},{130,2},{3,131},{131,3},{4... | collective-permute-start | bytes 6152 | tf_op jit(solution)/shard_map/ppermute | solution.py:274

commit v3 on v2

--- a/solution.py
+++ b/solution.py
@@ -40,6 +40,13 @@
     return jnp.dot(a, b, preferred_element_type=f32)
 
 
+def fetch(far, near, sems):
+    copies = [pltpu.make_async_copy(f, n, sems.at[i]) for i, (f, n) in enumerate(zip(far, near))]
+    for copy in copies:
+        copy.start()
+    return copies
+
+
 def pool_kernel(*refs):
     count = (len(refs) - 4) // 2
     far, out_ref, near = refs[:count], refs[count], refs[count + 1 : 2 * count - 2]
@@ -80,60 +87,55 @@
         copy.wait()
 
 
-def mask_kernel(
-    forget_ref, in_ref, read_ref, frames_ref, weights_ref, keys_ref, ends_ref, decay_ref, wide, turned, cum_t
+def decay_kernel(
+    forget_ref, in_ref, keys_ref, ends_ref, columns_out, rows_out, columns_ref, rows_ref, wide, turned, sems
 ):
     heads = forget_ref.shape[0]
-    blocks = weights_ref.shape[0]
+    blocks = keys_ref.shape[0]
     row_order = lax.broadcasted_iota(jnp.int32, (BLK, BLK), 0)
     col_order = lax.broadcasted_iota(jnp.int32, (BLK, BLK), 1)
-    causal = col_order <= row_order
     upper = jnp.where(row_order <= col_order, 1.0, 0.0).astype(bf16)
     for b in range(blocks):
-        lanes = slice(b * BLK, (b + 1) * BLK)
-        cum_t[:, lanes] = sum(dot(part, upper) for part in terms(forget_ref[:, lanes], 3))
-    turned[:heads, :] = cum_t[...]
+        span = slice(b * BLK, (b + 1) * BLK)
+        cum = sum(dot(part, upper) for part in terms(forget_ref[:, span], 3))
+        turned[:heads, span] = cum
+        end = cum[:, BLK - 1 :]
+        rise = jnp.exp(cum - end)
+        ends_ref[b] = jnp.broadcast_to(end, (heads, 128))
+        write_t = in_ref[span, :].astype(f32).T
+        for h in range(heads):
+            keys_ref[b, h] = (write_t * rise[h : h + 1, :]).astype(bf16)
+    rows_ref[...] = turned[:heads, :] * LOG2E
     wide[...] = turned[...].T
     before = jnp.zeros((1, heads), f32)
     for b in range(blocks):
-        rows = slice(b * BLK, (b + 1) * BLK)
-        cum = wide[rows, :heads]
-        decay_ref[0, rows, :] = jnp.concatenate(terms(jnp.exp(-(cum + before)), 3), axis=1)
-        decay_ref[1, rows, :] = jnp.concatenate(terms(jnp.exp(-cum), 3), axis=1)
+        span = slice(b * BLK, (b + 1) * BLK)
+        cum = wide[span, :heads]
+        parts = terms(jnp.exp(-(cum + before)), 3) + terms(jnp.exp(-cum), 3) + terms(cum * LOG2E, 3)
+        columns_ref[span, :] = jnp.concatenate(parts, axis=1)
         before = before + cum[BLK - 1 :, :]
-
-    def block(b, carry):
-        rows = pl.ds(pl.multiple_of(b * BLK, BLK), BLK)
-        scores = lax.dot_general(
-            read_ref[rows, :], in_ref[rows, :], (((1,), (1,)), ((), ())), preferred_element_type=f32
-        )
-        frame_row = frames_ref[:, rows].astype(f32)
-        frame_col = jnp.broadcast_to(frame_row, (128, BLK)).T
-        same = jnp.concatenate([frame_col, frame_col], axis=1) == frame_row
-        scored = jnp.where(causal | same, scores, 0.0)
-        write_t = in_ref[rows, :].astype(f32).T
-        cum_b = cum_t[:, rows]
-        end = cum_b[:, BLK - 1 :]
-        rise = jnp.exp(cum_b - end)
-        ends_ref[b] = jnp.broadcast_to(end, (heads, 128))
-        scaled_rows = cum_b * LOG2E
-        scaled_cols = wide[rows, :] * LOG2E
-        for h in range(heads):
-            distance = jnp.abs(scaled_cols[:, h : h + 1] - scaled_rows[h : h + 1, :])
-            weights_ref[b, h] = (scored * jnp.exp2(-distance)).astype(bf16)
-            keys_ref[b, h] = (write_t * rise[h : h + 1, :]).astype(bf16)
-        return carry
-
-    lax.fori_loop(0, blocks, block, 0)
+    for copy in fetch((columns_ref, rows_ref), (columns_out, rows_out), sems):
+        copy.wait()
 
 
 def stream_kernel(
-    mine_ref, other_ref, w_ref, embed_ref, keys_ref, ends_ref, stream_ref, pay_ref, first_ref, pooled_ref
+    mine_ref, other_ref, w_ref, embed_ref, keys_ref, ends_ref, pay_ref, *refs
 ):
+    stream_out, first_out, pooled_out, stream_ref, first_ref, pooled_ref, sems = refs
     packed = mine_ref[...] + other_ref[...]
     pooled = jnp.concatenate([packed[:, :CF], packed[:, CF:]], axis=0)
     pooled_ref[...] = jnp.concatenate(terms(pooled, 3), axis=1)
     heads = first_ref.shape[0]
+    saved = pltpu.make_async_copy(pooled_ref, pooled_out, sems.at[0, heads // 2])
+    saved.start()
+
+    def results(q):
+        lanes = pl.ds(pl.multiple_of(q * 256, 256), 256)
+        both = pl.ds(2 * q, 2)
+        return (
+            pltpu.make_async_copy(stream_ref.at[:, lanes], stream_out.at[:, lanes], sems.at[0, q]),
+            pltpu.make_async_copy(first_ref.at[both], first_out.at[both], sems.at[1, q]),
+        )
 
     def pair(q, carry):
         lanes = pl.ds(pl.multiple_of(q * 256, 256), 256)
@@ -151,9 +153,18 @@
             first_ref[h] = early
             pay_ref[h, :N, :] = jnp.exp(-end_late) * early + late
             pay_ref[h, N:, :] = jnp.broadcast_to(end_early + end_late, (EXTRA, P_SIZE))
+        for copy in results(q):
+            copy.start()
+        return carry
+
+    def finish(q, carry):
+        for copy in results(q):
+            copy.wait()
         return carry
 
     lax.fori_loop(0, heads // 2, pair, 0, unroll=2)
+    lax.fori_loop(0, heads // 2, finish, 0)
+    saved.wait()
 
 
 def pick(heads, q):
@@ -169,12 +180,38 @@
     return jnp.concatenate(parts, axis=1)
 
 
-def within_kernel(
-    weights_ref, stream_ref, pooled_ref, w_ref, skip_ref, first_ref, read_ref, decay_ref, base_ref, gain_ref
-):
+def within_kernel(skip_ref, *refs):
+    far, (base_out, gain_out), near = refs[:9], refs[9:11], refs[11:20]
+    base_ref, gain_ref, scored, in_sems, out_sems = refs[20:]
+    copies = fetch(far, near, in_sems)
+    in_ref, read_ref, frames_ref, rows_ref, columns_ref, w_ref, pooled_ref, first_ref, stream_ref = near
     heads = first_ref.shape[0]
+    row_order = lax.broadcasted_iota(jnp.int32, (BLK, BLK), 0)
+    col_order = lax.broadcasted_iota(jnp.int32, (BLK, BLK), 1)
+    causal = col_order <= row_order
+    for copy in copies[:3]:
+        copy.wait()
+    for b in range(scored.shape[0]):
+        span = slice(b * BLK, (b + 1) * BLK)
+        scores = lax.dot_general(
+            read_ref[span, :], in_ref[span, :], (((1,), (1,)), ((), ())), preferred_element_type=f32
+        )
+        frame_row = frames_ref[:, span].astype(f32)
+        frame_col = jnp.broadcast_to(frame_row, (128, BLK)).T
+        same = jnp.concatenate([frame_col, frame_col], axis=1) == frame_row
+        scored[b] = jnp.where(causal | same, scores, 0.0)
+    for copy in copies[3:]:
+        copy.wait()
     read = read_ref[BLK:, :]
     read_twice = jnp.concatenate([read, read], axis=1)
+    late_rows = slice(BLK, 2 * BLK)
+
+    def results(q):
+        lanes = pl.ds(pl.multiple_of(q * 2 * P_SIZE, 2 * P_SIZE), 2 * P_SIZE)
+        return (
+            pltpu.make_async_copy(base_ref.at[:, lanes], base_out.at[:, lanes], out_sems.at[0, q]),
+            pltpu.make_async_copy(gain_ref.at[:, lanes], gain_out.at[:, lanes], out_sems.at[1, q]),
+        )
 
     def pair(q, carry):
         lanes = pl.ds(pl.multiple_of(q * 2 * P_SIZE, 2 * P_SIZE), 2 * P_SIZE)
@@ -182,21 +219,36 @@
         gate = dot(pooled_ref[...], jnp.concatenate([w, w, w], axis=0))
         silu = gate / (1.0 + jnp.exp(-gate))
         chosen = pick(heads, q)
-        gain_ref[:, lanes] = silu * dot(decay_ref[0], chosen)
+        gain_ref[:, lanes] = silu * dot(columns_ref[:, : 3 * heads], chosen)
+        cum_col = dot(columns_ref[:, 6 * heads :], chosen)
         stream = stream_ref[:, lanes]
-        early, late = [], []
+        mixed = [[], []]
         for j in range(2):
             h = 2 * q + j
-            part = stream[:, j * P_SIZE : (j + 1) * P_SIZE]
-            direct = skip_ref[0, h] * part.astype(f32)
-            early.append(dot(weights_ref[0, h], part[:BLK]) + direct[:BLK])
-            late.append(dot(weights_ref[1, h], part[BLK:]) + direct[BLK:])
-        carried = dot(decay_ref[1, BLK:, :], chosen) * dot(read_twice, side_by_side(first_ref, q))
-        base_ref[:BLK, lanes] = jnp.concatenate(early, axis=1) * silu[:BLK]
-        base_ref[BLK:, lanes] = (jnp.concatenate(late, axis=1) + carried) * silu[BLK:]
+            cum_row = rows_ref[pl.ds(h, 1), :]
+            side = slice(j * P_SIZE, (j + 1) * P_SIZE)
+            for b in range(2):
+                span = slice(b * BLK, (b + 1) * BLK)
+                column = cum_col[span, side]
+                distance = jnp.abs(jnp.concatenate([column, column], axis=1) - cum_row[:, span])
+                weights = (scored[b] * jnp.exp2(-distance)).astype(bf16)
+                part = stream[span, side]
+                mixed[b].append(dot(weights, part) + skip_ref[0, h] * part.astype(f32))
+        own = dot(columns_ref[late_rows, 3 * heads : 6 * heads], chosen)
+        carried = own * dot(read_twice, side_by_side(first_ref, q))
+        base_ref[:BLK, lanes] = jnp.concatenate(mixed[0], axis=1) * silu[:BLK]
+        base_ref[BLK:, lanes] = (jnp.concatenate(mixed[1], axis=1) + carried) * silu[BLK:]
+        for copy in results(q):
+            copy.start()
+        return carry
+
+    def finish(q, carry):
+        for copy in results(q):
+            copy.wait()
         return carry
 
     lax.fori_loop(0, heads // 2, pair, 0)
+    lax.fori_loop(0, heads // 2, finish, 0)
 
 
 def total_kernel(got_ref, total_ref):
@@ -212,31 +264,48 @@
 
 
 def spread_kernel(got_ref, totals_ref, place_ref, out_ref):
-    place = place_ref[0]
+    place = place_ref[...]
     state = jnp.zeros(out_ref.shape[1:], f32)
     for k in range(totals_ref.shape[0] - 1):
         later = jnp.exp(-totals_ref[k, N : N + 1, :]) * state + totals_ref[k, :N, :]
-        state = jnp.where(k < place, later, state)
+        state = jnp.where(jnp.broadcast_to(place, state.shape) > k, later, state)
     for i in range(got_ref.shape[0]):
         out_ref[i] = state
         state = jnp.exp(-got_ref[i, N : N + 1, :]) * state + got_ref[i, :N, :]
 
 
-def carry_kernel(state_ref, read_ref, base_ref, gain_ref, gated_ref, energy_ref, acc):
+def carry_kernel(state_ref, read_far, base_far, gain_far, gated_ref, energy_ref, read_ref, base_ref, gain_ref, acc, sems):
     heads = state_ref.shape[0]
+
+    def operands(q):
+        lanes = pl.ds(pl.multiple_of(q * 2 * P_SIZE, 2 * P_SIZE), 2 * P_SIZE)
+        return (
+            pltpu.make_async_copy(base_far.at[:, lanes], base_ref.at[:, lanes], sems.at[0, q]),
+            pltpu.make_async_copy(gain_far.at[:, lanes], gain_ref.at[:, lanes], sems.at[1, q]),
+        )
+
+    first = pltpu.make_async_copy(read_far, read_ref, sems.at[0, heads // 2])
+    first.start()
+    for q in range(heads // 2):
+        for copy in operands(q):
+            copy.start()
+    acc[...] = jnp.zeros_like(acc)
+    first.wait()
     read = read_ref[...]
     read_twice = jnp.concatenate([read, read], axis=1)
-    acc[...] = jnp.zeros_like(acc)
 
     def pair(q, carry):
         lanes = pl.ds(pl.multiple_of(q * 2 * P_SIZE, 2 * P_SIZE), 2 * P_SIZE)
-        gated = base_ref[:, lanes] + gain_ref[:, lanes] * dot(read_twice, side_by_side(state_ref, q))
+        carried = dot(read_twice, side_by_side(state_ref, q))
+        for copy in operands(q):
+            copy.wait()
+        gated = base_ref[:, lanes] + gain_ref[:, lanes] * carried
         gated_ref[:, lanes] = gated
         squares = gated * gated
         acc[...] += squares[:, :P_SIZE] + squares[:, P_SIZE:]
         return carry
 
-    lax.fori_loop(0, heads // 2, pair, 0, unroll=2)
+    lax.fori_loop(0, heads // 2, pair, 0)
     energy_ref[...] = jnp.sum(acc[...].T, axis=0, keepdims=True)
 
 
@@ -259,12 +328,18 @@
         copy.wait()
 
 
-def call(kernel, ins, outs, scratch=(), specs=None, out_specs=None):
+def outside(arrays):
+    return tuple(pltpu.with_memory_space_constraint(array, pltpu.HBM) for array in arrays)
+
+
+def call(kernel, ins, outs, scratch=(), specs=None):
     return pl.pallas_call(
         kernel,
-        out_shape=[jax.ShapeDtypeStruct(shape, dtype) for shape, dtype in outs],
+        out_shape=[
+            pltpu.HBM(*out[:2]) if out[2:] else jax.ShapeDtypeStruct(*out) for out in outs
+        ],
         in_specs=specs or [VMEM] * len(ins),
-        out_specs=out_specs or [VMEM] * len(outs),
+        out_specs=[HBM if out[2:] else VMEM for out in outs],
         scratch_shapes=list(scratch),
         compiler_params=PARAMS,
     )(*ins)
@@ -295,14 +370,13 @@
     shards = lax.axis_size("ctx")
     groups = [list(range(g, g + heads)) for g in range(0, shards, heads)]
     peers = [list(range(g, shards, heads)) for g in range(heads)]
-    place = (lax.axis_index("ctx") // heads).astype(jnp.int32).reshape(1)
+    place = jnp.full((1, P_SIZE), lax.axis_index("ctx") // heads, jnp.int32)
 
     near = (depth_logits.transpose(2, 0, 1), cell_index.transpose(2, 0, 1), features[0].T)
-    far = (forget.T, input_map, output_map, frame_ids.reshape(1, tokens))
-    far += (w_visual, embed, w_gate, norm_gain.reshape(1, width))
-    partial_sum, forget, input_map, output_map, frames, w_visual, embed, w_gate, norm_gain = call(
+    far = (forget.T, input_map, w_visual, embed, norm_gain.reshape(1, width))
+    partial_sum, forget_t, writes, w_visual, embed, norm_gain = call(
         pool_kernel,
-        tuple(pltpu.with_memory_space_constraint(array, pltpu.HBM) for array in near + far),
+        outside(near + far),
         [((tokens // 2, 2 * CF), f32)] + [(array.shape, array.dtype) for array in far],
         [
             pltpu.VMEM((bins, 1, pixels), f32),
@@ -310,69 +384,91 @@
             pltpu.VMEM((CF, pixels), bf16),
             pltpu.VMEM((bins, 1, pixels), f32),
             pltpu.VMEM((tokens, 2 * pixels), bf16),
-            pltpu.SemaphoreType.DMA((3 + len(far),)),
-        ],
-        specs=[HBM] * (3 + len(far)),
+            pltpu.SemaphoreType.DMA((len(near + far),)),
+        ],
+        specs=[HBM] * len(near + far),
     )
     chip_sum = partial_sum + swap(partial_sum, "mp")
     other_sum = swap(chip_sum, "section")
 
-    weights, keys, ends, decay = call(
-        mask_kernel,
-        (forget, input_map, output_map, frames),
-        [
-            ((blocks, heads, BLK, BLK), bf16),
+    keys, ends, columns, row_sums = call(
+        decay_kernel,
+        (forget_t, writes),
+        [
             ((blocks, heads, N, BLK), bf16),
             ((blocks, heads, 128), f32),
-            ((2, tokens, 3 * heads), bf16),
-        ],
-        [
+            ((tokens, 9 * heads), bf16, True),
+            ((heads, tokens), f32, True),
+        ],
+        [
+            pltpu.VMEM((tokens, 9 * heads), bf16),
+            pltpu.VMEM((heads, tokens), f32),
             pltpu.VMEM((tokens, 128), f32),
             pltpu.VMEM((128, tokens), f32),
-            pltpu.VMEM((heads, tokens), f32),
-        ],
-    )
-
-    stream, pay, first, pooled = call(
+            pltpu.SemaphoreType.DMA((2,)),
+        ],
+    )
+
+    pay, stream, first, pooled = call(
         stream_kernel,
         (chip_sum, other_sum, w_visual, embed, keys, ends),
         [
-            ((tokens, width), bf16),
             ((heads, N + EXTRA, P_SIZE), f32),
-            ((heads, N, P_SIZE), f32),
-            ((tokens, 3 * CF), bf16),
+            ((tokens, width), bf16, True),
+            ((heads, N, P_SIZE), f32, True),
+            ((tokens, 3 * CF), bf16, True),
+        ],
+        [
+            pltpu.VMEM((tokens, width), bf16),
+            pltpu.VMEM((heads, N, P_SIZE), f32),
+            pltpu.VMEM((tokens, 3 * CF), bf16),
+            pltpu.SemaphoreType.DMA((2, heads // 2 + 1)),
         ],
     )
     got = lax.all_to_all(pay, "ctx", 0, 0, axis_index_groups=groups, tiled=True)
 
+    held = (input_map, output_map, frame_ids.reshape(1, tokens), row_sums, columns)
+    held += (w_gate, pooled, first, stream)
     base, gain = call(
         within_kernel,
-        (weights, stream, pooled, w_gate, skip.reshape(1, heads), first, output_map, decay),
-        [((tokens, width), f32), ((tokens, width), f32)],
-        specs=[VMEM] * 4 + [SMEM] + [VMEM] * 3,
+        (skip.reshape(1, heads),) + outside(held),
+        [((tokens, width), f32, True), ((tokens, width), f32, True)],
+        [pltpu.VMEM(array.shape, array.dtype) for array in held]
+        + [
+            pltpu.VMEM((tokens, width), f32),
+            pltpu.VMEM((tokens, width), f32),
+            pltpu.VMEM((blocks, BLK, BLK), f32),
+            pltpu.SemaphoreType.DMA((len(held),)),
+            pltpu.SemaphoreType.DMA((2, heads // 2)),
+        ],
+        specs=[SMEM] + [HBM] * len(held),
     )
 
     (total,) = call(total_kernel, (got,), [((shards // heads, N + EXTRA, P_SIZE), f32)])
     totals = lax.all_to_all(total, "ctx", 0, 0, axis_index_groups=peers, tiled=True)
-    (sent,) = call(
-        spread_kernel, (got, totals, place), [((heads, N, P_SIZE), f32)], specs=[VMEM, VMEM, SMEM]
-    )
+    (sent,) = call(spread_kernel, (got, totals, place), [((heads, N, P_SIZE), f32)])
     incoming = lax.all_to_all(sent, "ctx", 0, 0, axis_index_groups=groups, tiled=True)
 
     gated, energy = call(
         carry_kernel,
-        (incoming, output_map, base, gain),
+        (incoming,) + outside((output_map, base, gain)),
         [((tokens, width), f32), ((1, tokens), f32)],
-        [pltpu.VMEM((tokens, P_SIZE), f32)],
+        [
+            pltpu.VMEM((tokens, N), bf16),
+            pltpu.VMEM((tokens, width), f32),
+            pltpu.VMEM((tokens, width), f32),
+            pltpu.VMEM((tokens, P_SIZE), f32),
+            pltpu.SemaphoreType.DMA((2, heads // 2 + 1)),
+        ],
+        specs=[VMEM, HBM, HBM, HBM],
     )
     chip_energy = energy + swap(energy, "mp")
     other_energy = swap(chip_energy, "section")
     (out,) = call(
         norm_kernel,
         (gated, chip_energy, other_energy, norm_gain),
-        [((tokens, width), bf16)],
+        [((tokens, width), bf16, True)],
         [pltpu.VMEM((tokens, width), bf16), pltpu.SemaphoreType.DMA((tokens // P_SIZE,))],
-        out_specs=[HBM],
     )
     return out
 

time: 95.1 us -> 92.4 us (0.972)
  local copies, waits for them, and re-layouts: 16.3 us -> 0.01 us
  Pallas kernels: 20.9 us -> 28.7 us
  waiting for transfers between devices: 12.5 us -> 17.8 us
  starting transfers between devices: 19.6 us -> 21.9 us
  blocking collectives: 25.1 us -> 23.6 us
    unnamed x32 -> x2, local copies, waits for them, and re-layouts: 16.3 us -> 0.01 us
    pallas_call x8, Pallas kernels: 20.9 us -> 28.7 us  [call(): pl.pallas_call(kernel, out_shape=[pltpu.HBM(*out[:2]) if out[2:] else jax...]
    all_to_all x1, waiting for transfers between devices: 0.01 us -> 2.76 us  [body(): lax.all_to_all(sent, 'ctx', 0, 0, axis_index_groups=groups, tiled=True)]
    ppermute x4, waiting for transfers between devices: 4.32 us -> 6.93 us  [swap(): return lax.ppermute(value, axis, [(0, 1), (1, 0)])]
    all_to_all x1, blocking collectives: 25.1 us -> 23.6 us  [body(): got = lax.all_to_all(pay, 'ctx', 0, 0, axis_index_groups=groups, tiled=True)]
    ppermute x4, starting transfers between devices: 8.53 us -> 9.77 us  [swap(): return lax.ppermute(value, axis, [(0, 1), (1, 0)])]
    all_to_all x1, starting transfers between devices: 3.79 us -> 4.88 us  [body(): lax.all_to_all(sent, 'ctx', 0, 0, axis_index_groups=groups, tiled=True)]
  transfers between devices with their start and end apart: 6 -> 6, of which waited for: 5 -> 6; matrix products, arithmetic and copies ran while one was open for 0% -> 0% of each run, Pallas kernels for 8% -> 13%
where the time goes in v3:
time: 92.4 us; the launch traced here: 92.1 us
  Pallas kernels  28.7 us (31%)
  blocking collectives  23.6 us (26%)
  starting transfers between devices  21.9 us (24%)
  waiting for transfers between devices  17.8 us (19%)
    pallas_call x8, Pallas kernels, call(): pl.pallas_call(kernel, out_shape=[pltpu.HBM(*out[:2]) if out[2:] else jax...  28.7 us
    all_to_all x1, blocking collectives, body(): got = lax.all_to_all(pay, 'ctx', 0, 0, axis_index_groups=groups, tiled=True)  23.6 us
    ppermute x4, starting transfers between devices, swap(): return lax.ppermute(value, axis, [(0, 1), (1, 0)])  9.77 us
    all_to_all x1, waiting for transfers between devices, body(): lax.all_to_all(total, 'ctx', 0, 0, axis_index_groups=peers, tiled=True)  8.13 us
    all_to_all x1, starting transfers between devices, body(): lax.all_to_all(total, 'ctx', 0, 0, axis_index_groups=peers, tiled=True)  7.3 us
    ppermute x4, waiting for transfers between devices, swap(): return lax.ppermute(value, axis, [(0, 1), (1, 0)])  6.93 us
    all_to_all x1, starting transfers between devices, body(): lax.all_to_all(sent, 'ctx', 0, 0, axis_index_groups=groups, tiled=True)  4.88 us
    all_to_all x1, waiting for transfers between devices, body(): lax.all_to_all(sent, 'ctx', 0, 0, axis_index_groups=groups, tiled=True)  2.76 us
  transfers between devices with their start and end apart: 6, of which 6 were waited for; matrix products, arithmetic and copies ran while one was open for 0% of the time, Pallas kernels for 13%

profile of v3, /device:TPU:1, one launch (start us, length us, event | category | flops | bytes accessed | tf_op | source)
XLA Modules:
  0.0 92.1 jit_solution(17642172702238511861)
XLA Ops:
  0.0 3.8 %shard_map.118 = (f32[256,128]{1,0:T(8,128)S(1)}, f32[16,512]{1,0:T(8,128)S(1)}, bf16[512,128]{1,0:T(8,128)(2,1)S(1)}, bf16[64,2048]{1,0:T(8,128)(2,1)S(1)}, bf1...) custom-call(f32[41,1,256]{2,1,0:T(1,128)} %bitcast.10, s32[41,1,256]{2,1,0:T(1,128)} %bitcast.11, ...), custom_call_target="tpu_custom_call" | custom-call | tf_op jit(solution)/shard_map/pallas_call | solution.py:336
  3.8 3.3 %collective-permute-start = (f32[256,128]{1,0:T(8,128)S(1)}, f32[256,128]{1,0:T(8,128)S(1)}, u32[]{:S(2)}, u32[]{:S(2)}) collective-permute-start(f32[256,128]{1,0:T(8,128)S(1)} %get-tuple-element.23), channel_id=1, source_target_pairs={{0,1},{1,0},{2,3},{3,2},{4,5},{5,4},{6,7},{7,6},{8,9},{9,8},{10,11... | collective-permute-start | bytes 393224 | tf_op jit(solution)/shard_map/ppermute | solution.py:349
  7.2 1.0 %collective-permute-done = f32[256,128]{1,0:T(8,128)S(1)} collective-permute-done((f32[256,128]{1,0:T(8,128)S(1)}, f32[256,128]{1,0:T(8,128)S(1)}, u32[]{:S(2)}, u32[]{:S(2)}) %collective-permute-start) | collective-permute-done | bytes 131104 | tf_op jit(solution)/shard_map/ppermute | solution.py:349
  8.2 0.1 collective-permute-start.1
  8.3 1.6 %shard_map.119 = (bf16[2,16,128,256]{3,2,1,0:T(8,128)(2,1)S(1)}, f32[2,16,128]{2,1,0:T(8,128)S(1)}, bf16[512,144]{1,0:T(8,128)(2,1)}, f32[16,512]{1,0:T(8,128)}) custom-call(f32[16,512]{1,0:T(8,128)S(1)} %get-tuple-element.26.forget_ref, bf16[512,128]{1,0:T(8,128)(2,1)S(1)} %get-tuple-element.27.in_ref), custom_call_target="tpu_custom_call" | custom-call | tf_op jit(solution)/shard_map/pallas_call | solution.py:336
  9.9 3.1 %collective-permute-done.1.other_ref = f32[256,128]{1,0:T(8,128)S(1)} collective-permute-done((f32[256,128]{1,0:T(8,128)S(1)}, f32[256,128]{1,0:T(8,128)S(1)}, u32[]{:S(2)}, u32[]{:S(2)}) %collective-permute-start.1) | collective-permute-done | bytes 131104 | tf_op jit(solution)/shard_map/ppermute | solution.py:349
  13.0 4.4 %shard_map.120 = (f32[16,136,128]{2,1,0:T(8,128)S(1)}, bf16[512,2048]{1,0:T(8,128)(2,1)}, f32[16,128,128]{2,1,0:T(8,128)}, bf16[512,192]{1,0:T(8,128)(2,1)}) custom-call(f32[256,128]{1,0:T(8,128)S(1)} %add.7.mine_ref, f32[256,128]{1,0:T(8,128)S(1)} %collective-permute-done.1.other_ref, bf16[64,2048]{1,0:T(8,128)(2,1)S(1)} %get-tuple-element.24.w_ref, ...), custom_call_target="tpu_custom_call" | custom-call | tf_op jit(solution)/shard_map/pallas_call | solution.py:336
  17.4 23.6 %all_to_all.15.got_ref = f32[16,136,128]{2,1,0:T(8,128)S(1)} all-to-all(f32[16,136,128]{2,1,0:T(8,128)S(1)} %get-tuple-element.30), channel_id=1, replica_groups={{0,2,4,6,8,10,12,14,16,18,20,22,24,26,28,30},{32,34,36,38,40,42,44,46,4..., dimensions={0} | all-to-all | bytes 2228224 | tf_op jit(solution)/shard_map/all_to_all | solution.py:428
  41.0 0.8 shard_map.121
  41.8 7.3 %all-to-all-start.1 = ((f32[4,136,128]{2,1,0:T(8,128)}), f32[4,136,128]{2,1,0:T(8,128)S(1)}, u32[]{:S(2)}, u32[]{:S(2)}) async-start(f32[4,136,128]{2,1,0:T(8,128)} %shard_map.121), calls=%async_computation.1 | async-start | bytes 557056 | tf_op jit(solution)/shard_map/all_to_all | solution.py:448
  49.1 8.1 %all-to-all-done.1.totals_ref = f32[4,136,128]{2,1,0:T(8,128)S(1)} async-done(((f32[4,136,128]{2,1,0:T(8,128)}), f32[4,136,128]{2,1,0:T(8,128)S(1)}, u32[]{:S(2)}, u32[]{:S(2)}) %all-to-all-start.1) | async-done | bytes 278560 | tf_op jit(solution)/shard_map/all_to_all | solution.py:448
  57.2 0.0 copy-start
  57.2 1.1 %shard_map.122 = f32[16,128,128]{2,1,0:T(8,128)} custom-call(f32[16,136,128]{2,1,0:T(8,128)S(1)} %all_to_all.15.got_ref, f32[4,136,128]{2,1,0:T(8,128)S(1)} %all-to-all-done.1.totals_ref, s32[1,128]{1,0:T(1,128)S(1)} %broadcast_in_dim.3.place_ref), custom_call_target="tpu_custom_call" | custom-call | tf_op jit(solution)/shard_map/pallas_call | solution.py:336
  58.3 4.9 %all-to-all-start.2 = ((f32[16,128,128]{2,1,0:T(8,128)}), f32[16,128,128]{2,1,0:T(8,128)S(1)}, u32[]{:S(2)}, u32[]{:S(2)}) async-start(f32[16,128,128]{2,1,0:T(8,128)} %shard_map.122), calls=%async_computation.2 | async-start | bytes 2097152 | tf_op jit(solution)/shard_map/all_to_all | solution.py:450
  63.2 0.0 copy-done
  63.2 10.5 %shard_map.123 = (f32[512,2048]{1,0:T(8,128)}, f32[512,2048]{1,0:T(8,128)}) custom-call(f32[1,16]{1,0:T(1,128)S(1)} %bitcast.9, bf16[512,128]{1,0:T(8,128)(2,1)} %refs_0_.1, bf16[512,128]{1,0:T(8,128)(2,1)} %read_far.1, s32[1,512]{1,0:T(1,128)} %bitcast.15, f32[16,512]{1,0:T(8,128)} %get-tuple-element.31.refs_3_, ...), custom_call_target="tpu_custom_call" | custom-call | tf_op jit(solution)/shard_map/pallas_call | solution.py:336
  73.7 2.8 %all-to-all-done.2.state_ref = f32[16,128,128]{2,1,0:T(8,128)S(1)} async-done(((f32[16,128,128]{2,1,0:T(8,128)}), f32[16,128,128]{2,1,0:T(8,128)S(1)}, u32[]{:S(2)}, u32[]{:S(2)}) %all-to-all-start.2) | async-done | bytes 1048608 | tf_op jit(solution)/shard_map/all_to_all | solution.py:450
  76.5 4.2 %shard_map.124 = (f32[512,2048]{1,0:T(8,128)S(1)}, f32[1,512]{1,0:T(1,128)S(1)}) custom-call(f32[16,128,128]{2,1,0:T(8,128)S(1)} %all-to-all-done.2.state_ref, bf16[512,128]{1,0:T(8,128)(2,1)} %read_far.1, f32[512,2048]{1,0:T(8,128)} %get-tuple-element.36.base_far, f32[512,2048]{1,0:T(8,128)} %get-tuple-element.37.gain_far), custom_call_target="tpu_custom_call" | custom-call | tf_op jit(solution)/shard_map/pallas_call | solution.py:336
  80.7 6.0 %collective-permute-start.2 = (f32[1,512]{1,0:T(1,128)S(1)}, f32[1,512]{1,0:T(1,128)S(1)}, u32[]{:S(2)}, u32[]{:S(2)}) collective-permute-start(f32[1,512]{1,0:T(1,128)S(1)} %get-tuple-element.39), channel_id=1, source_target_pairs={{0,1},{1,0},{2,3},{3,2},{4,5},{5,4},{6,7},{7,6},{8,9},{9,8},{10,11... | collective-permute-start | bytes 6152 | tf_op jit(solution)/shard_map/ppermute | solution.py:349
  86.6 0.8 collective-permute-done.2
  87.4 0.4 collective-permute-start.3
  87.8 2.0 %collective-permute-done.3.other_ref = f32[1,512]{1,0:T(1,128)S(1)} collective-permute-done((f32[1,512]{1,0:T(1,128)S(1)}, f32[1,512]{1,0:T(1,128)S(1)}, u32[]{:S(2)}, u32[]{:S(2)}) %collective-permute-start.3) | collective-permute-done | bytes 2080 | tf_op jit(solution)/shard_map/ppermute | solution.py:349
  89.9 2.2 %shard_map.125 = bf16[512,2048]{1,0:T(8,128)(2,1)} custom-call(f32[512,2048]{1,0:T(8,128)S(1)} %get-tuple-element.38.gated_ref, f32[1,512]{1,0:T(1,128)S(1)} %add.8.mine_ref, f32[1,512]{1,0:T(1,128)S(1)} %collective-permute-done.3.other_ref, f32[1,2048]{1,0:T(1,128)S(1)} %get-tuple-element.40.gain_ref), custom_call_target="tpu_custom_call" | custom-call | tf_op jit(solution)/shard_map/pallas_call | solution.py:336
  (3 shorter events, 0.0 us)
Async XLA Ops:
  3.8 4.3 %collective-permute-start = (f32[256,128]{1,0:T(8,128)S(1)}, f32[256,128]{1,0:T(8,128)S(1)}, u32[]{:S(2)}, u32[]{:S(2)}) collective-permute-start(f32[256,128]{1,0:T(8,128)S(1)} %get-tuple-element.23), channel_id=1, source_target_pairs={{0,1},{1,0},{2,3},{3,2},{4,5},{5,4},{6,7},{7,6},{8,9},{9,8},{10,11... | collective-permute-start | bytes 393224 | tf_op jit(solution)/shard_map/ppermute | solution.py:349
  8.2 4.8 %collective-permute-start.1 = (f32[256,128]{1,0:T(8,128)S(1)}, f32[256,128]{1,0:T(8,128)S(1)}, u32[]{:S(2)}, u32[]{:S(2)}) collective-permute-start(f32[256,128]{1,0:T(8,128)S(1)} %add.7.mine_ref), channel_id=1, source_target_pairs={{0,128},{128,0},{1,129},{129,1},{2,130},{130,2},{3,131},{131,3},{4... | collective-permute-start | bytes 393224 | tf_op jit(solution)/shard_map/ppermute | solution.py:349
  41.8 15.4 %all-to-all-start.1 = ((f32[4,136,128]{2,1,0:T(8,128)}), f32[4,136,128]{2,1,0:T(8,128)S(1)}, u32[]{:S(2)}, u32[]{:S(2)}) async-start(f32[4,136,128]{2,1,0:T(8,128)} %shard_map.121), calls=%async_computation.1 | async-start | bytes 557056 | tf_op jit(solution)/shard_map/all_to_all | solution.py:448
  57.2 6.0 %copy-start = (f32[16]{0:T(128)S(1)}, f32[16]{0:T(128)}, u32[]{:S(2)}) copy-start(f32[16]{0:T(128)} %param.21) | copy-start | bytes 196
  58.3 18.2 %all-to-all-start.2 = ((f32[16,128,128]{2,1,0:T(8,128)}), f32[16,128,128]{2,1,0:T(8,128)S(1)}, u32[]{:S(2)}, u32[]{:S(2)}) async-start(f32[16,128,128]{2,1,0:T(8,128)} %shard_map.122), calls=%async_computation.2 | async-start | bytes 2097152 | tf_op jit(solution)/shard_map/all_to_all | solution.py:450
  80.7 6.8 %collective-permute-start.2 = (f32[1,512]{1,0:T(1,128)S(1)}, f32[1,512]{1,0:T(1,128)S(1)}, u32[]{:S(2)}, u32[]{:S(2)}) collective-permute-start(f32[1,512]{1,0:T(1,128)S(1)} %get-tuple-element.39), channel_id=1, source_target_pairs={{0,1},{1,0},{2,3},{3,2},{4,5},{5,4},{6,7},{7,6},{8,9},{9,8},{10,11... | collective-permute-start | bytes 6152 | tf_op jit(solution)/shard_map/ppermute | solution.py:349
  87.4 2.4 %collective-permute-start.3 = (f32[1,512]{1,0:T(1,128)S(1)}, f32[1,512]{1,0:T(1,128)S(1)}, u32[]{:S(2)}, u32[]{:S(2)}) collective-permute-start(f32[1,512]{1,0:T(1,128)S(1)} %add.8.mine_ref), channel_id=1, source_target_pairs={{0,128},{128,0},{1,129},{129,1},{2,130},{130,2},{3,131},{131,3},{4... | collective-permute-start | bytes 6152 | tf_op jit(solution)/shard_map/ppermute | solution.py:349

commit v4 on v3

--- a/solution.py
+++ b/solution.py
@@ -274,31 +274,23 @@
         state = jnp.exp(-got_ref[i, N : N + 1, :]) * state + got_ref[i, :N, :]
 
 
-def carry_kernel(state_ref, read_far, base_far, gain_far, gated_ref, energy_ref, read_ref, base_ref, gain_ref, acc, sems):
+def carry_kernel(state_ref, read_ref, base_ref, gain_far, gated_ref, energy_ref, gain_ref, acc, sems):
     heads = state_ref.shape[0]
 
-    def operands(q):
+    def gains(q):
         lanes = pl.ds(pl.multiple_of(q * 2 * P_SIZE, 2 * P_SIZE), 2 * P_SIZE)
-        return (
-            pltpu.make_async_copy(base_far.at[:, lanes], base_ref.at[:, lanes], sems.at[0, q]),
-            pltpu.make_async_copy(gain_far.at[:, lanes], gain_ref.at[:, lanes], sems.at[1, q]),
-        )
-
-    first = pltpu.make_async_copy(read_far, read_ref, sems.at[0, heads // 2])
-    first.start()
+        return pltpu.make_async_copy(gain_far.at[:, lanes], gain_ref.at[:, lanes], sems.at[q])
+
     for q in range(heads // 2):
-        for copy in operands(q):
-            copy.start()
-    acc[...] = jnp.zeros_like(acc)
-    first.wait()
+        gains(q).start()
     read = read_ref[...]
     read_twice = jnp.concatenate([read, read], axis=1)
+    acc[...] = jnp.zeros_like(acc)
 
     def pair(q, carry):
         lanes = pl.ds(pl.multiple_of(q * 2 * P_SIZE, 2 * P_SIZE), 2 * P_SIZE)
         carried = dot(read_twice, side_by_side(state_ref, q))
-        for copy in operands(q):
-            copy.wait()
+        gains(q).wait()
         gated = base_ref[:, lanes] + gain_ref[:, lanes] * carried
         gated_ref[:, lanes] = gated
         squares = gated * gated
@@ -444,6 +436,7 @@
         specs=[SMEM] + [HBM] * len(held),
     )
 
+    got, base, gain = lax.optimization_barrier((got, base, gain))
     (total,) = call(total_kernel, (got,), [((shards // heads, N + EXTRA, P_SIZE), f32)])
     totals = lax.all_to_all(total, "ctx", 0, 0, axis_index_groups=peers, tiled=True)
     (sent,) = call(spread_kernel, (got, totals, place), [((heads, N, P_SIZE), f32)])
@@ -451,16 +444,14 @@
 
     gated, energy = call(
         carry_kernel,
-        (incoming,) + outside((output_map, base, gain)),
+        (incoming, output_map, base) + outside((gain,)),
         [((tokens, width), f32), ((1, tokens), f32)],
         [
-            pltpu.VMEM((tokens, N), bf16),
-            pltpu.VMEM((tokens, width), f32),
             pltpu.VMEM((tokens, width), f32),
             pltpu.VMEM((tokens, P_SIZE), f32),
-            pltpu.SemaphoreType.DMA((2, heads // 2 + 1)),
-        ],
-        specs=[VMEM, HBM, HBM, HBM],
+            pltpu.SemaphoreType.DMA((heads // 2,)),
+        ],
+        specs=[VMEM] * 3 + [HBM],
     )
     chip_energy = energy + swap(energy, "mp")
     other_energy = swap(chip_energy, "section")

time: 92.4 us -> 92.9 us (level)
  blocking collectives: 23.6 us -> 20.3 us
  waiting for transfers between devices: 17.8 us -> 20.2 us
  starting transfers between devices: 21.9 us -> 23.5 us
    all_to_all x1, blocking collectives: 23.6 us -> 20.3 us  [body(): lax.all_to_all(sent, 'ctx', 0, 0, axis_index_groups=groups, tiled=True)]
    all_to_all x1, waiting for transfers between devices: 2.76 us -> 5.15 us  [body(): got = lax.all_to_all(pay, 'ctx', 0, 0, axis_index_groups=groups, tiled=True)]
    all_to_all x1, starting transfers between devices: 4.88 us -> 6.37 us  [body(): got = lax.all_to_all(pay, 'ctx', 0, 0, axis_index_groups=groups, tiled=True)]
where the time goes in v4:
time: 92.9 us; the launch traced here: 92.7 us
  Pallas kernels  28.5 us (31%)
  starting transfers between devices  23.5 us (25%)
  blocking collectives  20.3 us (22%)
  waiting for transfers between devices  20.2 us (22%)
    pallas_call x8, Pallas kernels, call(): pl.pallas_call(kernel, out_shape=[pltpu.HBM(*out[:2]) if out[2:] else jax...  28.5 us
    all_to_all x1, blocking collectives, body(): lax.all_to_all(sent, 'ctx', 0, 0, axis_index_groups=groups, tiled=True)  20.3 us
    ppermute x4, starting transfers between devices, swap(): return lax.ppermute(value, axis, [(0, 1), (1, 0)])  9.79 us
    all_to_all x1, waiting for transfers between devices, body(): lax.all_to_all(total, 'ctx', 0, 0, axis_index_groups=peers, tiled=True)  8.12 us
    all_to_all x1, starting transfers between devices, body(): lax.all_to_all(total, 'ctx', 0, 0, axis_index_groups=peers, tiled=True)  7.34 us
    ppermute x4, waiting for transfers between devices, swap(): return lax.ppermute(value, axis, [(0, 1), (1, 0)])  6.93 us
    all_to_all x1, starting transfers between devices, body(): got = lax.all_to_all(pay, 'ctx', 0, 0, axis_index_groups=groups, tiled=True)  6.37 us
    all_to_all x1, waiting for transfers between devices, body(): got = lax.all_to_all(pay, 'ctx', 0, 0, axis_index_groups=groups, tiled=True)  5.15 us
  transfers between devices with their start and end apart: 6, of which 6 were waited for; matrix products, arithmetic and copies ran while one was open for 0% of the time, Pallas kernels for 13%

profile of v4, /device:TPU:1, one launch (start us, length us, event | category | flops | bytes accessed | tf_op | source)
XLA Modules:
  0.0 92.7 jit_solution(11677375722222556637)
XLA Ops:
  0.0 3.8 %shard_map.118 = (f32[256,128]{1,0:T(8,128)S(1)}, f32[16,512]{1,0:T(8,128)S(1)}, bf16[512,128]{1,0:T(8,128)(2,1)S(1)}, bf16[64,2048]{1,0:T(8,128)(2,1)S(1)}, bf1...) custom-call(f32[41,1,256]{2,1,0:T(1,128)} %bitcast.10, s32[41,1,256]{2,1,0:T(1,128)} %bitcast.11, ...), custom_call_target="tpu_custom_call" | custom-call | tf_op jit(solution)/shard_map/pallas_call | solution.py:328
  3.8 3.3 %collective-permute-start = (f32[256,128]{1,0:T(8,128)S(1)}, f32[256,128]{1,0:T(8,128)S(1)}, u32[]{:S(2)}, u32[]{:S(2)}) collective-permute-start(f32[256,128]{1,0:T(8,128)S(1)} %get-tuple-element.26), channel_id=1, source_target_pairs={{0,1},{1,0},{2,3},{3,2},{4,5},{5,4},{6,7},{7,6},{8,9},{9,8},{10,11... | collective-permute-start | bytes 393224 | tf_op jit(solution)/shard_map/ppermute | solution.py:341
  7.2 1.0 %collective-permute-done = f32[256,128]{1,0:T(8,128)S(1)} collective-permute-done((f32[256,128]{1,0:T(8,128)S(1)}, f32[256,128]{1,0:T(8,128)S(1)}, u32[]{:S(2)}, u32[]{:S(2)}) %collective-permute-start) | collective-permute-done | bytes 131104 | tf_op jit(solution)/shard_map/ppermute | solution.py:341
  8.2 0.1 collective-permute-start.1
  8.3 1.6 %shard_map.119 = (bf16[2,16,128,256]{3,2,1,0:T(8,128)(2,1)S(1)}, f32[2,16,128]{2,1,0:T(8,128)S(1)}, bf16[512,144]{1,0:T(8,128)(2,1)}, f32[16,512]{1,0:T(8,128)}) custom-call(f32[16,512]{1,0:T(8,128)S(1)} %get-tuple-element.29.forget_ref, bf16[512,128]{1,0:T(8,128)(2,1)S(1)} %get-tuple-element.30.in_ref), custom_call_target="tpu_custom_call" | custom-call | tf_op jit(solution)/shard_map/pallas_call | solution.py:328
  9.9 3.1 %collective-permute-done.1.other_ref = f32[256,128]{1,0:T(8,128)S(1)} collective-permute-done((f32[256,128]{1,0:T(8,128)S(1)}, f32[256,128]{1,0:T(8,128)S(1)}, u32[]{:S(2)}, u32[]{:S(2)}) %collective-permute-start.1) | collective-permute-done | bytes 131104 | tf_op jit(solution)/shard_map/ppermute | solution.py:341
  13.0 5.5 %shard_map.120 = (f32[16,136,128]{2,1,0:T(8,128)}, bf16[512,2048]{1,0:T(8,128)(2,1)}, f32[16,128,128]{2,1,0:T(8,128)}, bf16[512,192]{1,0:T(8,128)(2,1)}) custom-call(f32[256,128]{1,0:T(8,128)S(1)} %add.7.mine_ref, f32[256,128]{1,0:T(8,128)S(1)} %collective-permute-done.1.other_ref, bf16[64,2048]{1,0:T(8,128)(2,1)S(1)} %get-tuple-element.27.w_ref, ...), custom_call_target="tpu_custom_call" | custom-call | tf_op jit(solution)/shard_map/pallas_call | solution.py:328
  18.5 0.0 copy-start.2
  18.5 6.4 %all-to-all-start = ((f32[16,136,128]{2,1,0:T(8,128)}), f32[16,136,128]{2,1,0:T(8,128)S(1)}, u32[]{:S(2)}, u32[]{:S(2)}) async-start(f32[16,136,128]{2,1,0:T(8,128)} %get-tuple-element.33), calls=%async_computation | async-start | bytes 2228224 | tf_op jit(solution)/shard_map/all_to_all | solution.py:420
  24.9 0.0 copy-done.2
  24.9 10.5 %shard_map.121 = (f32[512,2048]{1,0:T(8,128)}, f32[512,2048]{1,0:T(8,128)}) custom-call(f32[1,16]{1,0:T(1,128)S(1)} %bitcast.9, bf16[512,128]{1,0:T(8,128)(2,1)} %refs_0_.1, bf16[512,128]{1,0:T(8,128)(2,1)} %read_ref.1, s32[1,512]{1,0:T(1,128)} %bitcast.15, f32[16,512]{1,0:T(8,128)} %get-tuple-element.34.refs_3_, ...), custom_call_target="tpu_custom_call" | custom-call | tf_op jit(solution)/shard_map/pallas_call | solution.py:328
  35.4 5.2 %all-to-all-done.got_ref = f32[16,136,128]{2,1,0:T(8,128)S(1)} async-done(((f32[16,136,128]{2,1,0:T(8,128)}), f32[16,136,128]{2,1,0:T(8,128)S(1)}, u32[]{:S(2)}, u32[]{:S(2)}) %all-to-all-start) | async-done | bytes 1114144 | tf_op jit(solution)/shard_map/all_to_all | solution.py:420
  40.5 0.8 shard_map.122
  41.3 7.3 %all-to-all-start.1 = ((f32[4,136,128]{2,1,0:T(8,128)}), f32[4,136,128]{2,1,0:T(8,128)S(1)}, u32[]{:S(2)}, u32[]{:S(2)}) async-start(f32[4,136,128]{2,1,0:T(8,128)} %shard_map.122), calls=%async_computation.1 | async-start | bytes 557056 | tf_op jit(solution)/shard_map/all_to_all | solution.py:441
  48.7 8.1 %all-to-all-done.1.totals_ref = f32[4,136,128]{2,1,0:T(8,128)S(1)} async-done(((f32[4,136,128]{2,1,0:T(8,128)}), f32[4,136,128]{2,1,0:T(8,128)S(1)}, u32[]{:S(2)}, u32[]{:S(2)}) %all-to-all-start.1) | async-done | bytes 278560 | tf_op jit(solution)/shard_map/all_to_all | solution.py:441
  56.8 0.1 shard_map.123
  56.9 20.3 %all_to_all.15.state_ref = f32[16,128,128]{2,1,0:T(8,128)S(1)} all-to-all(f32[16,128,128]{2,1,0:T(8,128)S(1)} %shard_map.123), channel_id=1, replica_groups={{0,2,4,6,8,10,12,14,16,18,20,22,24,26,28,30},{32,34,36,38,40,42,44,46,4..., dimensions={0} | all-to-all | bytes 2097152 | tf_op jit(solution)/shard_map/all_to_all | solution.py:443
  77.2 0.0 copy-done.1
  77.2 4.0 %shard_map.124 = (f32[512,2048]{1,0:T(8,128)S(1)}, f32[1,512]{1,0:T(1,128)S(1)}) custom-call(f32[16,128,128]{2,1,0:T(8,128)S(1)} %all_to_all.15.state_ref, bf16[512,128]{1,0:T(8,128)(2,1)S(1)} %copy-done.1, f32[512,2048]{1,0:T(8,128)S(1)} %copy-done, f32[512,2048]{1,0:T(8,128)} %get-tuple-element.43.gain_far), custom_call_target="tpu_custom_call" | custom-call | tf_op jit(solution)/shard_map/pallas_call | solution.py:328
  81.2 6.0 %collective-permute-start.2 = (f32[1,512]{1,0:T(1,128)S(1)}, f32[1,512]{1,0:T(1,128)S(1)}, u32[]{:S(2)}, u32[]{:S(2)}) collective-permute-start(f32[1,512]{1,0:T(1,128)S(1)} %get-tuple-element.45), channel_id=1, source_target_pairs={{0,1},{1,0},{2,3},{3,2},{4,5},{5,4},{6,7},{7,6},{8,9},{9,8},{10,11... | collective-permute-start | bytes 6152 | tf_op jit(solution)/shard_map/ppermute | solution.py:341
  87.1 0.8 collective-permute-done.2
  88.0 0.4 collective-permute-start.3
  88.4 2.0 %collective-permute-done.3.other_ref = f32[1,512]{1,0:T(1,128)S(1)} collective-permute-done((f32[1,512]{1,0:T(1,128)S(1)}, f32[1,512]{1,0:T(1,128)S(1)}, u32[]{:S(2)}, u32[]{:S(2)}) %collective-permute-start.3) | collective-permute-done | bytes 2080 | tf_op jit(solution)/shard_map/ppermute | solution.py:341
  90.4 2.2 %shard_map.125 = bf16[512,2048]{1,0:T(8,128)(2,1)} custom-call(f32[512,2048]{1,0:T(8,128)S(1)} %get-tuple-element.44.gated_ref, f32[1,512]{1,0:T(1,128)S(1)} %add.8.mine_ref, f32[1,512]{1,0:T(1,128)S(1)} %collective-permute-done.3.other_ref, f32[1,2048]{1,0:T(1,128)S(1)} %get-tuple-element.46.gain_ref), custom_call_target="tpu_custom_call" | custom-call | tf_op jit(solution)/shard_map/pallas_call | solution.py:328
  (6 shorter events, 0.0 us)
Async XLA Ops:
  3.8 4.3 %collective-permute-start = (f32[256,128]{1,0:T(8,128)S(1)}, f32[256,128]{1,0:T(8,128)S(1)}, u32[]{:S(2)}, u32[]{:S(2)}) collective-permute-start(f32[256,128]{1,0:T(8,128)S(1)} %get-tuple-element.26), channel_id=1, source_target_pairs={{0,1},{1,0},{2,3},{3,2},{4,5},{5,4},{6,7},{7,6},{8,9},{9,8},{10,11... | collective-permute-start | bytes 393224 | tf_op jit(solution)/shard_map/ppermute | solution.py:341
  8.2 4.8 %collective-permute-start.1 = (f32[256,128]{1,0:T(8,128)S(1)}, f32[256,128]{1,0:T(8,128)S(1)}, u32[]{:S(2)}, u32[]{:S(2)}) collective-permute-start(f32[256,128]{1,0:T(8,128)S(1)} %add.7.mine_ref), channel_id=1, source_target_pairs={{0,128},{128,0},{1,129},{129,1},{2,130},{130,2},{3,131},{131,3},{4... | collective-permute-start | bytes 393224 | tf_op jit(solution)/shard_map/ppermute | solution.py:341
  18.5 6.4 %copy-start.2 = (f32[16]{0:T(128)S(1)}, f32[16]{0:T(128)}, u32[]{:S(2)}) copy-start(f32[16]{0:T(128)} %param.21) | copy-start | bytes 196
  18.5 22.0 %all-to-all-start = ((f32[16,136,128]{2,1,0:T(8,128)}), f32[16,136,128]{2,1,0:T(8,128)S(1)}, u32[]{:S(2)}, u32[]{:S(2)}) async-start(f32[16,136,128]{2,1,0:T(8,128)} %get-tuple-element.33), calls=%async_computation | async-start | bytes 2228224 | tf_op jit(solution)/shard_map/all_to_all | solution.py:420
  41.3 15.5 %all-to-all-start.1 = ((f32[4,136,128]{2,1,0:T(8,128)}), f32[4,136,128]{2,1,0:T(8,128)S(1)}, u32[]{:S(2)}, u32[]{:S(2)}) async-start(f32[4,136,128]{2,1,0:T(8,128)} %shard_map.122), calls=%async_computation.1 | async-start | bytes 557056 | tf_op jit(solution)/shard_map/all_to_all | solution.py:441
  56.8 20.4 %copy-start = (f32[512,2048]{1,0:T(8,128)S(1)}, f32[512,2048]{1,0:T(8,128)}, u32[]{:S(2)}) copy-start(f32[512,2048]{1,0:T(8,128)} %get-tuple-element.42.base_ref) | copy-start | bytes 12582916
  56.8 20.4 %copy-start.1 = (bf16[512,128]{1,0:T(8,128)(2,1)S(1)}, bf16[512,128]{1,0:T(8,128)(2,1)}, u32[]{:S(2)}) copy-start(bf16[512,128]{1,0:T(8,128)(2,1)} %read_ref.1) | copy-start | bytes 393220
  81.2 6.8 %collective-permute-start.2 = (f32[1,512]{1,0:T(1,128)S(1)}, f32[1,512]{1,0:T(1,128)S(1)}, u32[]{:S(2)}, u32[]{:S(2)}) collective-permute-start(f32[1,512]{1,0:T(1,128)S(1)} %get-tuple-element.45), channel_id=1, source_target_pairs={{0,1},{1,0},{2,3},{3,2},{4,5},{5,4},{6,7},{7,6},{8,9},{9,8},{10,11... | collective-permute-start | bytes 6152 | tf_op jit(solution)/shard_map/ppermute | solution.py:341
  88.0 2.4 %collective-permute-start.3 = (f32[1,512]{1,0:T(1,128)S(1)}, f32[1,512]{1,0:T(1,128)S(1)}, u32[]{:S(2)}, u32[]{:S(2)}) collective-permute-start(f32[1,512]{1,0:T(1,128)S(1)} %add.8.mine_ref), channel_id=1, source_target_pairs={{0,128},{128,0},{1,129},{129,1},{2,130},{130,2},{3,131},{131,3},{4... | collective-permute-start | bytes 6152 | tf_op jit(solution)/shard_map/ppermute | solution.py:341

commit v5 on v3

--- a/solution.py
+++ b/solution.py
@@ -88,7 +88,7 @@
 
 
 def decay_kernel(
-    forget_ref, in_ref, keys_ref, ends_ref, columns_out, rows_out, columns_ref, rows_ref, wide, turned, sems
+    forget_ref, in_ref, keys_ref, ends_ref, columns_out, rows_out, early_out, columns_ref, rows_ref, wide, turned, sems
 ):
     heads = forget_ref.shape[0]
     blocks = keys_ref.shape[0]
@@ -105,6 +105,9 @@
         write_t = in_ref[span, :].astype(f32).T
         for h in range(heads):
             keys_ref[b, h] = (write_t * rise[h : h + 1, :]).astype(bf16)
+        if b == 0:
+            early = pltpu.make_async_copy(keys_ref.at[0], early_out, sems.at[2])
+            early.start()
     rows_ref[...] = turned[:heads, :] * LOG2E
     wide[...] = turned[...].T
     before = jnp.zeros((1, heads), f32)
@@ -116,33 +119,33 @@
         before = before + cum[BLK - 1 :, :]
     for copy in fetch((columns_ref, rows_ref), (columns_out, rows_out), sems):
         copy.wait()
+    early.wait()
 
 
 def stream_kernel(
-    mine_ref, other_ref, w_ref, embed_ref, keys_ref, ends_ref, pay_ref, *refs
+    mine_ref, other_ref, w_ref, embed_ref, keys_ref, ends_ref, pay_ref, stream_out, pooled_out, stream_ref, pooled_ref, sems
 ):
-    stream_out, first_out, pooled_out, stream_ref, first_ref, pooled_ref, sems = refs
     packed = mine_ref[...] + other_ref[...]
     pooled = jnp.concatenate([packed[:, :CF], packed[:, CF:]], axis=0)
     pooled_ref[...] = jnp.concatenate(terms(pooled, 3), axis=1)
-    heads = first_ref.shape[0]
-    saved = pltpu.make_async_copy(pooled_ref, pooled_out, sems.at[0, heads // 2])
+    heads = pay_ref.shape[0]
+    saved = pltpu.make_async_copy(pooled_ref, pooled_out, sems.at[heads // 2])
     saved.start()
 
-    def results(q):
+    def result(q):
         lanes = pl.ds(pl.multiple_of(q * 256, 256), 256)
-        both = pl.ds(2 * q, 2)
-        return (
-            pltpu.make_async_copy(stream_ref.at[:, lanes], stream_out.at[:, lanes], sems.at[0, q]),
-            pltpu.make_async_copy(first_ref.at[both], first_out.at[both], sems.at[1, q]),
-        )
+        return pltpu.make_async_copy(stream_ref.at[:, lanes], stream_out.at[:, lanes], sems.at[q])
 
     def pair(q, carry):
         lanes = pl.ds(pl.multiple_of(q * 256, 256), 256)
         w = w_ref[:, lanes]
         visual = dot(pooled_ref[...], jnp.concatenate([w, w, w], axis=0))
-        stream = (embed_ref[:, lanes].astype(f32) + visual).astype(bf16)
-        stream_ref[:, lanes] = stream
+        stream_ref[:, lanes] = (embed_ref[:, lanes].astype(f32) + visual).astype(bf16)
+        result(q).start()
+        return carry
+
+    def states(q, carry):
+        stream = stream_ref[:, pl.ds(pl.multiple_of(q * 256, 256), 256)]
         for j in range(2):
             h = 2 * q + j
             part = stream[:, j * P_SIZE : (j + 1) * P_SIZE]
@@ -150,19 +153,16 @@
             late = dot(keys_ref[1, h], part[BLK:])
             end_early = ends_ref[0, pl.ds(h, 1), :]
             end_late = ends_ref[1, pl.ds(h, 1), :]
-            first_ref[h] = early
             pay_ref[h, :N, :] = jnp.exp(-end_late) * early + late
             pay_ref[h, N:, :] = jnp.broadcast_to(end_early + end_late, (EXTRA, P_SIZE))
-        for copy in results(q):
-            copy.start()
         return carry
 
     def finish(q, carry):
-        for copy in results(q):
-            copy.wait()
+        result(q).wait()
         return carry
 
     lax.fori_loop(0, heads // 2, pair, 0, unroll=2)
+    lax.fori_loop(0, heads // 2, states, 0, unroll=2)
     lax.fori_loop(0, heads // 2, finish, 0)
     saved.wait()
 
@@ -175,17 +175,16 @@
     return jnp.where(hit, 1.0, 0.0).astype(bf16)
 
 
-def side_by_side(ref, q):
-    parts = [jnp.concatenate(terms(ref[2 * q + j], 2), axis=0) for j in range(2)]
-    return jnp.concatenate(parts, axis=1)
+def side_by_side(states):
+    return jnp.concatenate([jnp.concatenate(terms(state, 2), axis=0) for state in states], axis=1)
 
 
 def within_kernel(skip_ref, *refs):
     far, (base_out, gain_out), near = refs[:9], refs[9:11], refs[11:20]
     base_ref, gain_ref, scored, in_sems, out_sems = refs[20:]
     copies = fetch(far, near, in_sems)
-    in_ref, read_ref, frames_ref, rows_ref, columns_ref, w_ref, pooled_ref, first_ref, stream_ref = near
-    heads = first_ref.shape[0]
+    in_ref, read_ref, frames_ref, rows_ref, columns_ref, w_ref, pooled_ref, keys_ref, stream_ref = near
+    heads = keys_ref.shape[0]
     row_order = lax.broadcasted_iota(jnp.int32, (BLK, BLK), 0)
     col_order = lax.broadcasted_iota(jnp.int32, (BLK, BLK), 1)
     causal = col_order <= row_order
@@ -235,7 +234,10 @@
                 part = stream[span, side]
                 mixed[b].append(dot(weights, part) + skip_ref[0, h] * part.astype(f32))
         own = dot(columns_ref[late_rows, 3 * heads : 6 * heads], chosen)
-        carried = own * dot(read_twice, side_by_side(first_ref, q))
+        first = [
+            dot(keys_ref[2 * q + j], stream[:BLK, j * P_SIZE : (j + 1) * P_SIZE]) for j in range(2)
+        ]
+        carried = own * dot(read_twice, side_by_side(first))
         base_ref[:BLK, lanes] = jnp.concatenate(mixed[0], axis=1) * silu[:BLK]
         base_ref[BLK:, lanes] = (jnp.concatenate(mixed[1], axis=1) + carried) * silu[BLK:]
         for copy in results(q):
@@ -296,7 +298,7 @@
 
     def pair(q, carry):
         lanes = pl.ds(pl.multiple_of(q * 2 * P_SIZE, 2 * P_SIZE), 2 * P_SIZE)
-        carried = dot(read_twice, side_by_side(state_ref, q))
+        carried = dot(read_twice, side_by_side([state_ref[2 * q], state_ref[2 * q + 1]]))
         for copy in operands(q):
             copy.wait()
         gated = base_ref[:, lanes] + gain_ref[:, lanes] * carried
@@ -388,10 +390,11 @@
         ],
         specs=[HBM] * len(near + far),
     )
+    partial_sum, place = lax.optimization_barrier((partial_sum, place))
     chip_sum = partial_sum + swap(partial_sum, "mp")
     other_sum = swap(chip_sum, "section")
 
-    keys, ends, columns, row_sums = call(
+    keys, ends, columns, row_sums, early_keys = call(
         decay_kernel,
         (forget_t, writes),
         [
@@ -399,36 +402,35 @@
             ((blocks, heads, 128), f32),
             ((tokens, 9 * heads), bf16, True),
             ((heads, tokens), f32, True),
+            ((heads, N, BLK), bf16, True),
         ],
         [
             pltpu.VMEM((tokens, 9 * heads), bf16),
             pltpu.VMEM((heads, tokens), f32),
             pltpu.VMEM((tokens, 128), f32),
             pltpu.VMEM((128, tokens), f32),
-            pltpu.SemaphoreType.DMA((2,)),
-        ],
-    )
-
-    pay, stream, first, pooled = call(
+            pltpu.SemaphoreType.DMA((3,)),
+        ],
+    )
+
+    pay, stream, pooled = call(
         stream_kernel,
         (chip_sum, other_sum, w_visual, embed, keys, ends),
         [
             ((heads, N + EXTRA, P_SIZE), f32),
             ((tokens, width), bf16, True),
-            ((heads, N, P_SIZE), f32, True),
             ((tokens, 3 * CF), bf16, True),
         ],
         [
             pltpu.VMEM((tokens, width), bf16),
-            pltpu.VMEM((heads, N, P_SIZE), f32),
             pltpu.VMEM((tokens, 3 * CF), bf16),
-            pltpu.SemaphoreType.DMA((2, heads // 2 + 1)),
+            pltpu.SemaphoreType.DMA((heads // 2 + 1,)),
         ],
     )
     got = lax.all_to_all(pay, "ctx", 0, 0, axis_index_groups=groups, tiled=True)
 
     held = (input_map, output_map, frame_ids.reshape(1, tokens), row_sums, columns)
-    held += (w_gate, pooled, first, stream)
+    held += (w_gate, pooled, early_keys, stream)
     base, gain = call(
         within_kernel,
         (skip.reshape(1, heads),) + outside(held),

time: 92.4 us -> 90 us (0.974)
  blocking collectives: 23.6 us -> 39.1 us
  waiting for transfers between devices: 17.8 us -> 8.31 us
  starting transfers between devices: 21.9 us -> 14 us
    all_to_all x0 -> x1, blocking collectives: none -> 15.5 us  [body(): lax.all_to_all(total, 'ctx', 0, 0, axis_index_groups=peers, tiled=True)]
    all_to_all x1 -> x0, waiting for transfers between devices: 8.13 us -> none  [body(): lax.all_to_all(total, 'ctx', 0, 0, axis_index_groups=peers, tiled=True)]
    all_to_all x1 -> x0, starting transfers between devices: 7.3 us -> none  [body(): lax.all_to_all(total, 'ctx', 0, 0, axis_index_groups=peers, tiled=True)]
    all_to_all x1, waiting for transfers between devices: 2.76 us -> 1.45 us  [body(): lax.all_to_all(sent, 'ctx', 0, 0, axis_index_groups=groups, tiled=True)]
  transfers between devices with their start and end apart: 6 -> 5, of which waited for: 6 -> 5; matrix products, arithmetic and copies ran while one was open for 0% -> 0% of each run, Pallas kernels for 13% -> 15%
where the time goes in v5:
time: 90 us; the launch traced here: 89.8 us
  blocking collectives  39.1 us (43%)
  Pallas kernels  28.3 us (31%)
  starting transfers between devices  14 us (16%)
  waiting for transfers between devices  8.31 us (9%)
    pallas_call x8, Pallas kernels, call(): pl.pallas_call(kernel, out_shape=[pltpu.HBM(*out[:2]) if out[2:] else jax...  28.3 us
    all_to_all x1, blocking collectives, body(): got = lax.all_to_all(pay, 'ctx', 0, 0, axis_index_groups=groups, tiled=True)  23.6 us
    all_to_all x1, blocking collectives, body(): lax.all_to_all(total, 'ctx', 0, 0, axis_index_groups=peers, tiled=True)  15.5 us
    ppermute x4, starting transfers between devices, swap(): return lax.ppermute(value, axis, [(0, 1), (1, 0)])  9.44 us
    ppermute x4, waiting for transfers between devices, swap(): return lax.ppermute(value, axis, [(0, 1), (1, 0)])  6.86 us
    all_to_all x1, starting transfers between devices, body(): lax.all_to_all(sent, 'ctx', 0, 0, axis_index_groups=groups, tiled=True)  4.55 us
  transfers between devices with their start and end apart: 5, of which 5 were waited for; matrix products, arithmetic and copies ran while one was open for 0% of the time, Pallas kernels for 15%

profile of v5, /device:TPU:1, one launch (start us, length us, event | category | flops | bytes accessed | tf_op | source)
XLA Modules:
  0.0 89.8 jit_solution(3729554878794054032)
XLA Ops:
  0.0 3.8 %shard_map.118 = (f32[256,128]{1,0:T(8,128)S(1)}, f32[16,512]{1,0:T(8,128)S(1)}, bf16[512,128]{1,0:T(8,128)(2,1)S(1)}, bf16[64,2048]{1,0:T(8,128)(2,1)S(1)}, bf1...) custom-call(f32[41,1,256]{2,1,0:T(1,128)} %bitcast.10, s32[41,1,256]{2,1,0:T(1,128)} %bitcast.11, ...), custom_call_target="tpu_custom_call" | custom-call | tf_op jit(solution)/shard_map/pallas_call | solution.py:338
  3.8 3.3 %collective-permute-start = (f32[256,128]{1,0:T(8,128)S(1)}, f32[256,128]{1,0:T(8,128)S(1)}, u32[]{:S(2)}, u32[]{:S(2)}) collective-permute-start(f32[256,128]{1,0:T(8,128)S(1)} %get-tuple-element.26), channel_id=1, source_target_pairs={{0,1},{1,0},{2,3},{3,2},{4,5},{5,4},{6,7},{7,6},{8,9},{9,8},{10,11... | collective-permute-start | bytes 393224 | tf_op jit(solution)/shard_map/ppermute | solution.py:351
  7.2 1.0 %collective-permute-done = f32[256,128]{1,0:T(8,128)S(1)} collective-permute-done((f32[256,128]{1,0:T(8,128)S(1)}, f32[256,128]{1,0:T(8,128)S(1)}, u32[]{:S(2)}, u32[]{:S(2)}) %collective-permute-start) | collective-permute-done | bytes 131104 | tf_op jit(solution)/shard_map/ppermute | solution.py:351
  8.2 0.1 collective-permute-start.1
  8.3 1.7 %shard_map.119 = (bf16[2,16,128,256]{3,2,1,0:T(8,128)(2,1)S(1)}, f32[2,16,128]{2,1,0:T(8,128)S(1)}, bf16[512,144]{1,0:T(8,128)(2,1)}, f32[16,512]{1,0:T(8,128)}, bf16[16,128,256]{2,1,0:T(8,128)(2,1)}) custom-call(f32[16,512]{1,0:T(8,128)S(1)} %get-tuple-element.29.forget_ref, bf16[512,128]{1,0:T(8,128)(2,1)S(1)} %get-tuple-element.30.in_ref), custom_call_target="tpu_custom_call" | custom-call | tf_op jit(solution)/shard_map/pallas_call | solution.py:338
  10.0 3.0 %collective-permute-done.1.other_ref = f32[256,128]{1,0:T(8,128)S(1)} collective-permute-done((f32[256,128]{1,0:T(8,128)S(1)}, f32[256,128]{1,0:T(8,128)S(1)}, u32[]{:S(2)}, u32[]{:S(2)}) %collective-permute-start.1) | collective-permute-done | bytes 131104 | tf_op jit(solution)/shard_map/ppermute | solution.py:351
  13.0 3.0 %shard_map.120 = (f32[16,136,128]{2,1,0:T(8,128)S(1)}, bf16[512,2048]{1,0:T(8,128)(2,1)}, bf16[512,192]{1,0:T(8,128)(2,1)}) custom-call(f32[256,128]{1,0:T(8,128)S(1)} %add.7.mine_ref, f32[256,128]{1,0:T(8,128)S(1)} %collective-permute-done.1.other_ref, bf16[64,2048]{1,0:T(8,128)(2,1)S(1)} %get-tuple-element.27.w_ref, ...), custom_call_target="tpu_custom_call" | custom-call | tf_op jit(solution)/shard_map/pallas_call | solution.py:338
  16.0 23.6 %all_to_all.15.got_ref = f32[16,136,128]{2,1,0:T(8,128)S(1)} all-to-all(f32[16,136,128]{2,1,0:T(8,128)S(1)} %get-tuple-element.33), channel_id=1, replica_groups={{0,2,4,6,8,10,12,14,16,18,20,22,24,26,28,30},{32,34,36,38,40,42,44,46,4..., dimensions={0} | all-to-all | bytes 2228224 | tf_op jit(solution)/shard_map/all_to_all | solution.py:430
  39.6 0.1 shard_map.121
  39.7 15.5 %all_to_all.16.totals_ref = f32[4,136,128]{2,1,0:T(8,128)S(1)} all-to-all(f32[4,136,128]{2,1,0:T(8,128)S(1)} %shard_map.121), channel_id=1, replica_groups={{0,32,64,96},{2,34,66,98},{4,36,68,100},{6,38,70,102},{8,40,72,104},{10..., dimensions={0} | all-to-all | bytes 557056 | tf_op jit(solution)/shard_map/all_to_all | solution.py:450
  55.1 0.0 copy-start
  55.1 1.1 %shard_map.122 = f32[16,128,128]{2,1,0:T(8,128)} custom-call(f32[16,136,128]{2,1,0:T(8,128)S(1)} %all_to_all.15.got_ref, f32[4,136,128]{2,1,0:T(8,128)S(1)} %all_to_all.16.totals_ref, s32[1,128]{1,0:T(1,128)S(1)} %broadcast_in_dim.3.place_ref), custom_call_target="tpu_custom_call" | custom-call | tf_op jit(solution)/shard_map/pallas_call | solution.py:338
  56.2 4.5 %all-to-all-start.2 = ((f32[16,128,128]{2,1,0:T(8,128)}), f32[16,128,128]{2,1,0:T(8,128)S(1)}, u32[]{:S(2)}, u32[]{:S(2)}) async-start(f32[16,128,128]{2,1,0:T(8,128)} %shard_map.122), calls=%async_computation.2 | async-start | bytes 2097152 | tf_op jit(solution)/shard_map/all_to_all | solution.py:452
  60.8 0.0 copy-done
  60.8 12.2 %shard_map.123 = (f32[512,2048]{1,0:T(8,128)}, f32[512,2048]{1,0:T(8,128)}) custom-call(f32[1,16]{1,0:T(1,128)S(1)} %bitcast.9, bf16[512,128]{1,0:T(8,128)(2,1)} %refs_0_.1, bf16[512,128]{1,0:T(8,128)(2,1)} %read_far.1, s32[1,512]{1,0:T(1,128)} %bitcast.15, f32[16,512]{1,0:T(8,128)} %get-tuple-element.35.refs_3_, ...), custom_call_target="tpu_custom_call" | custom-call | tf_op jit(solution)/shard_map/pallas_call | solution.py:338
  73.0 1.4 %all-to-all-done.2.state_ref = f32[16,128,128]{2,1,0:T(8,128)S(1)} async-done(((f32[16,128,128]{2,1,0:T(8,128)}), f32[16,128,128]{2,1,0:T(8,128)S(1)}, u32[]{:S(2)}, u32[]{:S(2)}) %all-to-all-start.2) | async-done | bytes 1048608 | tf_op jit(solution)/shard_map/all_to_all | solution.py:452
  74.4 4.2 %shard_map.124 = (f32[512,2048]{1,0:T(8,128)S(1)}, f32[1,512]{1,0:T(1,128)S(1)}) custom-call(f32[16,128,128]{2,1,0:T(8,128)S(1)} %all-to-all-done.2.state_ref, bf16[512,128]{1,0:T(8,128)(2,1)} %read_far.1, f32[512,2048]{1,0:T(8,128)} %get-tuple-element.40.base_far, f32[512,2048]{1,0:T(8,128)} %get-tuple-element.41.gain_far), custom_call_target="tpu_custom_call" | custom-call | tf_op jit(solution)/shard_map/pallas_call | solution.py:338
  78.6 5.6 %collective-permute-start.2 = (f32[1,512]{1,0:T(1,128)S(1)}, f32[1,512]{1,0:T(1,128)S(1)}, u32[]{:S(2)}, u32[]{:S(2)}) collective-permute-start(f32[1,512]{1,0:T(1,128)S(1)} %get-tuple-element.43), channel_id=1, source_target_pairs={{0,1},{1,0},{2,3},{3,2},{4,5},{5,4},{6,7},{7,6},{8,9},{9,8},{10,11... | collective-permute-start | bytes 6152 | tf_op jit(solution)/shard_map/ppermute | solution.py:351
  84.2 0.8 collective-permute-done.2
  85.1 0.4 collective-permute-start.3
  85.4 2.1 %collective-permute-done.3.other_ref = f32[1,512]{1,0:T(1,128)S(1)} collective-permute-done((f32[1,512]{1,0:T(1,128)S(1)}, f32[1,512]{1,0:T(1,128)S(1)}, u32[]{:S(2)}, u32[]{:S(2)}) %collective-permute-start.3) | collective-permute-done | bytes 2080 | tf_op jit(solution)/shard_map/ppermute | solution.py:351
  87.5 2.2 %shard_map.125 = bf16[512,2048]{1,0:T(8,128)(2,1)} custom-call(f32[512,2048]{1,0:T(8,128)S(1)} %get-tuple-element.42.gated_ref, f32[1,512]{1,0:T(1,128)S(1)} %add.8.mine_ref, f32[1,512]{1,0:T(1,128)S(1)} %collective-permute-done.3.other_ref, f32[1,2048]{1,0:T(1,128)S(1)} %get-tuple-element.44.gain_ref), custom_call_target="tpu_custom_call" | custom-call | tf_op jit(solution)/shard_map/pallas_call | solution.py:338
  (3 shorter events, 0.0 us)
Async XLA Ops:
  3.8 4.3 %collective-permute-start = (f32[256,128]{1,0:T(8,128)S(1)}, f32[256,128]{1,0:T(8,128)S(1)}, u32[]{:S(2)}, u32[]{:S(2)}) collective-permute-start(f32[256,128]{1,0:T(8,128)S(1)} %get-tuple-element.26), channel_id=1, source_target_pairs={{0,1},{1,0},{2,3},{3,2},{4,5},{5,4},{6,7},{7,6},{8,9},{9,8},{10,11... | collective-permute-start | bytes 393224 | tf_op jit(solution)/shard_map/ppermute | solution.py:351
  8.2 4.8 %collective-permute-start.1 = (f32[256,128]{1,0:T(8,128)S(1)}, f32[256,128]{1,0:T(8,128)S(1)}, u32[]{:S(2)}, u32[]{:S(2)}) collective-permute-start(f32[256,128]{1,0:T(8,128)S(1)} %add.7.mine_ref), channel_id=1, source_target_pairs={{0,128},{128,0},{1,129},{129,1},{2,130},{130,2},{3,131},{131,3},{4... | collective-permute-start | bytes 393224 | tf_op jit(solution)/shard_map/ppermute | solution.py:351
  55.1 5.6 %copy-start = (f32[16]{0:T(128)S(1)}, f32[16]{0:T(128)}, u32[]{:S(2)}) copy-start(f32[16]{0:T(128)} %param.21) | copy-start | bytes 196
  56.2 18.2 %all-to-all-start.2 = ((f32[16,128,128]{2,1,0:T(8,128)}), f32[16,128,128]{2,1,0:T(8,128)S(1)}, u32[]{:S(2)}, u32[]{:S(2)}) async-start(f32[16,128,128]{2,1,0:T(8,128)} %shard_map.122), calls=%async_computation.2 | async-start | bytes 2097152 | tf_op jit(solution)/shard_map/all_to_all | solution.py:452
  78.6 6.5 %collective-permute-start.2 = (f32[1,512]{1,0:T(1,128)S(1)}, f32[1,512]{1,0:T(1,128)S(1)}, u32[]{:S(2)}, u32[]{:S(2)}) collective-permute-start(f32[1,512]{1,0:T(1,128)S(1)} %get-tuple-element.43), channel_id=1, source_target_pairs={{0,1},{1,0},{2,3},{3,2},{4,5},{5,4},{6,7},{7,6},{8,9},{9,8},{10,11... | collective-permute-start | bytes 6152 | tf_op jit(solution)/shard_map/ppermute | solution.py:351
  85.1 2.4 %collective-permute-start.3 = (f32[1,512]{1,0:T(1,128)S(1)}, f32[1,512]{1,0:T(1,128)S(1)}, u32[]{:S(2)}, u32[]{:S(2)}) collective-permute-start(f32[1,512]{1,0:T(1,128)S(1)} %add.8.mine_ref), channel_id=1, source_target_pairs={{0,128},{128,0},{1,129},{129,1},{2,130},{130,2},{3,131},{131,3},{4... | collective-permute-start | bytes 6152 | tf_op jit(solution)/shard_map/ppermute | solution.py:351

commit v6 on v5

--- a/solution.py
+++ b/solution.py
@@ -180,10 +180,10 @@
 
 
 def within_kernel(skip_ref, *refs):
-    far, (base_out, gain_out), near = refs[:9], refs[9:11], refs[11:20]
-    base_ref, gain_ref, scored, in_sems, out_sems = refs[20:]
+    far, base_out, near = refs[:7], refs[7], refs[8:15]
+    base_ref, scored, in_sems, out_sems = refs[15:]
     copies = fetch(far, near, in_sems)
-    in_ref, read_ref, frames_ref, rows_ref, columns_ref, w_ref, pooled_ref, keys_ref, stream_ref = near
+    in_ref, read_ref, frames_ref, rows_ref, columns_ref, keys_ref, stream_ref = near
     heads = keys_ref.shape[0]
     row_order = lax.broadcasted_iota(jnp.int32, (BLK, BLK), 0)
     col_order = lax.broadcasted_iota(jnp.int32, (BLK, BLK), 1)
@@ -203,22 +203,14 @@
         copy.wait()
     read = read_ref[BLK:, :]
     read_twice = jnp.concatenate([read, read], axis=1)
-    late_rows = slice(BLK, 2 * BLK)
-
-    def results(q):
+
+    def result(q):
         lanes = pl.ds(pl.multiple_of(q * 2 * P_SIZE, 2 * P_SIZE), 2 * P_SIZE)
-        return (
-            pltpu.make_async_copy(base_ref.at[:, lanes], base_out.at[:, lanes], out_sems.at[0, q]),
-            pltpu.make_async_copy(gain_ref.at[:, lanes], gain_out.at[:, lanes], out_sems.at[1, q]),
-        )
+        return pltpu.make_async_copy(base_ref.at[:, lanes], base_out.at[:, lanes], out_sems.at[q])
 
     def pair(q, carry):
         lanes = pl.ds(pl.multiple_of(q * 2 * P_SIZE, 2 * P_SIZE), 2 * P_SIZE)
-        w = w_ref[:, lanes]
-        gate = dot(pooled_ref[...], jnp.concatenate([w, w, w], axis=0))
-        silu = gate / (1.0 + jnp.exp(-gate))
         chosen = pick(heads, q)
-        gain_ref[:, lanes] = silu * dot(columns_ref[:, : 3 * heads], chosen)
         cum_col = dot(columns_ref[:, 6 * heads :], chosen)
         stream = stream_ref[:, lanes]
         mixed = [[], []]
@@ -233,23 +225,21 @@
                 weights = (scored[b] * jnp.exp2(-distance)).astype(bf16)
                 part = stream[span, side]
                 mixed[b].append(dot(weights, part) + skip_ref[0, h] * part.astype(f32))
-        own = dot(columns_ref[late_rows, 3 * heads : 6 * heads], chosen)
+        own = dot(columns_ref[BLK:, 3 * heads : 6 * heads], chosen)
         first = [
             dot(keys_ref[2 * q + j], stream[:BLK, j * P_SIZE : (j + 1) * P_SIZE]) for j in range(2)
         ]
         carried = own * dot(read_twice, side_by_side(first))
-        base_ref[:BLK, lanes] = jnp.concatenate(mixed[0], axis=1) * silu[:BLK]
-        base_ref[BLK:, lanes] = (jnp.concatenate(mixed[1], axis=1) + carried) * silu[BLK:]
-        for copy in results(q):
-            copy.start()
+        base_ref[:BLK, lanes] = jnp.concatenate(mixed[0], axis=1)
+        base_ref[BLK:, lanes] = jnp.concatenate(mixed[1], axis=1) + carried
+        result(q).start()
         return carry
 
     def finish(q, carry):
-        for copy in results(q):
-            copy.wait()
-        return carry
-
-    lax.fori_loop(0, heads // 2, pair, 0)
+        result(q).wait()
+        return carry
+
+    lax.fori_loop(0, heads // 2, pair, 0, unroll=2)
     lax.fori_loop(0, heads // 2, finish, 0)
 
 
@@ -276,38 +266,41 @@
         state = jnp.exp(-got_ref[i, N : N + 1, :]) * state + got_ref[i, :N, :]
 
 
-def carry_kernel(state_ref, read_far, base_far, gain_far, gated_ref, energy_ref, read_ref, base_ref, gain_ref, acc, sems):
+def carry_kernel(state_ref, *refs):
+    far, (gated_ref, energy_ref), near = refs[:5], refs[5:7], refs[7:12]
+    acc, sems = refs[12:]
+    read_ref, columns_ref, pooled_ref, w_ref, base_ref = near
     heads = state_ref.shape[0]
 
-    def operands(q):
+    def base(q):
         lanes = pl.ds(pl.multiple_of(q * 2 * P_SIZE, 2 * P_SIZE), 2 * P_SIZE)
-        return (
-            pltpu.make_async_copy(base_far.at[:, lanes], base_ref.at[:, lanes], sems.at[0, q]),
-            pltpu.make_async_copy(gain_far.at[:, lanes], gain_ref.at[:, lanes], sems.at[1, q]),
-        )
-
-    first = pltpu.make_async_copy(read_far, read_ref, sems.at[0, heads // 2])
-    first.start()
+        return pltpu.make_async_copy(far[4].at[:, lanes], base_ref.at[:, lanes], sems.at[q + 4])
+
+    copies = fetch(far[:4], near[:4], sems)
     for q in range(heads // 2):
-        for copy in operands(q):
-            copy.start()
+        base(q).start()
     acc[...] = jnp.zeros_like(acc)
-    first.wait()
+    for copy in copies:
+        copy.wait()
     read = read_ref[...]
     read_twice = jnp.concatenate([read, read], axis=1)
 
     def pair(q, carry):
         lanes = pl.ds(pl.multiple_of(q * 2 * P_SIZE, 2 * P_SIZE), 2 * P_SIZE)
+        w = w_ref[:, lanes]
+        gate = dot(pooled_ref[...], jnp.concatenate([w, w, w], axis=0))
+        half = 0.5 * gate
+        silu = half + half * jnp.tanh(half)
         carried = dot(read_twice, side_by_side([state_ref[2 * q], state_ref[2 * q + 1]]))
-        for copy in operands(q):
-            copy.wait()
-        gated = base_ref[:, lanes] + gain_ref[:, lanes] * carried
+        carried = dot(columns_ref[:, : 3 * heads], pick(heads, q)) * carried
+        base(q).wait()
+        gated = (base_ref[:, lanes] + carried) * silu
         gated_ref[:, lanes] = gated
         squares = gated * gated
         acc[...] += squares[:, :P_SIZE] + squares[:, P_SIZE:]
         return carry
 
-    lax.fori_loop(0, heads // 2, pair, 0)
+    lax.fori_loop(0, heads // 2, pair, 0, unroll=2)
     energy_ref[...] = jnp.sum(acc[...].T, axis=0, keepdims=True)
 
 
@@ -323,7 +316,7 @@
             held[rows, lanes] = (gated_ref[rows, lanes] * column * gain_ref[:, lanes]).astype(bf16)
             return carry
 
-        lax.fori_loop(0, held.shape[1] // P_SIZE, head, 0, unroll=4)
+        lax.fori_loop(0, held.shape[1] // P_SIZE, head, 0, unroll=8)
         copies.append(pltpu.make_async_copy(held.at[rows], out_ref.at[rows], sems.at[k]))
         copies[-1].start()
     for copy in copies:
@@ -430,18 +423,17 @@
     got = lax.all_to_all(pay, "ctx", 0, 0, axis_index_groups=groups, tiled=True)
 
     held = (input_map, output_map, frame_ids.reshape(1, tokens), row_sums, columns)
-    held += (w_gate, pooled, early_keys, stream)
-    base, gain = call(
+    held += (early_keys, stream)
+    (base,) = call(
         within_kernel,
         (skip.reshape(1, heads),) + outside(held),
-        [((tokens, width), f32, True), ((tokens, width), f32, True)],
+        [((tokens, width), f32, True)],
         [pltpu.VMEM(array.shape, array.dtype) for array in held]
         + [
             pltpu.VMEM((tokens, width), f32),
-            pltpu.VMEM((tokens, width), f32),
             pltpu.VMEM((blocks, BLK, BLK), f32),
             pltpu.SemaphoreType.DMA((len(held),)),
-            pltpu.SemaphoreType.DMA((2, heads // 2)),
+            pltpu.SemaphoreType.DMA((heads // 2,)),
         ],
         specs=[SMEM] + [HBM] * len(held),
     )
@@ -451,18 +443,14 @@
     (sent,) = call(spread_kernel, (got, totals, place), [((heads, N, P_SIZE), f32)])
     incoming = lax.all_to_all(sent, "ctx", 0, 0, axis_index_groups=groups, tiled=True)
 
+    held = (output_map, columns, pooled, w_gate, base)
     gated, energy = call(
         carry_kernel,
-        (incoming,) + outside((output_map, base, gain)),
+        (incoming,) + outside(held),
         [((tokens, width), f32), ((1, tokens), f32)],
-        [
-            pltpu.VMEM((tokens, N), bf16),
-            pltpu.VMEM((tokens, width), f32),
-            pltpu.VMEM((tokens, width), f32),
-            pltpu.VMEM((tokens, P_SIZE), f32),
-            pltpu.SemaphoreType.DMA((2, heads // 2 + 1)),
-        ],
-        specs=[VMEM, HBM, HBM, HBM],
+        [pltpu.VMEM(array.shape, array.dtype) for array in held]
+        + [pltpu.VMEM((tokens, P_SIZE), f32), pltpu.SemaphoreType.DMA((heads // 2 + 4,))],
+        specs=[VMEM] + [HBM] * len(held),
     )
     chip_energy = energy + swap(energy, "mp")
     other_energy = swap(chip_energy, "section")

time: 90 us -> 91.8 us (1.020)
  waiting for transfers between devices: 8.31 us -> 11.3 us
  Pallas kernels: 28.3 us -> 27 us
    all_to_all x1, waiting for transfers between devices: 1.45 us -> 4.46 us  [body(): lax.all_to_all(sent, 'ctx', 0, 0, axis_index_groups=groups, tiled=True)]
    pallas_call x8, Pallas kernels: 28.3 us -> 27 us  [call(): pl.pallas_call(kernel, out_shape=[pltpu.HBM(*out[:2]) if out[2:] else jax...]
  transfers between devices with their start and end apart: 5 -> 5, of which waited for: 5 -> 5; matrix products, arithmetic and copies ran while one was open for 0% -> 0% of each run, Pallas kernels for 15% -> 12%
where the time goes in v6:
time: 91.8 us; the launch traced here: 91.5 us
  blocking collectives  39.1 us (43%)
  Pallas kernels  27 us (29%)
  starting transfers between devices  14 us (15%)
  waiting for transfers between devices  11.3 us (12%)
    pallas_call x8, Pallas kernels, call(): pl.pallas_call(kernel, out_shape=[pltpu.HBM(*out[:2]) if out[2:] else jax...  27 us
    all_to_all x1, blocking collectives, body(): got = lax.all_to_all(pay, 'ctx', 0, 0, axis_index_groups=groups, tiled=True)  23.6 us
    all_to_all x1, blocking collectives, body(): lax.all_to_all(total, 'ctx', 0, 0, axis_index_groups=peers, tiled=True)  15.5 us
    ppermute x4, starting transfers between devices, swap(): return lax.ppermute(value, axis, [(0, 1), (1, 0)])  9.44 us
    ppermute x4, waiting for transfers between devices, swap(): return lax.ppermute(value, axis, [(0, 1), (1, 0)])  6.85 us
    all_to_all x1, starting transfers between devices, body(): lax.all_to_all(sent, 'ctx', 0, 0, axis_index_groups=groups, tiled=True)  4.55 us
    all_to_all x1, waiting for transfers between devices, body(): lax.all_to_all(sent, 'ctx', 0, 0, axis_index_groups=groups, tiled=True)  4.46 us
  transfers between devices with their start and end apart: 5, of which 5 were waited for; matrix products, arithmetic and copies ran while one was open for 0% of the time, Pallas kernels for 12%

profile of v6, /device:TPU:1, one launch (start us, length us, event | category | flops | bytes accessed | tf_op | source)
XLA Modules:
  0.0 91.5 jit_solution(11462060646643869892)
XLA Ops:
  0.0 3.8 %shard_map.118 = (f32[256,128]{1,0:T(8,128)S(1)}, f32[16,512]{1,0:T(8,128)S(1)}, bf16[512,128]{1,0:T(8,128)(2,1)S(1)}, bf16[64,2048]{1,0:T(8,128)(2,1)S(1)}, bf1...) custom-call(f32[41,1,256]{2,1,0:T(1,128)} %bitcast.10, s32[41,1,256]{2,1,0:T(1,128)} %bitcast.11, ...), custom_call_target="tpu_custom_call" | custom-call | tf_op jit(solution)/shard_map/pallas_call | solution.py:331
  3.8 3.3 %collective-permute-start = (f32[256,128]{1,0:T(8,128)S(1)}, f32[256,128]{1,0:T(8,128)S(1)}, u32[]{:S(2)}, u32[]{:S(2)}) collective-permute-start(f32[256,128]{1,0:T(8,128)S(1)} %get-tuple-element.24), channel_id=1, source_target_pairs={{0,1},{1,0},{2,3},{3,2},{4,5},{5,4},{6,7},{7,6},{8,9},{9,8},{10,11... | collective-permute-start | bytes 393224 | tf_op jit(solution)/shard_map/ppermute | solution.py:344
  7.2 1.0 %collective-permute-done = f32[256,128]{1,0:T(8,128)S(1)} collective-permute-done((f32[256,128]{1,0:T(8,128)S(1)}, f32[256,128]{1,0:T(8,128)S(1)}, u32[]{:S(2)}, u32[]{:S(2)}) %collective-permute-start) | collective-permute-done | bytes 131104 | tf_op jit(solution)/shard_map/ppermute | solution.py:344
  8.2 0.1 collective-permute-start.1
  8.3 1.7 %shard_map.119 = (bf16[2,16,128,256]{3,2,1,0:T(8,128)(2,1)S(1)}, f32[2,16,128]{2,1,0:T(8,128)S(1)}, bf16[512,144]{1,0:T(8,128)(2,1)}, f32[16,512]{1,0:T(8,128)}, bf16[16,128,256]{2,1,0:T(8,128)(2,1)}) custom-call(f32[16,512]{1,0:T(8,128)S(1)} %get-tuple-element.27.forget_ref, bf16[512,128]{1,0:T(8,128)(2,1)S(1)} %get-tuple-element.28.in_ref), custom_call_target="tpu_custom_call" | custom-call | tf_op jit(solution)/shard_map/pallas_call | solution.py:331
  10.0 3.0 %collective-permute-done.1.other_ref = f32[256,128]{1,0:T(8,128)S(1)} collective-permute-done((f32[256,128]{1,0:T(8,128)S(1)}, f32[256,128]{1,0:T(8,128)S(1)}, u32[]{:S(2)}, u32[]{:S(2)}) %collective-permute-start.1) | collective-permute-done | bytes 131104 | tf_op jit(solution)/shard_map/ppermute | solution.py:344
  13.0 3.0 %shard_map.120 = (f32[16,136,128]{2,1,0:T(8,128)S(1)}, bf16[512,2048]{1,0:T(8,128)(2,1)}, bf16[512,192]{1,0:T(8,128)(2,1)}) custom-call(f32[256,128]{1,0:T(8,128)S(1)} %add.7.mine_ref, f32[256,128]{1,0:T(8,128)S(1)} %collective-permute-done.1.other_ref, bf16[64,2048]{1,0:T(8,128)(2,1)S(1)} %get-tuple-element.25.w_ref, ...), custom_call_target="tpu_custom_call" | custom-call | tf_op jit(solution)/shard_map/pallas_call | solution.py:331
  16.0 23.6 %all_to_all.15.got_ref = f32[16,136,128]{2,1,0:T(8,128)S(1)} all-to-all(f32[16,136,128]{2,1,0:T(8,128)S(1)} %get-tuple-element.31), channel_id=1, replica_groups={{0,2,4,6,8,10,12,14,16,18,20,22,24,26,28,30},{32,34,36,38,40,42,44,46,4..., dimensions={0} | all-to-all | bytes 2228224 | tf_op jit(solution)/shard_map/all_to_all | solution.py:423
  39.6 0.1 shard_map.121
  39.7 15.5 %all_to_all.16.totals_ref = f32[4,136,128]{2,1,0:T(8,128)S(1)} all-to-all(f32[4,136,128]{2,1,0:T(8,128)S(1)} %shard_map.121), channel_id=1, replica_groups={{0,32,64,96},{2,34,66,98},{4,36,68,100},{6,38,70,102},{8,40,72,104},{10..., dimensions={0} | all-to-all | bytes 557056 | tf_op jit(solution)/shard_map/all_to_all | solution.py:442
  55.1 0.0 copy-start
  55.1 1.1 %shard_map.122 = f32[16,128,128]{2,1,0:T(8,128)} custom-call(f32[16,136,128]{2,1,0:T(8,128)S(1)} %all_to_all.15.got_ref, f32[4,136,128]{2,1,0:T(8,128)S(1)} %all_to_all.16.totals_ref, s32[1,128]{1,0:T(1,128)S(1)} %broadcast_in_dim.3.place_ref), custom_call_target="tpu_custom_call" | custom-call | tf_op jit(solution)/shard_map/pallas_call | solution.py:331
  56.3 4.5 %all-to-all-start.2 = ((f32[16,128,128]{2,1,0:T(8,128)}), f32[16,128,128]{2,1,0:T(8,128)S(1)}, u32[]{:S(2)}, u32[]{:S(2)}) async-start(f32[16,128,128]{2,1,0:T(8,128)} %shard_map.122), calls=%async_computation.2 | async-start | bytes 2097152 | tf_op jit(solution)/shard_map/all_to_all | solution.py:444
  60.8 0.0 copy-done
  60.8 9.2 %shard_map.123.refs_4_ = f32[512,2048]{1,0:T(8,128)} custom-call(f32[1,16]{1,0:T(1,128)S(1)} %bitcast.9, bf16[512,128]{1,0:T(8,128)(2,1)} %refs_0_.2, bf16[512,128]{1,0:T(8,128)(2,1)} %refs_0_.3, s32[1,512]{1,0:T(1,128)} %bitcast.15, f32[16,512]{1,0:T(8,128)} %get-tuple-element.35.refs_3_, bf16[512,144]{1,0:T(8,128)(2,1)} %get-tuple-element.33.refs_4_.refs_1_, ...), custom_call_target="tpu_custom_call" | custom-call | tf_op jit(solution)/shard_map/pallas_call | solution.py:331
  70.0 4.5 %all-to-all-done.2.state_ref = f32[16,128,128]{2,1,0:T(8,128)S(1)} async-done(((f32[16,128,128]{2,1,0:T(8,128)}), f32[16,128,128]{2,1,0:T(8,128)S(1)}, u32[]{:S(2)}, u32[]{:S(2)}) %all-to-all-start.2) | async-done | bytes 1048608 | tf_op jit(solution)/shard_map/all_to_all | solution.py:444
  74.5 6.0 %shard_map.124 = (f32[512,2048]{1,0:T(8,128)S(1)}, f32[1,512]{1,0:T(1,128)S(1)}) custom-call(f32[16,128,128]{2,1,0:T(8,128)S(1)} %all-to-all-done.2.state_ref, bf16[512,128]{1,0:T(8,128)(2,1)} %refs_0_.3, bf16[512,144]{1,0:T(8,128)(2,1)} %get-tuple-element.33.refs_4_.refs_1_, bf16[512,192]{1,0:T(8,128)(2,1)} %get-tuple-element.34.refs_2_, ...), custom_call_target="tpu_custom_call" | custom-call | tf_op jit(solution)/shard_map/pallas_call | solution.py:331
  80.5 5.6 %collective-permute-start.2 = (f32[1,512]{1,0:T(1,128)S(1)}, f32[1,512]{1,0:T(1,128)S(1)}, u32[]{:S(2)}, u32[]{:S(2)}) collective-permute-start(f32[1,512]{1,0:T(1,128)S(1)} %get-tuple-element.39), channel_id=1, source_target_pairs={{0,1},{1,0},{2,3},{3,2},{4,5},{5,4},{6,7},{7,6},{8,9},{9,8},{10,11... | collective-permute-start | bytes 6152 | tf_op jit(solution)/shard_map/ppermute | solution.py:344
  86.1 0.8 collective-permute-done.2
  86.9 0.4 collective-permute-start.3
  87.3 2.0 %collective-permute-done.3.other_ref = f32[1,512]{1,0:T(1,128)S(1)} collective-permute-done((f32[1,512]{1,0:T(1,128)S(1)}, f32[1,512]{1,0:T(1,128)S(1)}, u32[]{:S(2)}, u32[]{:S(2)}) %collective-permute-start.3) | collective-permute-done | bytes 2080 | tf_op jit(solution)/shard_map/ppermute | solution.py:344
  89.4 2.2 %shard_map.125 = bf16[512,2048]{1,0:T(8,128)(2,1)} custom-call(f32[512,2048]{1,0:T(8,128)S(1)} %get-tuple-element.38.gated_ref, f32[1,512]{1,0:T(1,128)S(1)} %add.8.mine_ref, f32[1,512]{1,0:T(1,128)S(1)} %collective-permute-done.3.other_ref, f32[1,2048]{1,0:T(1,128)S(1)} %get-tuple-element.40.gain_ref), custom_call_target="tpu_custom_call" | custom-call | tf_op jit(solution)/shard_map/pallas_call | solution.py:331
  (3 shorter events, 0.0 us)
Async XLA Ops:
  3.8 4.3 %collective-permute-start = (f32[256,128]{1,0:T(8,128)S(1)}, f32[256,128]{1,0:T(8,128)S(1)}, u32[]{:S(2)}, u32[]{:S(2)}) collective-permute-start(f32[256,128]{1,0:T(8,128)S(1)} %get-tuple-element.24), channel_id=1, source_target_pairs={{0,1},{1,0},{2,3},{3,2},{4,5},{5,4},{6,7},{7,6},{8,9},{9,8},{10,11... | collective-permute-start | bytes 393224 | tf_op jit(solution)/shard_map/ppermute | solution.py:344
  8.2 4.8 %collective-permute-start.1 = (f32[256,128]{1,0:T(8,128)S(1)}, f32[256,128]{1,0:T(8,128)S(1)}, u32[]{:S(2)}, u32[]{:S(2)}) collective-permute-start(f32[256,128]{1,0:T(8,128)S(1)} %add.7.mine_ref), channel_id=1, source_target_pairs={{0,128},{128,0},{1,129},{129,1},{2,130},{130,2},{3,131},{131,3},{4... | collective-permute-start | bytes 393224 | tf_op jit(solution)/shard_map/ppermute | solution.py:344
  55.1 5.7 %copy-start = (f32[16]{0:T(128)S(1)}, f32[16]{0:T(128)}, u32[]{:S(2)}) copy-start(f32[16]{0:T(128)} %param.21) | copy-start | bytes 196
  56.3 18.2 %all-to-all-start.2 = ((f32[16,128,128]{2,1,0:T(8,128)}), f32[16,128,128]{2,1,0:T(8,128)S(1)}, u32[]{:S(2)}, u32[]{:S(2)}) async-start(f32[16,128,128]{2,1,0:T(8,128)} %shard_map.122), calls=%async_computation.2 | async-start | bytes 2097152 | tf_op jit(solution)/shard_map/all_to_all | solution.py:444
  80.5 6.4 %collective-permute-start.2 = (f32[1,512]{1,0:T(1,128)S(1)}, f32[1,512]{1,0:T(1,128)S(1)}, u32[]{:S(2)}, u32[]{:S(2)}) collective-permute-start(f32[1,512]{1,0:T(1,128)S(1)} %get-tuple-element.39), channel_id=1, source_target_pairs={{0,1},{1,0},{2,3},{3,2},{4,5},{5,4},{6,7},{7,6},{8,9},{9,8},{10,11... | collective-permute-start | bytes 6152 | tf_op jit(solution)/shard_map/ppermute | solution.py:344
  86.9 2.4 %collective-permute-start.3 = (f32[1,512]{1,0:T(1,128)S(1)}, f32[1,512]{1,0:T(1,128)S(1)}, u32[]{:S(2)}, u32[]{:S(2)}) collective-permute-start(f32[1,512]{1,0:T(1,128)S(1)} %add.8.mine_ref), channel_id=1, source_target_pairs={{0,128},{128,0},{1,129},{129,1},{2,130},{130,2},{3,131},{131,3},{4... | collective-permute-start | bytes 6152 | tf_op jit(solution)/shard_map/ppermute | solution.py:344

commit v7 on v5

--- a/solution.py
+++ b/solution.py
@@ -180,8 +180,8 @@
 
 
 def within_kernel(skip_ref, *refs):
-    far, (base_out, gain_out), near = refs[:9], refs[9:11], refs[11:20]
-    base_ref, gain_ref, scored, in_sems, out_sems = refs[20:]
+    far, (base_out, gain_ref), near = refs[:9], refs[9:11], refs[11:20]
+    base_ref, scored, in_sems, out_sems = refs[20:]
     copies = fetch(far, near, in_sems)
     in_ref, read_ref, frames_ref, rows_ref, columns_ref, w_ref, pooled_ref, keys_ref, stream_ref = near
     heads = keys_ref.shape[0]
@@ -205,20 +205,18 @@
     read_twice = jnp.concatenate([read, read], axis=1)
     late_rows = slice(BLK, 2 * BLK)
 
-    def results(q):
+    def result(q):
         lanes = pl.ds(pl.multiple_of(q * 2 * P_SIZE, 2 * P_SIZE), 2 * P_SIZE)
-        return (
-            pltpu.make_async_copy(base_ref.at[:, lanes], base_out.at[:, lanes], out_sems.at[0, q]),
-            pltpu.make_async_copy(gain_ref.at[:, lanes], gain_out.at[:, lanes], out_sems.at[1, q]),
-        )
+        return pltpu.make_async_copy(base_ref.at[:, lanes], base_out.at[:, lanes], out_sems.at[q])
 
     def pair(q, carry):
         lanes = pl.ds(pl.multiple_of(q * 2 * P_SIZE, 2 * P_SIZE), 2 * P_SIZE)
         w = w_ref[:, lanes]
         gate = dot(pooled_ref[...], jnp.concatenate([w, w, w], axis=0))
-        silu = gate / (1.0 + jnp.exp(-gate))
+        half = 0.5 * gate
+        silu = half + half * jnp.tanh(half)
         chosen = pick(heads, q)
-        gain_ref[:, lanes] = silu * dot(columns_ref[:, : 3 * heads], chosen)
+        gain_ref[:, lanes] = (silu * dot(columns_ref[:, : 3 * heads], chosen)).astype(bf16)
         cum_col = dot(columns_ref[:, 6 * heads :], chosen)
         stream = stream_ref[:, lanes]
         mixed = [[], []]
@@ -240,13 +238,11 @@
         carried = own * dot(read_twice, side_by_side(first))
         base_ref[:BLK, lanes] = jnp.concatenate(mixed[0], axis=1) * silu[:BLK]
         base_ref[BLK:, lanes] = (jnp.concatenate(mixed[1], axis=1) + carried) * silu[BLK:]
-        for copy in results(q):
-            copy.start()
+        result(q).start()
         return carry
 
     def finish(q, carry):
-        for copy in results(q):
-            copy.wait()
+        result(q).wait()
         return carry
 
     lax.fori_loop(0, heads // 2, pair, 0)
@@ -276,21 +272,17 @@
         state = jnp.exp(-got_ref[i, N : N + 1, :]) * state + got_ref[i, :N, :]
 
 
-def carry_kernel(state_ref, read_far, base_far, gain_far, gated_ref, energy_ref, read_ref, base_ref, gain_ref, acc, sems):
+def carry_kernel(state_ref, gain_ref, read_far, base_far, gated_ref, energy_ref, read_ref, base_ref, acc, sems):
     heads = state_ref.shape[0]
 
-    def operands(q):
+    def base(q):
         lanes = pl.ds(pl.multiple_of(q * 2 * P_SIZE, 2 * P_SIZE), 2 * P_SIZE)
-        return (
-            pltpu.make_async_copy(base_far.at[:, lanes], base_ref.at[:, lanes], sems.at[0, q]),
-            pltpu.make_async_copy(gain_far.at[:, lanes], gain_ref.at[:, lanes], sems.at[1, q]),
-        )
-
-    first = pltpu.make_async_copy(read_far, read_ref, sems.at[0, heads // 2])
+        return pltpu.make_async_copy(base_far.at[:, lanes], base_ref.at[:, lanes], sems.at[q])
+
+    first = pltpu.make_async_copy(read_far, read_ref, sems.at[heads // 2])
     first.start()
     for q in range(heads // 2):
-        for copy in operands(q):
-            copy.start()
+        base(q).start()
     acc[...] = jnp.zeros_like(acc)
     first.wait()
     read = read_ref[...]
@@ -299,9 +291,8 @@
     def pair(q, carry):
         lanes = pl.ds(pl.multiple_of(q * 2 * P_SIZE, 2 * P_SIZE), 2 * P_SIZE)
         carried = dot(read_twice, side_by_side([state_ref[2 * q], state_ref[2 * q + 1]]))
-        for copy in operands(q):
-            copy.wait()
-        gated = base_ref[:, lanes] + gain_ref[:, lanes] * carried
+        base(q).wait()
+        gated = base_ref[:, lanes] + gain_ref[:, lanes].astype(f32) * carried
         gated_ref[:, lanes] = gated
         squares = gated * gated
         acc[...] += squares[:, :P_SIZE] + squares[:, P_SIZE:]
@@ -323,7 +314,7 @@
             held[rows, lanes] = (gated_ref[rows, lanes] * column * gain_ref[:, lanes]).astype(bf16)
             return carry
 
-        lax.fori_loop(0, held.shape[1] // P_SIZE, head, 0, unroll=4)
+        lax.fori_loop(0, held.shape[1] // P_SIZE, head, 0, unroll=8)
         copies.append(pltpu.make_async_copy(held.at[rows], out_ref.at[rows], sems.at[k]))
         copies[-1].start()
     for copy in copies:
@@ -434,14 +425,13 @@
     base, gain = call(
         within_kernel,
         (skip.reshape(1, heads),) + outside(held),
-        [((tokens, width), f32, True), ((tokens, width), f32, True)],
+        [((tokens, width), f32, True), ((tokens, width), bf16)],
         [pltpu.VMEM(array.shape, array.dtype) for array in held]
         + [
             pltpu.VMEM((tokens, width), f32),
-            pltpu.VMEM((tokens, width), f32),
             pltpu.VMEM((blocks, BLK, BLK), f32),
             pltpu.SemaphoreType.DMA((len(held),)),
-            pltpu.SemaphoreType.DMA((2, heads // 2)),
+            pltpu.SemaphoreType.DMA((heads // 2,)),
         ],
         specs=[SMEM] + [HBM] * len(held),
     )
@@ -453,16 +443,15 @@
 
     gated, energy = call(
         carry_kernel,
-        (incoming,) + outside((output_map, base, gain)),
+        (incoming, gain) + outside((output_map, base)),
         [((tokens, width), f32), ((1, tokens), f32)],
         [
             pltpu.VMEM((tokens, N), bf16),
             pltpu.VMEM((tokens, width), f32),
-            pltpu.VMEM((tokens, width), f32),
             pltpu.VMEM((tokens, P_SIZE), f32),
-            pltpu.SemaphoreType.DMA((2, heads // 2 + 1)),
-        ],
-        specs=[VMEM, HBM, HBM, HBM],
+            pltpu.SemaphoreType.DMA((heads // 2 + 1,)),
+        ],
+        specs=[VMEM, VMEM, HBM, HBM],
     )
     chip_energy = energy + swap(energy, "mp")
     other_energy = swap(chip_energy, "section")

time: 90 us -> 89.8 us (level)
  no operation moved by 1% of the time
where the time goes in v7:
time: 89.8 us; the launch traced here: 89.5 us
  blocking collectives  39.1 us (44%)
  Pallas kernels  27.9 us (31%)
  starting transfers between devices  14 us (16%)
  waiting for transfers between devices  8.43 us (9%)
    pallas_call x8, Pallas kernels, call(): pl.pallas_call(kernel, out_shape=[pltpu.HBM(*out[:2]) if out[2:] else jax...  27.9 us
    all_to_all x1, blocking collectives, body(): got = lax.all_to_all(pay, 'ctx', 0, 0, axis_index_groups=groups, tiled=True)  23.6 us
    all_to_all x1, blocking collectives, body(): lax.all_to_all(total, 'ctx', 0, 0, axis_index_groups=peers, tiled=True)  15.5 us
    ppermute x4, starting transfers between devices, swap(): return lax.ppermute(value, axis, [(0, 1), (1, 0)])  9.46 us
    ppermute x4, waiting for transfers between devices, swap(): return lax.ppermute(value, axis, [(0, 1), (1, 0)])  6.85 us
    all_to_all x1, starting transfers between devices, body(): lax.all_to_all(sent, 'ctx', 0, 0, axis_index_groups=groups, tiled=True)  4.55 us
  transfers between devices with their start and end apart: 5, of which 5 were waited for; matrix products, arithmetic and copies ran while one was open for 0% of the time, Pallas kernels for 15%

profile of v7, /device:TPU:1, one launch (start us, length us, event | category | flops | bytes accessed | tf_op | source)
XLA Modules:
  0.0 89.5 jit_solution(16291608149832555208)
XLA Ops:
  0.0 3.8 %shard_map.118 = (f32[256,128]{1,0:T(8,128)S(1)}, f32[16,512]{1,0:T(8,128)S(1)}, bf16[512,128]{1,0:T(8,128)(2,1)S(1)}, bf16[64,2048]{1,0:T(8,128)(2,1)S(1)}, bf1...) custom-call(f32[41,1,256]{2,1,0:T(1,128)} %bitcast.10, s32[41,1,256]{2,1,0:T(1,128)} %bitcast.11, ...), custom_call_target="tpu_custom_call" | custom-call | tf_op jit(solution)/shard_map/pallas_call | solution.py:329
  3.8 3.3 %collective-permute-start = (f32[256,128]{1,0:T(8,128)S(1)}, f32[256,128]{1,0:T(8,128)S(1)}, u32[]{:S(2)}, u32[]{:S(2)}) collective-permute-start(f32[256,128]{1,0:T(8,128)S(1)} %get-tuple-element.26), channel_id=1, source_target_pairs={{0,1},{1,0},{2,3},{3,2},{4,5},{5,4},{6,7},{7,6},{8,9},{9,8},{10,11... | collective-permute-start | bytes 393224 | tf_op jit(solution)/shard_map/ppermute | solution.py:342
  7.2 1.0 %collective-permute-done = f32[256,128]{1,0:T(8,128)S(1)} collective-permute-done((f32[256,128]{1,0:T(8,128)S(1)}, f32[256,128]{1,0:T(8,128)S(1)}, u32[]{:S(2)}, u32[]{:S(2)}) %collective-permute-start) | collective-permute-done | bytes 131104 | tf_op jit(solution)/shard_map/ppermute | solution.py:342
  8.2 0.1 collective-permute-start.1
  8.3 1.7 %shard_map.119 = (bf16[2,16,128,256]{3,2,1,0:T(8,128)(2,1)S(1)}, f32[2,16,128]{2,1,0:T(8,128)S(1)}, bf16[512,144]{1,0:T(8,128)(2,1)}, f32[16,512]{1,0:T(8,128)}, bf16[16,128,256]{2,1,0:T(8,128)(2,1)}) custom-call(f32[16,512]{1,0:T(8,128)S(1)} %get-tuple-element.29.forget_ref, bf16[512,128]{1,0:T(8,128)(2,1)S(1)} %get-tuple-element.30.in_ref), custom_call_target="tpu_custom_call" | custom-call | tf_op jit(solution)/shard_map/pallas_call | solution.py:329
  10.0 3.0 %collective-permute-done.1.other_ref = f32[256,128]{1,0:T(8,128)S(1)} collective-permute-done((f32[256,128]{1,0:T(8,128)S(1)}, f32[256,128]{1,0:T(8,128)S(1)}, u32[]{:S(2)}, u32[]{:S(2)}) %collective-permute-start.1) | collective-permute-done | bytes 131104 | tf_op jit(solution)/shard_map/ppermute | solution.py:342
  13.0 3.0 %shard_map.120 = (f32[16,136,128]{2,1,0:T(8,128)S(1)}, bf16[512,2048]{1,0:T(8,128)(2,1)}, bf16[512,192]{1,0:T(8,128)(2,1)}) custom-call(f32[256,128]{1,0:T(8,128)S(1)} %add.7.mine_ref, f32[256,128]{1,0:T(8,128)S(1)} %collective-permute-done.1.other_ref, bf16[64,2048]{1,0:T(8,128)(2,1)S(1)} %get-tuple-element.27.w_ref, ...), custom_call_target="tpu_custom_call" | custom-call | tf_op jit(solution)/shard_map/pallas_call | solution.py:329
  16.0 23.6 %all_to_all.15.got_ref = f32[16,136,128]{2,1,0:T(8,128)S(1)} all-to-all(f32[16,136,128]{2,1,0:T(8,128)S(1)} %get-tuple-element.33), channel_id=1, replica_groups={{0,2,4,6,8,10,12,14,16,18,20,22,24,26,28,30},{32,34,36,38,40,42,44,46,4..., dimensions={0} | all-to-all | bytes 2228224 | tf_op jit(solution)/shard_map/all_to_all | solution.py:421
  39.6 0.1 shard_map.121
  39.7 15.5 %all_to_all.16.totals_ref = f32[4,136,128]{2,1,0:T(8,128)S(1)} all-to-all(f32[4,136,128]{2,1,0:T(8,128)S(1)} %shard_map.121), channel_id=1, replica_groups={{0,32,64,96},{2,34,66,98},{4,36,68,100},{6,38,70,102},{8,40,72,104},{10..., dimensions={0} | all-to-all | bytes 557056 | tf_op jit(solution)/shard_map/all_to_all | solution.py:440
  55.1 0.0 copy-start
  55.1 1.1 %shard_map.122 = f32[16,128,128]{2,1,0:T(8,128)} custom-call(f32[16,136,128]{2,1,0:T(8,128)S(1)} %all_to_all.15.got_ref, f32[4,136,128]{2,1,0:T(8,128)S(1)} %all_to_all.16.totals_ref, s32[1,128]{1,0:T(1,128)S(1)} %broadcast_in_dim.3.place_ref), custom_call_target="tpu_custom_call" | custom-call | tf_op jit(solution)/shard_map/pallas_call | solution.py:329
  56.3 4.5 %all-to-all-start.2 = ((f32[16,128,128]{2,1,0:T(8,128)}), f32[16,128,128]{2,1,0:T(8,128)S(1)}, u32[]{:S(2)}, u32[]{:S(2)}) async-start(f32[16,128,128]{2,1,0:T(8,128)} %shard_map.122), calls=%async_computation.2 | async-start | bytes 2097152 | tf_op jit(solution)/shard_map/all_to_all | solution.py:442
  60.8 0.0 copy-done
  60.8 12.1 %shard_map.123 = (f32[512,2048]{1,0:T(8,128)}, bf16[512,2048]{1,0:T(8,128)(2,1)S(1)}) custom-call(f32[1,16]{1,0:T(1,128)S(1)} %bitcast.9, bf16[512,128]{1,0:T(8,128)(2,1)} %refs_0_.1, bf16[512,128]{1,0:T(8,128)(2,1)} %read_far.1, s32[1,512]{1,0:T(1,128)} %bitcast.15, f32[16,512]{1,0:T(8,128)} %get-tuple-element.35.refs_3_, ...), custom_call_target="tpu_custom_call" | custom-call | tf_op jit(solution)/shard_map/pallas_call | solution.py:329
  72.9 1.6 %all-to-all-done.2.state_ref = f32[16,128,128]{2,1,0:T(8,128)S(1)} async-done(((f32[16,128,128]{2,1,0:T(8,128)}), f32[16,128,128]{2,1,0:T(8,128)S(1)}, u32[]{:S(2)}, u32[]{:S(2)}) %all-to-all-start.2) | async-done | bytes 1048608 | tf_op jit(solution)/shard_map/all_to_all | solution.py:442
  74.5 4.0 %shard_map.124 = (f32[512,2048]{1,0:T(8,128)S(1)}, f32[1,512]{1,0:T(1,128)S(1)}) custom-call(f32[16,128,128]{2,1,0:T(8,128)S(1)} %all-to-all-done.2.state_ref, bf16[512,2048]{1,0:T(8,128)(2,1)S(1)} %get-tuple-element.40.gain_ref, bf16[512,128]{1,0:T(8,128)(2,1)} %read_far.1, f32[512,2048]{1,0:T(8,128)} %get-tuple-element.41.base_far), custom_call_target="tpu_custom_call" | custom-call | tf_op jit(solution)/shard_map/pallas_call | solution.py:329
  78.5 5.6 %collective-permute-start.2 = (f32[1,512]{1,0:T(1,128)S(1)}, f32[1,512]{1,0:T(1,128)S(1)}, u32[]{:S(2)}, u32[]{:S(2)}) collective-permute-start(f32[1,512]{1,0:T(1,128)S(1)} %get-tuple-element.43), channel_id=1, source_target_pairs={{0,1},{1,0},{2,3},{3,2},{4,5},{5,4},{6,7},{7,6},{8,9},{9,8},{10,11... | collective-permute-start | bytes 6152 | tf_op jit(solution)/shard_map/ppermute | solution.py:342
  84.1 0.8 collective-permute-done.2
  84.9 0.4 collective-permute-start.3
  85.3 2.0 %collective-permute-done.3.other_ref = f32[1,512]{1,0:T(1,128)S(1)} collective-permute-done((f32[1,512]{1,0:T(1,128)S(1)}, f32[1,512]{1,0:T(1,128)S(1)}, u32[]{:S(2)}, u32[]{:S(2)}) %collective-permute-start.3) | collective-permute-done | bytes 2080 | tf_op jit(solution)/shard_map/ppermute | solution.py:342
  87.4 2.2 %shard_map.125 = bf16[512,2048]{1,0:T(8,128)(2,1)} custom-call(f32[512,2048]{1,0:T(8,128)S(1)} %get-tuple-element.42.gated_ref, f32[1,512]{1,0:T(1,128)S(1)} %add.8.mine_ref, f32[1,512]{1,0:T(1,128)S(1)} %collective-permute-done.3.other_ref, f32[1,2048]{1,0:T(1,128)S(1)} %get-tuple-element.44.gain_ref), custom_call_target="tpu_custom_call" | custom-call | tf_op jit(solution)/shard_map/pallas_call | solution.py:329
  (3 shorter events, 0.0 us)
Async XLA Ops:
  3.8 4.3 %collective-permute-start = (f32[256,128]{1,0:T(8,128)S(1)}, f32[256,128]{1,0:T(8,128)S(1)}, u32[]{:S(2)}, u32[]{:S(2)}) collective-permute-start(f32[256,128]{1,0:T(8,128)S(1)} %get-tuple-element.26), channel_id=1, source_target_pairs={{0,1},{1,0},{2,3},{3,2},{4,5},{5,4},{6,7},{7,6},{8,9},{9,8},{10,11... | collective-permute-start | bytes 393224 | tf_op jit(solution)/shard_map/ppermute | solution.py:342
  8.2 4.8 %collective-permute-start.1 = (f32[256,128]{1,0:T(8,128)S(1)}, f32[256,128]{1,0:T(8,128)S(1)}, u32[]{:S(2)}, u32[]{:S(2)}) collective-permute-start(f32[256,128]{1,0:T(8,128)S(1)} %add.7.mine_ref), channel_id=1, source_target_pairs={{0,128},{128,0},{1,129},{129,1},{2,130},{130,2},{3,131},{131,3},{4... | collective-permute-start | bytes 393224 | tf_op jit(solution)/shard_map/ppermute | solution.py:342
  55.1 5.7 %copy-start = (f32[16]{0:T(128)S(1)}, f32[16]{0:T(128)}, u32[]{:S(2)}) copy-start(f32[16]{0:T(128)} %param.21) | copy-start | bytes 196
  56.3 18.2 %all-to-all-start.2 = ((f32[16,128,128]{2,1,0:T(8,128)}), f32[16,128,128]{2,1,0:T(8,128)S(1)}, u32[]{:S(2)}, u32[]{:S(2)}) async-start(f32[16,128,128]{2,1,0:T(8,128)} %shard_map.122), calls=%async_computation.2 | async-start | bytes 2097152 | tf_op jit(solution)/shard_map/all_to_all | solution.py:442
  78.5 6.4 %collective-permute-start.2 = (f32[1,512]{1,0:T(1,128)S(1)}, f32[1,512]{1,0:T(1,128)S(1)}, u32[]{:S(2)}, u32[]{:S(2)}) collective-permute-start(f32[1,512]{1,0:T(1,128)S(1)} %get-tuple-element.43), channel_id=1, source_target_pairs={{0,1},{1,0},{2,3},{3,2},{4,5},{5,4},{6,7},{7,6},{8,9},{9,8},{10,11... | collective-permute-start | bytes 6152 | tf_op jit(solution)/shard_map/ppermute | solution.py:342
  84.9 2.4 %collective-permute-start.3 = (f32[1,512]{1,0:T(1,128)S(1)}, f32[1,512]{1,0:T(1,128)S(1)}, u32[]{:S(2)}, u32[]{:S(2)}) collective-permute-start(f32[1,512]{1,0:T(1,128)S(1)} %add.8.mine_ref), channel_id=1, source_target_pairs={{0,128},{128,0},{1,129},{129,1},{2,130},{130,2},{3,131},{131,3},{4... | collective-permute-start | bytes 6152 | tf_op jit(solution)/shard_map/ppermute | solution.py:342

commit v8 on v5

--- a/solution.py
+++ b/solution.py
@@ -14,7 +14,8 @@
 DI = 8192
 EPSILON = 1e-05
 LOG2E = math.log2(math.e)
-CHUNK = 64
+SPAN = 128
+CHUNK = 32
 EXTRA = 8
 
 f32 = jnp.float32
@@ -48,9 +49,9 @@
 
 
 def pool_kernel(*refs):
-    count = (len(refs) - 4) // 2
+    count = (len(refs) - 5) // 2
     far, out_ref, near = refs[:count], refs[count], refs[count + 1 : 2 * count - 2]
-    logits_ref, cells_ref, feats_ref, prob, hits, sems = refs[2 * count - 2 :]
+    logits_ref, cells_ref, feats_ref, place, prob, hits, sems = refs[2 * count - 2 :]
     near = (logits_ref, cells_ref, feats_ref) + tuple(near)
     copies = [pltpu.make_async_copy(far[i], near[i], sems.at[i]) for i in range(count)]
     for copy in copies:
@@ -58,22 +59,29 @@
     for copy in copies[:3]:
         copy.wait()
     bins, _, rows = logits_ref.shape
+    spans = hits.shape[0] // SPAN
     logits = logits_ref[...]
     raised = jnp.exp(logits - jnp.max(logits, axis=0, keepdims=True))
-    prob[...] = raised / jnp.sum(raised, axis=0, keepdims=True)
-
-    def chunk(k, carry):
-        first = pl.multiple_of(k * CHUNK, CHUNK)
+    probability = raised / jnp.sum(raised, axis=0, keepdims=True)
+    cells = cells_ref[...]
+    place[...] = cells & (SPAN - 1)
+    for k in range(spans):
+        prob[k] = jnp.where(cells // SPAN == k, probability, 0.0)
+
+    def chunk(i, carry):
+        first = pl.multiple_of(i * CHUNK, CHUNK)
         ids = lax.broadcasted_iota(jnp.int32, (CHUNK, rows), 0) + first
-        acc = jnp.zeros((CHUNK, rows), f32)
+        sums = [jnp.zeros((CHUNK, rows), f32) for _ in range(spans)]
         for d in range(bins):
-            acc = acc + jnp.where(cells_ref[d] == ids, prob[d], 0.0)
-        high, low = terms(acc, 2)
-        hits[pl.ds(first, CHUNK), :rows] = high
-        hits[pl.ds(first, CHUNK), rows:] = low
-        return carry
-
-    lax.fori_loop(0, hits.shape[0] // CHUNK, chunk, 0)
+            hit = place[d] == ids
+            sums = [sums[k] + jnp.where(hit, prob[k, d], 0.0) for k in range(spans)]
+        for k in range(spans):
+            high, low = terms(sums[k], 2)
+            hits[pl.ds(k * SPAN + first, CHUNK), :rows] = high
+            hits[pl.ds(k * SPAN + first, CHUNK), rows:] = low
+        return carry
+
+    lax.fori_loop(0, SPAN // CHUNK, chunk, 0)
     feats = feats_ref[...]
     pooled = lax.dot_general(
         hits[...],
@@ -216,7 +224,8 @@
         lanes = pl.ds(pl.multiple_of(q * 2 * P_SIZE, 2 * P_SIZE), 2 * P_SIZE)
         w = w_ref[:, lanes]
         gate = dot(pooled_ref[...], jnp.concatenate([w, w, w], axis=0))
-        silu = gate / (1.0 + jnp.exp(-gate))
+        half = 0.5 * gate
+        silu = half + half * jnp.tanh(half)
         chosen = pick(heads, q)
         gain_ref[:, lanes] = silu * dot(columns_ref[:, : 3 * heads], chosen)
         cum_col = dot(columns_ref[:, 6 * heads :], chosen)
@@ -249,7 +258,7 @@
             copy.wait()
         return carry
 
-    lax.fori_loop(0, heads // 2, pair, 0)
+    lax.fori_loop(0, heads // 2, pair, 0, unroll=2)
     lax.fori_loop(0, heads // 2, finish, 0)
 
 
@@ -265,15 +274,20 @@
         total_ref[k, N:, :] = log
 
 
-def spread_kernel(got_ref, totals_ref, place_ref, out_ref):
+def spread_kernel(got_ref, totals_ref, place_ref, out_ref, held, sems):
     place = place_ref[...]
-    state = jnp.zeros(out_ref.shape[1:], f32)
+    state = jnp.zeros(held.shape[1:], f32)
     for k in range(totals_ref.shape[0] - 1):
         later = jnp.exp(-totals_ref[k, N : N + 1, :]) * state + totals_ref[k, :N, :]
         state = jnp.where(jnp.broadcast_to(place, state.shape) > k, later, state)
+    copies = []
     for i in range(got_ref.shape[0]):
-        out_ref[i] = state
+        held[i] = state
+        copies.append(pltpu.make_async_copy(held.at[i], out_ref.at[i], sems.at[i]))
+        copies[-1].start()
         state = jnp.exp(-got_ref[i, N : N + 1, :]) * state + got_ref[i, :N, :]
+    for copy in copies:
+        copy.wait()
 
 
 def carry_kernel(state_ref, read_far, base_far, gain_far, gated_ref, energy_ref, read_ref, base_ref, gain_ref, acc, sems):
@@ -298,16 +312,21 @@
 
     def pair(q, carry):
         lanes = pl.ds(pl.multiple_of(q * 2 * P_SIZE, 2 * P_SIZE), 2 * P_SIZE)
-        carried = dot(read_twice, side_by_side([state_ref[2 * q], state_ref[2 * q + 1]]))
+        gated_ref[:, lanes] = dot(read_twice, side_by_side([state_ref[2 * q], state_ref[2 * q + 1]]))
+        return carry
+
+    def gate(q, carry):
+        lanes = pl.ds(pl.multiple_of(q * 2 * P_SIZE, 2 * P_SIZE), 2 * P_SIZE)
         for copy in operands(q):
             copy.wait()
-        gated = base_ref[:, lanes] + gain_ref[:, lanes] * carried
+        gated = base_ref[:, lanes] + gain_ref[:, lanes] * gated_ref[:, lanes]
         gated_ref[:, lanes] = gated
         squares = gated * gated
         acc[...] += squares[:, :P_SIZE] + squares[:, P_SIZE:]
         return carry
 
-    lax.fori_loop(0, heads // 2, pair, 0)
+    lax.fori_loop(0, heads // 2, pair, 0, unroll=2)
+    lax.fori_loop(0, heads // 2, gate, 0)
     energy_ref[...] = jnp.sum(acc[...].T, axis=0, keepdims=True)
 
 
@@ -323,7 +342,7 @@
             held[rows, lanes] = (gated_ref[rows, lanes] * column * gain_ref[:, lanes]).astype(bf16)
             return carry
 
-        lax.fori_loop(0, held.shape[1] // P_SIZE, head, 0, unroll=4)
+        lax.fori_loop(0, held.shape[1] // P_SIZE, head, 0, unroll=8)
         copies.append(pltpu.make_async_copy(held.at[rows], out_ref.at[rows], sems.at[k]))
         copies[-1].start()
     for copy in copies:
@@ -384,7 +403,8 @@
             pltpu.VMEM((bins, 1, pixels), f32),
             pltpu.VMEM((bins, 1, pixels), jnp.int32),
             pltpu.VMEM((CF, pixels), bf16),
-            pltpu.VMEM((bins, 1, pixels), f32),
+            pltpu.VMEM((bins, 1, pixels), jnp.int32),
+            pltpu.VMEM((tokens // SPAN, bins, 1, pixels), f32),
             pltpu.VMEM((tokens, 2 * pixels), bf16),
             pltpu.SemaphoreType.DMA((len(near + far),)),
         ],
@@ -448,7 +468,12 @@
 
     (total,) = call(total_kernel, (got,), [((shards // heads, N + EXTRA, P_SIZE), f32)])
     totals = lax.all_to_all(total, "ctx", 0, 0, axis_index_groups=peers, tiled=True)
-    (sent,) = call(spread_kernel, (got, totals, place), [((heads, N, P_SIZE), f32)])
+    (sent,) = call(
+        spread_kernel,
+        (got, totals, place),
+        [((heads, N, P_SIZE), f32, True)],
+        [pltpu.VMEM((heads, N, P_SIZE), f32), pltpu.SemaphoreType.DMA((heads,))],
+    )
     incoming = lax.all_to_all(sent, "ctx", 0, 0, axis_index_groups=groups, tiled=True)
 
     gated, energy = call(

time: 90 us -> 89.2 us (level)
  Pallas kernels: 28.3 us -> 26.6 us
    pallas_call x8, Pallas kernels: 28.3 us -> 26.6 us  [call(): pl.pallas_call(kernel, out_shape=[pltpu.HBM(*out[:2]) if out[2:] else jax...]
where the time goes in v8:
time: 89.2 us; the launch traced here: 88.9 us
  blocking collectives  39.1 us (44%)
  Pallas kernels  26.6 us (30%)
  starting transfers between devices  14 us (16%)
  waiting for transfers between devices  9.12 us (10%)
    pallas_call x8, Pallas kernels, call(): pl.pallas_call(kernel, out_shape=[pltpu.HBM(*out[:2]) if out[2:] else jax...  26.6 us
    all_to_all x1, blocking collectives, body(): got = lax.all_to_all(pay, 'ctx', 0, 0, axis_index_groups=groups, tiled=True)  23.6 us
    all_to_all x1, blocking collectives, body(): lax.all_to_all(total, 'ctx', 0, 0, axis_index_groups=peers, tiled=True)  15.5 us
    ppermute x4, starting transfers between devices, swap(): return lax.ppermute(value, axis, [(0, 1), (1, 0)])  9.45 us
    ppermute x4, waiting for transfers between devices, swap(): return lax.ppermute(value, axis, [(0, 1), (1, 0)])  6.84 us
    all_to_all x1, starting transfers between devices, body(): lax.all_to_all(sent, 'ctx', 0, 0, axis_index_groups=groups, tiled=True)  4.58 us
    all_to_all x1, waiting for transfers between devices, body(): lax.all_to_all(sent, 'ctx', 0, 0, axis_index_groups=groups, tiled=True)  2.27 us
  transfers between devices with their start and end apart: 5, of which 5 were waited for; matrix products, arithmetic and copies ran while one was open for 0% of the time, Pallas kernels for 15%

profile of v8, /device:TPU:1, one launch (start us, length us, event | category | flops | bytes accessed | tf_op | source)
XLA Modules:
  0.0 88.9 jit_solution(1725793729858349400)
XLA Ops:
  0.0 3.2 %shard_map.118 = (f32[256,128]{1,0:T(8,128)S(1)}, f32[16,512]{1,0:T(8,128)S(1)}, bf16[512,128]{1,0:T(8,128)(2,1)S(1)}, bf16[64,2048]{1,0:T(8,128)(2,1)S(1)}, bf1...) custom-call(f32[41,1,256]{2,1,0:T(1,128)} %bitcast.10, s32[41,1,256]{2,1,0:T(1,128)} %bitcast.11, ...), custom_call_target="tpu_custom_call" | custom-call | tf_op jit(solution)/shard_map/pallas_call | solution.py:357
  3.2 3.3 %collective-permute-start = (f32[256,128]{1,0:T(8,128)S(1)}, f32[256,128]{1,0:T(8,128)S(1)}, u32[]{:S(2)}, u32[]{:S(2)}) collective-permute-start(f32[256,128]{1,0:T(8,128)S(1)} %get-tuple-element.26), channel_id=1, source_target_pairs={{0,1},{1,0},{2,3},{3,2},{4,5},{5,4},{6,7},{7,6},{8,9},{9,8},{10,11... | collective-permute-start | bytes 393224 | tf_op jit(solution)/shard_map/ppermute | solution.py:370
  6.6 1.0 %collective-permute-done = f32[256,128]{1,0:T(8,128)S(1)} collective-permute-done((f32[256,128]{1,0:T(8,128)S(1)}, f32[256,128]{1,0:T(8,128)S(1)}, u32[]{:S(2)}, u32[]{:S(2)}) %collective-permute-start) | collective-permute-done | bytes 131104 | tf_op jit(solution)/shard_map/ppermute | solution.py:370
  7.6 0.1 collective-permute-start.1
  7.7 1.7 %shard_map.119 = (bf16[2,16,128,256]{3,2,1,0:T(8,128)(2,1)S(1)}, f32[2,16,128]{2,1,0:T(8,128)S(1)}, bf16[512,144]{1,0:T(8,128)(2,1)}, f32[16,512]{1,0:T(8,128)}, bf16[16,128,256]{2,1,0:T(8,128)(2,1)}) custom-call(f32[16,512]{1,0:T(8,128)S(1)} %get-tuple-element.29.forget_ref, bf16[512,128]{1,0:T(8,128)(2,1)S(1)} %get-tuple-element.30.in_ref), custom_call_target="tpu_custom_call" | custom-call | tf_op jit(solution)/shard_map/pallas_call | solution.py:357
  9.4 3.0 %collective-permute-done.1.other_ref = f32[256,128]{1,0:T(8,128)S(1)} collective-permute-done((f32[256,128]{1,0:T(8,128)S(1)}, f32[256,128]{1,0:T(8,128)S(1)}, u32[]{:S(2)}, u32[]{:S(2)}) %collective-permute-start.1) | collective-permute-done | bytes 131104 | tf_op jit(solution)/shard_map/ppermute | solution.py:370
  12.4 3.0 %shard_map.120 = (f32[16,136,128]{2,1,0:T(8,128)S(1)}, bf16[512,2048]{1,0:T(8,128)(2,1)}, bf16[512,192]{1,0:T(8,128)(2,1)}) custom-call(f32[256,128]{1,0:T(8,128)S(1)} %add.7.mine_ref, f32[256,128]{1,0:T(8,128)S(1)} %collective-permute-done.1.other_ref, bf16[64,2048]{1,0:T(8,128)(2,1)S(1)} %get-tuple-element.27.w_ref, ...), custom_call_target="tpu_custom_call" | custom-call | tf_op jit(solution)/shard_map/pallas_call | solution.py:357
  15.4 23.6 %all_to_all.15.got_ref = f32[16,136,128]{2,1,0:T(8,128)S(1)} all-to-all(f32[16,136,128]{2,1,0:T(8,128)S(1)} %get-tuple-element.33), channel_id=1, replica_groups={{0,2,4,6,8,10,12,14,16,18,20,22,24,26,28,30},{32,34,36,38,40,42,44,46,4..., dimensions={0} | all-to-all | bytes 2228224 | tf_op jit(solution)/shard_map/all_to_all | solution.py:450
  38.9 0.1 shard_map.121
  39.0 15.5 %all_to_all.16.totals_ref = f32[4,136,128]{2,1,0:T(8,128)S(1)} all-to-all(f32[4,136,128]{2,1,0:T(8,128)S(1)} %shard_map.121), channel_id=1, replica_groups={{0,32,64,96},{2,34,66,98},{4,36,68,100},{6,38,70,102},{8,40,72,104},{10..., dimensions={0} | all-to-all | bytes 557056 | tf_op jit(solution)/shard_map/all_to_all | solution.py:470
  54.5 0.0 copy-start
  54.5 1.1 %shard_map.122 = f32[16,128,128]{2,1,0:T(8,128)} custom-call(f32[16,136,128]{2,1,0:T(8,128)S(1)} %all_to_all.15.got_ref, f32[4,136,128]{2,1,0:T(8,128)S(1)} %all_to_all.16.totals_ref, s32[1,128]{1,0:T(1,128)S(1)} %broadcast_in_dim.3.place_ref), custom_call_target="tpu_custom_call" | custom-call | tf_op jit(solution)/shard_map/pallas_call | solution.py:357
  55.7 4.6 %all-to-all-start.2 = ((f32[16,128,128]{2,1,0:T(8,128)}), f32[16,128,128]{2,1,0:T(8,128)S(1)}, u32[]{:S(2)}, u32[]{:S(2)}) async-start(f32[16,128,128]{2,1,0:T(8,128)} %shard_map.122), calls=%async_computation.2 | async-start | bytes 2097152 | tf_op jit(solution)/shard_map/all_to_all | solution.py:477
  60.2 0.0 copy-done
  60.2 11.4 %shard_map.123 = (f32[512,2048]{1,0:T(8,128)}, f32[512,2048]{1,0:T(8,128)}) custom-call(f32[1,16]{1,0:T(1,128)S(1)} %bitcast.9, bf16[512,128]{1,0:T(8,128)(2,1)} %refs_0_.1, bf16[512,128]{1,0:T(8,128)(2,1)} %read_far.1, s32[1,512]{1,0:T(1,128)} %bitcast.15, f32[16,512]{1,0:T(8,128)} %get-tuple-element.35.refs_3_, ...), custom_call_target="tpu_custom_call" | custom-call | tf_op jit(solution)/shard_map/pallas_call | solution.py:357
  71.6 2.3 %all-to-all-done.2.state_ref = f32[16,128,128]{2,1,0:T(8,128)S(1)} async-done(((f32[16,128,128]{2,1,0:T(8,128)}), f32[16,128,128]{2,1,0:T(8,128)S(1)}, u32[]{:S(2)}, u32[]{:S(2)}) %all-to-all-start.2) | async-done | bytes 1048608 | tf_op jit(solution)/shard_map/all_to_all | solution.py:477
  73.9 4.0 %shard_map.124 = (f32[512,2048]{1,0:T(8,128)S(1)}, f32[1,512]{1,0:T(1,128)S(1)}) custom-call(f32[16,128,128]{2,1,0:T(8,128)S(1)} %all-to-all-done.2.state_ref, bf16[512,128]{1,0:T(8,128)(2,1)} %read_far.1, f32[512,2048]{1,0:T(8,128)} %get-tuple-element.40.base_far, f32[512,2048]{1,0:T(8,128)} %get-tuple-element.41.gain_far), custom_call_target="tpu_custom_call" | custom-call | tf_op jit(solution)/shard_map/pallas_call | solution.py:357
  77.9 5.6 %collective-permute-start.2 = (f32[1,512]{1,0:T(1,128)S(1)}, f32[1,512]{1,0:T(1,128)S(1)}, u32[]{:S(2)}, u32[]{:S(2)}) collective-permute-start(f32[1,512]{1,0:T(1,128)S(1)} %get-tuple-element.43), channel_id=1, source_target_pairs={{0,1},{1,0},{2,3},{3,2},{4,5},{5,4},{6,7},{7,6},{8,9},{9,8},{10,11... | collective-permute-start | bytes 6152 | tf_op jit(solution)/shard_map/ppermute | solution.py:370
  83.5 0.8 collective-permute-done.2
  84.3 0.4 collective-permute-start.3
  84.7 2.0 %collective-permute-done.3.other_ref = f32[1,512]{1,0:T(1,128)S(1)} collective-permute-done((f32[1,512]{1,0:T(1,128)S(1)}, f32[1,512]{1,0:T(1,128)S(1)}, u32[]{:S(2)}, u32[]{:S(2)}) %collective-permute-start.3) | collective-permute-done | bytes 2080 | tf_op jit(solution)/shard_map/ppermute | solution.py:370
  86.8 2.2 %shard_map.125 = bf16[512,2048]{1,0:T(8,128)(2,1)} custom-call(f32[512,2048]{1,0:T(8,128)S(1)} %get-tuple-element.42.gated_ref, f32[1,512]{1,0:T(1,128)S(1)} %add.8.mine_ref, f32[1,512]{1,0:T(1,128)S(1)} %collective-permute-done.3.other_ref, f32[1,2048]{1,0:T(1,128)S(1)} %get-tuple-element.44.gain_ref), custom_call_target="tpu_custom_call" | custom-call | tf_op jit(solution)/shard_map/pallas_call | solution.py:357
  (3 shorter events, 0.0 us)
Async XLA Ops:
  3.2 4.3 %collective-permute-start = (f32[256,128]{1,0:T(8,128)S(1)}, f32[256,128]{1,0:T(8,128)S(1)}, u32[]{:S(2)}, u32[]{:S(2)}) collective-permute-start(f32[256,128]{1,0:T(8,128)S(1)} %get-tuple-element.26), channel_id=1, source_target_pairs={{0,1},{1,0},{2,3},{3,2},{4,5},{5,4},{6,7},{7,6},{8,9},{9,8},{10,11... | collective-permute-start | bytes 393224 | tf_op jit(solution)/shard_map/ppermute | solution.py:370
  7.6 4.8 %collective-permute-start.1 = (f32[256,128]{1,0:T(8,128)S(1)}, f32[256,128]{1,0:T(8,128)S(1)}, u32[]{:S(2)}, u32[]{:S(2)}) collective-permute-start(f32[256,128]{1,0:T(8,128)S(1)} %add.7.mine_ref), channel_id=1, source_target_pairs={{0,128},{128,0},{1,129},{129,1},{2,130},{130,2},{3,131},{131,3},{4... | collective-permute-start | bytes 393224 | tf_op jit(solution)/shard_map/ppermute | solution.py:370
  54.5 5.7 %copy-start = (f32[16]{0:T(128)S(1)}, f32[16]{0:T(128)}, u32[]{:S(2)}) copy-start(f32[16]{0:T(128)} %param.21) | copy-start | bytes 196
  55.7 18.2 %all-to-all-start.2 = ((f32[16,128,128]{2,1,0:T(8,128)}), f32[16,128,128]{2,1,0:T(8,128)S(1)}, u32[]{:S(2)}, u32[]{:S(2)}) async-start(f32[16,128,128]{2,1,0:T(8,128)} %shard_map.122), calls=%async_computation.2 | async-start | bytes 2097152 | tf_op jit(solution)/shard_map/all_to_all | solution.py:477
  77.9 6.5 %collective-permute-start.2 = (f32[1,512]{1,0:T(1,128)S(1)}, f32[1,512]{1,0:T(1,128)S(1)}, u32[]{:S(2)}, u32[]{:S(2)}) collective-permute-start(f32[1,512]{1,0:T(1,128)S(1)} %get-tuple-element.43), channel_id=1, source_target_pairs={{0,1},{1,0},{2,3},{3,2},{4,5},{5,4},{6,7},{7,6},{8,9},{9,8},{10,11... | collective-permute-start | bytes 6152 | tf_op jit(solution)/shard_map/ppermute | solution.py:370
  84.3 2.4 %collective-permute-start.3 = (f32[1,512]{1,0:T(1,128)S(1)}, f32[1,512]{1,0:T(1,128)S(1)}, u32[]{:S(2)}, u32[]{:S(2)}) collective-permute-start(f32[1,512]{1,0:T(1,128)S(1)} %add.8.mine_ref), channel_id=1, source_target_pairs={{0,128},{128,0},{1,129},{129,1},{2,130},{130,2},{3,131},{131,3},{4... | collective-permute-start | bytes 6152 | tf_op jit(solution)/shard_map/ppermute | solution.py:370

commit v9 on v8

--- a/solution.py
+++ b/solution.py
@@ -188,8 +188,8 @@
 
 
 def within_kernel(skip_ref, *refs):
-    far, (base_out, gain_out), near = refs[:9], refs[9:11], refs[11:20]
-    base_ref, gain_ref, scored, in_sems, out_sems = refs[20:]
+    far, (base_out, gain_out, gain_near), near = refs[:9], refs[9:12], refs[12:21]
+    base_ref, gain_ref, scored, in_sems, out_sems = refs[21:]
     copies = fetch(far, near, in_sems)
     in_ref, read_ref, frames_ref, rows_ref, columns_ref, w_ref, pooled_ref, keys_ref, stream_ref = near
     heads = keys_ref.shape[0]
@@ -213,21 +213,24 @@
     read_twice = jnp.concatenate([read, read], axis=1)
     late_rows = slice(BLK, 2 * BLK)
 
-    def results(q):
+    kept = gain_near.shape[1] // (2 * P_SIZE)
+
+    def base_result(q):
         lanes = pl.ds(pl.multiple_of(q * 2 * P_SIZE, 2 * P_SIZE), 2 * P_SIZE)
-        return (
-            pltpu.make_async_copy(base_ref.at[:, lanes], base_out.at[:, lanes], out_sems.at[0, q]),
-            pltpu.make_async_copy(gain_ref.at[:, lanes], gain_out.at[:, lanes], out_sems.at[1, q]),
-        )
-
-    def pair(q, carry):
+        return pltpu.make_async_copy(base_ref.at[:, lanes], base_out.at[:, lanes], out_sems.at[0, q])
+
+    def gain_result(q):
+        lanes = pl.ds(pl.multiple_of((q - kept) * 2 * P_SIZE, 2 * P_SIZE), 2 * P_SIZE)
+        return pltpu.make_async_copy(gain_ref.at[:, lanes], gain_out.at[:, lanes], out_sems.at[1, q])
+
+    def pair(q, gains, gain_lanes):
         lanes = pl.ds(pl.multiple_of(q * 2 * P_SIZE, 2 * P_SIZE), 2 * P_SIZE)
         w = w_ref[:, lanes]
         gate = dot(pooled_ref[...], jnp.concatenate([w, w, w], axis=0))
         half = 0.5 * gate
         silu = half + half * jnp.tanh(half)
         chosen = pick(heads, q)
-        gain_ref[:, lanes] = silu * dot(columns_ref[:, : 3 * heads], chosen)
+        gains[:, gain_lanes] = silu * dot(columns_ref[:, : 3 * heads], chosen)
         cum_col = dot(columns_ref[:, 6 * heads :], chosen)
         stream = stream_ref[:, lanes]
         mixed = [[], []]
@@ -249,17 +252,29 @@
         carried = own * dot(read_twice, side_by_side(first))
         base_ref[:BLK, lanes] = jnp.concatenate(mixed[0], axis=1) * silu[:BLK]
         base_ref[BLK:, lanes] = (jnp.concatenate(mixed[1], axis=1) + carried) * silu[BLK:]
-        for copy in results(q):
-            copy.start()
-        return carry
-
-    def finish(q, carry):
-        for copy in results(q):
-            copy.wait()
-        return carry
-
-    lax.fori_loop(0, heads // 2, pair, 0, unroll=2)
-    lax.fori_loop(0, heads // 2, finish, 0)
+        base_result(q).start()
+
+    def near_pair(q, carry):
+        pair(q, gain_near, pl.ds(pl.multiple_of(q * 2 * P_SIZE, 2 * P_SIZE), 2 * P_SIZE))
+        return carry
+
+    def far_pair(q, carry):
+        pair(q, gain_ref, pl.ds(pl.multiple_of((q - kept) * 2 * P_SIZE, 2 * P_SIZE), 2 * P_SIZE))
+        gain_result(q).start()
+        return carry
+
+    def base_finish(q, carry):
+        base_result(q).wait()
+        return carry
+
+    def gain_finish(q, carry):
+        gain_result(q).wait()
+        return carry
+
+    lax.fori_loop(0, kept, near_pair, 0)
+    lax.fori_loop(kept, heads // 2, far_pair, 0)
+    lax.fori_loop(0, heads // 2, base_finish, 0)
+    lax.fori_loop(kept, heads // 2, gain_finish, 0)
 
 
 def total_kernel(got_ref, total_ref):
@@ -290,48 +305,63 @@
         copy.wait()
 
 
-def carry_kernel(state_ref, read_far, base_far, gain_far, gated_ref, energy_ref, read_ref, base_ref, gain_ref, acc, sems):
+def carry_kernel(
+    state_ref, gain_near, read_far, base_far, gain_far, gated_ref, energy_ref, read_ref, base_ref, gain_ref, acc, sems
+):
     heads = state_ref.shape[0]
-
-    def operands(q):
-        lanes = pl.ds(pl.multiple_of(q * 2 * P_SIZE, 2 * P_SIZE), 2 * P_SIZE)
-        return (
-            pltpu.make_async_copy(base_far.at[:, lanes], base_ref.at[:, lanes], sems.at[0, q]),
-            pltpu.make_async_copy(gain_far.at[:, lanes], gain_ref.at[:, lanes], sems.at[1, q]),
-        )
+    kept = gain_near.shape[1] // (2 * P_SIZE)
+
+    def span(q):
+        return pl.ds(pl.multiple_of(q * 2 * P_SIZE, 2 * P_SIZE), 2 * P_SIZE)
+
+    def base(q):
+        return pltpu.make_async_copy(base_far.at[:, span(q)], base_ref.at[:, span(q)], sems.at[0, q])
+
+    def gain(q):
+        lanes = span(q - kept)
+        return pltpu.make_async_copy(gain_far.at[:, lanes], gain_ref.at[:, lanes], sems.at[1, q])
 
     first = pltpu.make_async_copy(read_far, read_ref, sems.at[0, heads // 2])
     first.start()
     for q in range(heads // 2):
-        for copy in operands(q):
-            copy.start()
+        base(q).start()
+        if q >= kept:
+            gain(q).start()
     acc[...] = jnp.zeros_like(acc)
     first.wait()
     read = read_ref[...]
     read_twice = jnp.concatenate([read, read], axis=1)
 
     def pair(q, carry):
-        lanes = pl.ds(pl.multiple_of(q * 2 * P_SIZE, 2 * P_SIZE), 2 * P_SIZE)
-        gated_ref[:, lanes] = dot(read_twice, side_by_side([state_ref[2 * q], state_ref[2 * q + 1]]))
-        return carry
-
-    def gate(q, carry):
-        lanes = pl.ds(pl.multiple_of(q * 2 * P_SIZE, 2 * P_SIZE), 2 * P_SIZE)
-        for copy in operands(q):
-            copy.wait()
-        gated = base_ref[:, lanes] + gain_ref[:, lanes] * gated_ref[:, lanes]
-        gated_ref[:, lanes] = gated
+        states = side_by_side([state_ref[2 * q], state_ref[2 * q + 1]])
+        gated_ref[:, span(q)] = dot(read_twice, states)
+        return carry
+
+    def gate(q, gains):
+        base(q).wait()
+        gated = base_ref[:, span(q)] + gains * gated_ref[:, span(q)]
+        gated_ref[:, span(q)] = gated
         squares = gated * gated
         acc[...] += squares[:, :P_SIZE] + squares[:, P_SIZE:]
+
+    def near_gate(q, carry):
+        gate(q, gain_near[:, span(q)])
+        return carry
+
+    def far_gate(q, carry):
+        gain(q).wait()
+        gate(q, gain_ref[:, span(q - kept)])
         return carry
 
     lax.fori_loop(0, heads // 2, pair, 0, unroll=2)
-    lax.fori_loop(0, heads // 2, gate, 0)
+    lax.fori_loop(0, kept, near_gate, 0)
+    lax.fori_loop(kept, heads // 2, far_gate, 0)
     energy_ref[...] = jnp.sum(acc[...].T, axis=0, keepdims=True)
 
 
-def norm_kernel(gated_ref, mine_ref, other_ref, gain_ref, out_ref, held, sems):
-    inverse = lax.rsqrt((mine_ref[...] + other_ref[...]) / DI + EPSILON)
+def norm_kernel(gated_ref, mine_ref, core_ref, side_ref, cross_ref, gain_ref, out_ref, held, sems):
+    energy = (mine_ref[...] + core_ref[...]) + (side_ref[...] + cross_ref[...])
+    inverse = lax.rsqrt(energy / DI + EPSILON)
     copies = []
     for k in range(held.shape[0] // P_SIZE):
         rows = slice(k * P_SIZE, (k + 1) * P_SIZE)
@@ -451,14 +481,18 @@
 
     held = (input_map, output_map, frame_ids.reshape(1, tokens), row_sums, columns)
     held += (w_gate, pooled, early_keys, stream)
-    base, gain = call(
+    base, gain, gain_near = call(
         within_kernel,
         (skip.reshape(1, heads),) + outside(held),
-        [((tokens, width), f32, True), ((tokens, width), f32, True)],
+        [
+            ((tokens, width), f32, True),
+            ((tokens, width // 2), f32, True),
+            ((tokens, width // 2), f32),
+        ],
         [pltpu.VMEM(array.shape, array.dtype) for array in held]
         + [
             pltpu.VMEM((tokens, width), f32),
-            pltpu.VMEM((tokens, width), f32),
+            pltpu.VMEM((tokens, width // 2), f32),
             pltpu.VMEM((blocks, BLK, BLK), f32),
             pltpu.SemaphoreType.DMA((len(held),)),
             pltpu.SemaphoreType.DMA((2, heads // 2)),
@@ -478,22 +512,23 @@
 
     gated, energy = call(
         carry_kernel,
-        (incoming,) + outside((output_map, base, gain)),
+        (incoming, gain_near) + outside((output_map, base, gain)),
         [((tokens, width), f32), ((1, tokens), f32)],
         [
             pltpu.VMEM((tokens, N), bf16),
             pltpu.VMEM((tokens, width), f32),
-            pltpu.VMEM((tokens, width), f32),
+            pltpu.VMEM((tokens, width // 2), f32),
             pltpu.VMEM((tokens, P_SIZE), f32),
             pltpu.SemaphoreType.DMA((2, heads // 2 + 1)),
         ],
-        specs=[VMEM, HBM, HBM, HBM],
-    )
-    chip_energy = energy + swap(energy, "mp")
-    other_energy = swap(chip_energy, "section")
+        specs=[VMEM] * 2 + [HBM] * 3,
+    )
+    others = [
+        lax.ppermute(energy, ("section", "mp"), [(i, i ^ k) for i in range(4)]) for k in (1, 2, 3)
+    ]
     (out,) = call(
         norm_kernel,
-        (gated, chip_energy, other_energy, norm_gain),
+        (gated, energy, *others, norm_gain),
         [((tokens, width), bf16, True)],
         [pltpu.VMEM((tokens, width), bf16), pltpu.SemaphoreType.DMA((tokens // P_SIZE,))],
     )

time: 89.2 us -> 88.7 us (level)
  waiting for transfers between devices: 9.12 us -> 6.59 us
  Pallas kernels: 26.6 us -> 27.7 us
  starting transfers between devices: 14 us -> 15 us
    ppermute x0 -> x3, starting transfers between devices: none -> 6.98 us  [body(): lax.ppermute(energy, ('section', 'mp'), [(i, i ^ k) for i in range(4)])]
    ppermute x4 -> x2, starting transfers between devices: 9.45 us -> 3.42 us  [swap(): return lax.ppermute(value, axis, [(0, 1), (1, 0)])]
    ppermute x4 -> x2, waiting for transfers between devices: 6.84 us -> 3.98 us  [swap(): return lax.ppermute(value, axis, [(0, 1), (1, 0)])]
    ppermute x0 -> x3, waiting for transfers between devices: none -> 1.38 us  [body(): lax.ppermute(energy, ('section', 'mp'), [(i, i ^ k) for i in range(4)])]
    pallas_call x8, Pallas kernels: 26.6 us -> 27.7 us  [call(): pl.pallas_call(kernel, out_shape=[pltpu.HBM(*out[:2]) if out[2:] else jax...]
    all_to_all x1, waiting for transfers between devices: 2.27 us -> 1.23 us  [body(): lax.all_to_all(sent, 'ctx', 0, 0, axis_index_groups=groups, tiled=True)]
  transfers between devices with their start and end apart: 5 -> 6, of which waited for: 5 -> 5; matrix products, arithmetic and copies ran while one was open for 0% -> 0% of each run, Pallas kernels for 15% -> 16%
where the time goes in v9:
time: 88.7 us; the launch traced here: 88.5 us
  blocking collectives  39.1 us (44%)
  Pallas kernels  27.7 us (31%)
  starting transfers between devices  15 us (17%)
  waiting for transfers between devices  6.59 us (7%)
    pallas_call x8, Pallas kernels, call(): pl.pallas_call(kernel, out_shape=[pltpu.HBM(*out[:2]) if out[2:] else jax...  27.7 us
    all_to_all x1, blocking collectives, body(): got = lax.all_to_all(pay, 'ctx', 0, 0, axis_index_groups=groups, tiled=True)  23.6 us
    all_to_all x1, blocking collectives, body(): lax.all_to_all(total, 'ctx', 0, 0, axis_index_groups=peers, tiled=True)  15.5 us
    ppermute x3, starting transfers between devices, body(): lax.ppermute(energy, ('section', 'mp'), [(i, i ^ k) for i in range(4)])  6.98 us
    all_to_all x1, starting transfers between devices, body(): lax.all_to_all(sent, 'ctx', 0, 0, axis_index_groups=groups, tiled=True)  4.57 us
    ppermute x2, waiting for transfers between devices, swap(): return lax.ppermute(value, axis, [(0, 1), (1, 0)])  3.98 us
    ppermute x2, starting transfers between devices, swap(): return lax.ppermute(value, axis, [(0, 1), (1, 0)])  3.42 us
  transfers between devices with their start and end apart: 6, of which 5 were waited for; matrix products, arithmetic and copies ran while one was open for 0% of the time, Pallas kernels for 16%

profile of v9, /device:TPU:1, one launch (start us, length us, event | category | flops | bytes accessed | tf_op | source)
XLA Modules:
  0.0 88.5 jit_solution(3375925050088330993)
XLA Ops:
  0.0 3.2 %shard_map.118 = (f32[256,128]{1,0:T(8,128)S(1)}, f32[16,512]{1,0:T(8,128)S(1)}, bf16[512,128]{1,0:T(8,128)(2,1)S(1)}, bf16[64,2048]{1,0:T(8,128)(2,1)S(1)}, bf1...) custom-call(f32[41,1,256]{2,1,0:T(1,128)} %bitcast.10, s32[41,1,256]{2,1,0:T(1,128)} %bitcast.11, ...), custom_call_target="tpu_custom_call" | custom-call | tf_op jit(solution)/shard_map/pallas_call | solution.py:387
  3.2 3.3 %collective-permute-start = (f32[256,128]{1,0:T(8,128)S(1)}, f32[256,128]{1,0:T(8,128)S(1)}, u32[]{:S(2)}, u32[]{:S(2)}) collective-permute-start(f32[256,128]{1,0:T(8,128)S(1)} %get-tuple-element.27), channel_id=1, source_target_pairs={{0,1},{1,0},{2,3},{3,2},{4,5},{5,4},{6,7},{7,6},{8,9},{9,8},{10,11... | collective-permute-start | bytes 393224 | tf_op jit(solution)/shard_map/ppermute | solution.py:400
  6.6 1.0 %collective-permute-done = f32[256,128]{1,0:T(8,128)S(1)} collective-permute-done((f32[256,128]{1,0:T(8,128)S(1)}, f32[256,128]{1,0:T(8,128)S(1)}, u32[]{:S(2)}, u32[]{:S(2)}) %collective-permute-start) | collective-permute-done | bytes 131104 | tf_op jit(solution)/shard_map/ppermute | solution.py:400
  7.6 0.1 collective-permute-start.1
  7.7 1.7 %shard_map.119 = (bf16[2,16,128,256]{3,2,1,0:T(8,128)(2,1)S(1)}, f32[2,16,128]{2,1,0:T(8,128)S(1)}, bf16[512,144]{1,0:T(8,128)(2,1)}, f32[16,512]{1,0:T(8,128)}, bf16[16,128,256]{2,1,0:T(8,128)(2,1)}) custom-call(f32[16,512]{1,0:T(8,128)S(1)} %get-tuple-element.30.forget_ref, bf16[512,128]{1,0:T(8,128)(2,1)S(1)} %get-tuple-element.31.in_ref), custom_call_target="tpu_custom_call" | custom-call | tf_op jit(solution)/shard_map/pallas_call | solution.py:387
  9.4 3.0 %collective-permute-done.1.other_ref = f32[256,128]{1,0:T(8,128)S(1)} collective-permute-done((f32[256,128]{1,0:T(8,128)S(1)}, f32[256,128]{1,0:T(8,128)S(1)}, u32[]{:S(2)}, u32[]{:S(2)}) %collective-permute-start.1) | collective-permute-done | bytes 131104 | tf_op jit(solution)/shard_map/ppermute | solution.py:400
  12.4 3.0 %shard_map.120 = (f32[16,136,128]{2,1,0:T(8,128)S(1)}, bf16[512,2048]{1,0:T(8,128)(2,1)}, bf16[512,192]{1,0:T(8,128)(2,1)}) custom-call(f32[256,128]{1,0:T(8,128)S(1)} %add.4.mine_ref, f32[256,128]{1,0:T(8,128)S(1)} %collective-permute-done.1.other_ref, bf16[64,2048]{1,0:T(8,128)(2,1)S(1)} %get-tuple-element.28.w_ref, ...), custom_call_target="tpu_custom_call" | custom-call | tf_op jit(solution)/shard_map/pallas_call | solution.py:387
  15.4 23.6 %all_to_all.15.got_ref = f32[16,136,128]{2,1,0:T(8,128)S(1)} all-to-all(f32[16,136,128]{2,1,0:T(8,128)S(1)} %get-tuple-element.34), channel_id=1, replica_groups={{0,2,4,6,8,10,12,14,16,18,20,22,24,26,28,30},{32,34,36,38,40,42,44,46,4..., dimensions={0} | all-to-all | bytes 2228224 | tf_op jit(solution)/shard_map/all_to_all | solution.py:480
  38.9 0.1 shard_map.121
  39.0 15.5 %all_to_all.16.totals_ref = f32[4,136,128]{2,1,0:T(8,128)S(1)} all-to-all(f32[4,136,128]{2,1,0:T(8,128)S(1)} %shard_map.121), channel_id=1, replica_groups={{0,32,64,96},{2,34,66,98},{4,36,68,100},{6,38,70,102},{8,40,72,104},{10..., dimensions={0} | all-to-all | bytes 557056 | tf_op jit(solution)/shard_map/all_to_all | solution.py:504
  54.5 0.0 copy-start
  54.5 1.2 %shard_map.122 = f32[16,128,128]{2,1,0:T(8,128)} custom-call(f32[16,136,128]{2,1,0:T(8,128)S(1)} %all_to_all.15.got_ref, f32[4,136,128]{2,1,0:T(8,128)S(1)} %all_to_all.16.totals_ref, s32[1,128]{1,0:T(1,128)S(1)} %broadcast_in_dim.3.place_ref), custom_call_target="tpu_custom_call" | custom-call | tf_op jit(solution)/shard_map/pallas_call | solution.py:387
  55.7 4.6 %all-to-all-start.2 = ((f32[16,128,128]{2,1,0:T(8,128)}), f32[16,128,128]{2,1,0:T(8,128)S(1)}, u32[]{:S(2)}, u32[]{:S(2)}) async-start(f32[16,128,128]{2,1,0:T(8,128)} %shard_map.122), calls=%async_computation.2 | async-start | bytes 2097152 | tf_op jit(solution)/shard_map/all_to_all | solution.py:511
  60.3 0.0 copy-done
  60.3 12.4 %shard_map.123 = (f32[512,2048]{1,0:T(8,128)}, f32[512,1024]{1,0:T(8,128)}, f32[512,1024]{1,0:T(8,128)S(1)}) custom-call(f32[1,16]{1,0:T(1,128)S(1)} %bitcast.9, bf16[512,128]{1,0:T(8,128)(2,1)} %refs_0_.1, bf16[512,128]{1,0:T(8,128)(2,1)} %read_far.1, s32[1,512]{1,0:T(1,128)} %bitcast.15, f32[16,512]{1,0:T(8,128)} %get-tuple-element.36.refs_3_, ...), custom_call_target="tpu_custom_call" | custom-call | tf_op jit(solution)/shard_map/pallas_call | solution.py:387
  72.7 1.2 %all-to-all-done.2.state_ref = f32[16,128,128]{2,1,0:T(8,128)S(1)} async-done(((f32[16,128,128]{2,1,0:T(8,128)}), f32[16,128,128]{2,1,0:T(8,128)S(1)}, u32[]{:S(2)}, u32[]{:S(2)}) %all-to-all-start.2) | async-done | bytes 1048608 | tf_op jit(solution)/shard_map/all_to_all | solution.py:511
  74.0 4.0 %shard_map.124 = (f32[512,2048]{1,0:T(8,128)S(1)}, f32[1,512]{1,0:T(1,128)S(1)}) custom-call(f32[16,128,128]{2,1,0:T(8,128)S(1)} %all-to-all-done.2.state_ref, f32[512,1024]{1,0:T(8,128)S(1)} %get-tuple-element.41.gain_near, bf16[512,128]{1,0:T(8,128)(2,1)} %read_far.1, f32[512,2048]{1,0:T(8,128)} %get-tuple-element.42.base_far, ...), custom_call_target="tpu_custom_call" | custom-call | tf_op jit(solution)/shard_map/pallas_call | solution.py:387
  77.9 5.9 %collective-permute-start.4 = (f32[1,512]{1,0:T(1,128)S(1)}, f32[1,512]{1,0:T(1,128)S(1)}, u32[]{:S(2)}, u32[]{:S(2)}) collective-permute-start(f32[1,512]{1,0:T(1,128)S(1)} %get-tuple-element.45.mine_ref), channel_id=1, source_target_pairs={{0,129},{1,128},{128,1},{129,0},{2,131},{3,130},{130,3},{131,2},{4... | collective-permute-start | bytes 6152 | tf_op jit(solution)/shard_map/ppermute | solution.py:527
  83.9 1.1 %collective-permute-start.3 = (f32[1,512]{1,0:T(1,128)S(1)}, f32[1,512]{1,0:T(1,128)S(1)}, u32[]{:S(2)}, u32[]{:S(2)}) collective-permute-start(f32[1,512]{1,0:T(1,128)S(1)} %get-tuple-element.45.mine_ref), channel_id=1, source_target_pairs={{0,128},{1,129},{128,0},{129,1},{2,130},{3,131},{130,2},{131,3},{4... | collective-permute-start | bytes 6152 | tf_op jit(solution)/shard_map/ppermute | solution.py:527
  84.9 0.0 collective-permute-start.2
  84.9 0.2 collective-permute-done.4.cross_ref
  85.1 1.2 %collective-permute-done.3.side_ref = f32[1,512]{1,0:T(1,128)S(1)} collective-permute-done((f32[1,512]{1,0:T(1,128)S(1)}, f32[1,512]{1,0:T(1,128)S(1)}, u32[]{:S(2)}, u32[]{:S(2)}) %collective-permute-start.3) | collective-permute-done | bytes 2080 | tf_op jit(solution)/shard_map/ppermute | solution.py:527
  86.3 0.0 collective-permute-done.2.core_ref
  86.3 2.2 %shard_map.125 = bf16[512,2048]{1,0:T(8,128)(2,1)} custom-call(f32[512,2048]{1,0:T(8,128)S(1)} %get-tuple-element.44.gated_ref, f32[1,512]{1,0:T(1,128)S(1)} %get-tuple-element.45.mine_ref, f32[1,512]{1,0:T(1,128)S(1)} %collective-permute-done.2.core_ref, f32[1,512]{1,0:T(1,128)S(1)} %collective-permute-done.3.side_ref, ...), custom_call_target="tpu_custom_call" | custom-call | tf_op jit(solution)/shard_map/pallas_call | solution.py:387
  (2 shorter events, 0.0 us)
Async XLA Ops:
  3.2 4.3 %collective-permute-start = (f32[256,128]{1,0:T(8,128)S(1)}, f32[256,128]{1,0:T(8,128)S(1)}, u32[]{:S(2)}, u32[]{:S(2)}) collective-permute-start(f32[256,128]{1,0:T(8,128)S(1)} %get-tuple-element.27), channel_id=1, source_target_pairs={{0,1},{1,0},{2,3},{3,2},{4,5},{5,4},{6,7},{7,6},{8,9},{9,8},{10,11... | collective-permute-start | bytes 393224 | tf_op jit(solution)/shard_map/ppermute | solution.py:400
  7.6 4.8 %collective-permute-start.1 = (f32[256,128]{1,0:T(8,128)S(1)}, f32[256,128]{1,0:T(8,128)S(1)}, u32[]{:S(2)}, u32[]{:S(2)}) collective-permute-start(f32[256,128]{1,0:T(8,128)S(1)} %add.4.mine_ref), channel_id=1, source_target_pairs={{0,128},{128,0},{1,129},{129,1},{2,130},{130,2},{3,131},{131,3},{4... | collective-permute-start | bytes 393224 | tf_op jit(solution)/shard_map/ppermute | solution.py:400
  54.5 5.8 %copy-start = (f32[16]{0:T(128)S(1)}, f32[16]{0:T(128)}, u32[]{:S(2)}) copy-start(f32[16]{0:T(128)} %param.21) | copy-start | bytes 196
  55.7 18.2 %all-to-all-start.2 = ((f32[16,128,128]{2,1,0:T(8,128)}), f32[16,128,128]{2,1,0:T(8,128)S(1)}, u32[]{:S(2)}, u32[]{:S(2)}) async-start(f32[16,128,128]{2,1,0:T(8,128)} %shard_map.122), calls=%async_computation.2 | async-start | bytes 2097152 | tf_op jit(solution)/shard_map/all_to_all | solution.py:511
  77.9 7.2 %collective-permute-start.4 = (f32[1,512]{1,0:T(1,128)S(1)}, f32[1,512]{1,0:T(1,128)S(1)}, u32[]{:S(2)}, u32[]{:S(2)}) collective-permute-start(f32[1,512]{1,0:T(1,128)S(1)} %get-tuple-element.45.mine_ref), channel_id=1, source_target_pairs={{0,129},{1,128},{128,1},{129,0},{2,131},{3,130},{130,3},{131,2},{4... | collective-permute-start | bytes 6152 | tf_op jit(solution)/shard_map/ppermute | solution.py:527
  83.9 2.4 %collective-permute-start.3 = (f32[1,512]{1,0:T(1,128)S(1)}, f32[1,512]{1,0:T(1,128)S(1)}, u32[]{:S(2)}, u32[]{:S(2)}) collective-permute-start(f32[1,512]{1,0:T(1,128)S(1)} %get-tuple-element.45.mine_ref), channel_id=1, source_target_pairs={{0,128},{1,129},{128,0},{129,1},{2,130},{3,131},{130,2},{131,3},{4... | collective-permute-start | bytes 6152 | tf_op jit(solution)/shard_map/ppermute | solution.py:527
  84.9 1.4 %collective-permute-start.2 = (f32[1,512]{1,0:T(1,128)S(1)}, f32[1,512]{1,0:T(1,128)S(1)}, u32[]{:S(2)}, u32[]{:S(2)}) collective-permute-start(f32[1,512]{1,0:T(1,128)S(1)} %get-tuple-element.45.mine_ref), channel_id=1, source_target_pairs={{0,1},{1,0},{128,129},{129,128},{2,3},{3,2},{130,131},{131,130},{4... | collective-permute-start | bytes 6152 | tf_op jit(solution)/shard_map/ppermute | solution.py:527

commit v10 on v9

--- a/solution.py
+++ b/solution.py
@@ -271,8 +271,8 @@
         gain_result(q).wait()
         return carry
 
-    lax.fori_loop(0, kept, near_pair, 0)
-    lax.fori_loop(kept, heads // 2, far_pair, 0)
+    lax.fori_loop(0, kept, near_pair, 0, unroll=2)
+    lax.fori_loop(kept, heads // 2, far_pair, 0, unroll=2)
     lax.fori_loop(0, heads // 2, base_finish, 0)
     lax.fori_loop(kept, heads // 2, gain_finish, 0)
 
@@ -306,7 +306,7 @@
 
 
 def carry_kernel(
-    state_ref, gain_near, read_far, base_far, gain_far, gated_ref, energy_ref, read_ref, base_ref, gain_ref, acc, sems
+    state_ref, gain_near, read_ref, base_far, gain_far, gated_ref, energy_ref, base_ref, gain_ref, acc, sems
 ):
     heads = state_ref.shape[0]
     kept = gain_near.shape[1] // (2 * P_SIZE)
@@ -321,14 +321,11 @@
         lanes = span(q - kept)
         return pltpu.make_async_copy(gain_far.at[:, lanes], gain_ref.at[:, lanes], sems.at[1, q])
 
-    first = pltpu.make_async_copy(read_far, read_ref, sems.at[0, heads // 2])
-    first.start()
     for q in range(heads // 2):
         base(q).start()
         if q >= kept:
             gain(q).start()
     acc[...] = jnp.zeros_like(acc)
-    first.wait()
     read = read_ref[...]
     read_twice = jnp.concatenate([read, read], axis=1)
 
@@ -338,7 +335,6 @@
         return carry
 
     def gate(q, gains):
-        base(q).wait()
         gated = base_ref[:, span(q)] + gains * gated_ref[:, span(q)]
         gated_ref[:, span(q)] = gated
         squares = gated * gated
@@ -349,13 +345,17 @@
         return carry
 
     def far_gate(q, carry):
+        gate(q, gain_ref[:, span(q - kept)])
+        return carry
+
+    lax.fori_loop(0, heads // 2, pair, 0, unroll=2)
+    for q in range(kept):
+        base(q).wait()
+    lax.fori_loop(0, kept, near_gate, 0, unroll=2)
+    for q in range(kept, heads // 2):
+        base(q).wait()
         gain(q).wait()
-        gate(q, gain_ref[:, span(q - kept)])
-        return carry
-
-    lax.fori_loop(0, heads // 2, pair, 0, unroll=2)
-    lax.fori_loop(0, kept, near_gate, 0)
-    lax.fori_loop(kept, heads // 2, far_gate, 0)
+    lax.fori_loop(kept, heads // 2, far_gate, 0, unroll=2)
     energy_ref[...] = jnp.sum(acc[...].T, axis=0, keepdims=True)
 
 
@@ -424,8 +424,8 @@
     place = jnp.full((1, P_SIZE), lax.axis_index("ctx") // heads, jnp.int32)
 
     near = (depth_logits.transpose(2, 0, 1), cell_index.transpose(2, 0, 1), features[0].T)
-    far = (forget.T, input_map, w_visual, embed, norm_gain.reshape(1, width))
-    partial_sum, forget_t, writes, w_visual, embed, norm_gain = call(
+    far = (forget.T, input_map, w_visual, embed, norm_gain.reshape(1, width), output_map)
+    partial_sum, forget_t, writes, w_visual, embed, norm_gain, reads = call(
         pool_kernel,
         outside(near + far),
         [((tokens // 2, 2 * CF), f32)] + [(array.shape, array.dtype) for array in far],
@@ -512,16 +512,15 @@
 
     gated, energy = call(
         carry_kernel,
-        (incoming, gain_near) + outside((output_map, base, gain)),
+        (incoming, gain_near, reads) + outside((base, gain)),
         [((tokens, width), f32), ((1, tokens), f32)],
         [
-            pltpu.VMEM((tokens, N), bf16),
             pltpu.VMEM((tokens, width), f32),
             pltpu.VMEM((tokens, width // 2), f32),
             pltpu.VMEM((tokens, P_SIZE), f32),
-            pltpu.SemaphoreType.DMA((2, heads // 2 + 1)),
-        ],
-        specs=[VMEM] * 2 + [HBM] * 3,
+            pltpu.SemaphoreType.DMA((2, heads // 2)),
+        ],
+        specs=[VMEM] * 3 + [HBM] * 2,
     )
     others = [
         lax.ppermute(energy, ("section", "mp"), [(i, i ^ k) for i in range(4)]) for k in (1, 2, 3)

time: 88.7 us -> 88.7 us (level)
  Pallas kernels: 27.7 us -> 26.7 us
  waiting for transfers between devices: 6.59 us -> 7.56 us
    all_to_all x1, waiting for transfers between devices: 1.23 us -> 2.21 us  [body(): lax.all_to_all(sent, 'ctx', 0, 0, axis_index_groups=groups, tiled=True)]
    pallas_call x8, Pallas kernels: 27.7 us -> 26.7 us  [call(): pl.pallas_call(kernel, out_shape=[pltpu.HBM(*out[:2]) if out[2:] else jax...]
  transfers between devices with their start and end apart: 6 -> 6, of which waited for: 5 -> 5; matrix products, arithmetic and copies ran while one was open for 0% -> 0% of each run, Pallas kernels for 16% -> 15%
where the time goes in v10:
time: 88.7 us; the launch traced here: 88.5 us
  blocking collectives  39.1 us (44%)
  Pallas kernels  26.7 us (30%)
  starting transfers between devices  15 us (17%)
  waiting for transfers between devices  7.56 us (9%)
    pallas_call x8, Pallas kernels, call(): pl.pallas_call(kernel, out_shape=[pltpu.HBM(*out[:2]) if out[2:] else jax...  26.7 us
    all_to_all x1, blocking collectives, body(): got = lax.all_to_all(pay, 'ctx', 0, 0, axis_index_groups=groups, tiled=True)  23.6 us
    all_to_all x1, blocking collectives, body(): lax.all_to_all(total, 'ctx', 0, 0, axis_index_groups=peers, tiled=True)  15.5 us
    ppermute x3, starting transfers between devices, body(): lax.ppermute(energy, ('section', 'mp'), [(i, i ^ k) for i in range(4)])  6.98 us
    all_to_all x1, starting transfers between devices, body(): lax.all_to_all(sent, 'ctx', 0, 0, axis_index_groups=groups, tiled=True)  4.58 us
    ppermute x2, waiting for transfers between devices, swap(): return lax.ppermute(value, axis, [(0, 1), (1, 0)])  3.98 us
    ppermute x2, starting transfers between devices, swap(): return lax.ppermute(value, axis, [(0, 1), (1, 0)])  3.42 us
    all_to_all x1, waiting for transfers between devices, body(): lax.all_to_all(sent, 'ctx', 0, 0, axis_index_groups=groups, tiled=True)  2.21 us
  transfers between devices with their start and end apart: 6, of which 5 were waited for; matrix products, arithmetic and copies ran while one was open for 0% of the time, Pallas kernels for 15%

profile of v10, /device:TPU:1, one launch (start us, length us, event | category | flops | bytes accessed | tf_op | source)
XLA Modules:
  0.0 88.5 jit_solution(12830582593430697822)
XLA Ops:
  0.0 3.2 %shard_map.118 = (f32[256,128]{1,0:T(8,128)S(1)}, f32[16,512]{1,0:T(8,128)S(1)}, bf16[512,128]{1,0:T(8,128)(2,1)S(1)}, bf16[64,2048]{1,0:T(8,128)(2,1)S(1)}, bf1...) custom-call(f32[41,1,256]{2,1,0:T(1,128)} %bitcast.10, s32[41,1,256]{2,1,0:T(1,128)} %bitcast.11, ...), custom_call_target="tpu_custom_call" | custom-call | tf_op jit(solution)/shard_map/pallas_call | solution.py:387
  3.2 3.3 %collective-permute-start = (f32[256,128]{1,0:T(8,128)S(1)}, f32[256,128]{1,0:T(8,128)S(1)}, u32[]{:S(2)}, u32[]{:S(2)}) collective-permute-start(f32[256,128]{1,0:T(8,128)S(1)} %get-tuple-element.28), channel_id=1, source_target_pairs={{0,1},{1,0},{2,3},{3,2},{4,5},{5,4},{6,7},{7,6},{8,9},{9,8},{10,11... | collective-permute-start | bytes 393224 | tf_op jit(solution)/shard_map/ppermute | solution.py:400
  6.6 1.0 %collective-permute-done = f32[256,128]{1,0:T(8,128)S(1)} collective-permute-done((f32[256,128]{1,0:T(8,128)S(1)}, f32[256,128]{1,0:T(8,128)S(1)}, u32[]{:S(2)}, u32[]{:S(2)}) %collective-permute-start) | collective-permute-done | bytes 131104 | tf_op jit(solution)/shard_map/ppermute | solution.py:400
  7.6 0.1 collective-permute-start.1
  7.7 1.7 %shard_map.119 = (bf16[2,16,128,256]{3,2,1,0:T(8,128)(2,1)S(1)}, f32[2,16,128]{2,1,0:T(8,128)S(1)}, bf16[512,144]{1,0:T(8,128)(2,1)}, f32[16,512]{1,0:T(8,128)}, bf16[16,128,256]{2,1,0:T(8,128)(2,1)}) custom-call(f32[16,512]{1,0:T(8,128)S(1)} %get-tuple-element.31.forget_ref, bf16[512,128]{1,0:T(8,128)(2,1)S(1)} %get-tuple-element.32.in_ref), custom_call_target="tpu_custom_call" | custom-call | tf_op jit(solution)/shard_map/pallas_call | solution.py:387
  9.4 3.0 %collective-permute-done.1.other_ref = f32[256,128]{1,0:T(8,128)S(1)} collective-permute-done((f32[256,128]{1,0:T(8,128)S(1)}, f32[256,128]{1,0:T(8,128)S(1)}, u32[]{:S(2)}, u32[]{:S(2)}) %collective-permute-start.1) | collective-permute-done | bytes 131104 | tf_op jit(solution)/shard_map/ppermute | solution.py:400
  12.4 3.0 %shard_map.120 = (f32[16,136,128]{2,1,0:T(8,128)S(1)}, bf16[512,2048]{1,0:T(8,128)(2,1)}, bf16[512,192]{1,0:T(8,128)(2,1)}) custom-call(f32[256,128]{1,0:T(8,128)S(1)} %add.4.mine_ref, f32[256,128]{1,0:T(8,128)S(1)} %collective-permute-done.1.other_ref, bf16[64,2048]{1,0:T(8,128)(2,1)S(1)} %get-tuple-element.29.w_ref, ...), custom_call_target="tpu_custom_call" | custom-call | tf_op jit(solution)/shard_map/pallas_call | solution.py:387
  15.4 23.6 %all_to_all.15.got_ref = f32[16,136,128]{2,1,0:T(8,128)S(1)} all-to-all(f32[16,136,128]{2,1,0:T(8,128)S(1)} %get-tuple-element.35), channel_id=1, replica_groups={{0,2,4,6,8,10,12,14,16,18,20,22,24,26,28,30},{32,34,36,38,40,42,44,46,4..., dimensions={0} | all-to-all | bytes 2228224 | tf_op jit(solution)/shard_map/all_to_all | solution.py:480
  39.0 0.1 shard_map.121
  39.1 15.5 %all_to_all.16.totals_ref = f32[4,136,128]{2,1,0:T(8,128)S(1)} all-to-all(f32[4,136,128]{2,1,0:T(8,128)S(1)} %shard_map.121), channel_id=1, replica_groups={{0,32,64,96},{2,34,66,98},{4,36,68,100},{6,38,70,102},{8,40,72,104},{10..., dimensions={0} | all-to-all | bytes 557056 | tf_op jit(solution)/shard_map/all_to_all | solution.py:504
  54.5 0.0 copy-start
  54.5 1.2 %shard_map.122 = f32[16,128,128]{2,1,0:T(8,128)} custom-call(f32[16,136,128]{2,1,0:T(8,128)S(1)} %all_to_all.15.got_ref, f32[4,136,128]{2,1,0:T(8,128)S(1)} %all_to_all.16.totals_ref, s32[1,128]{1,0:T(1,128)S(1)} %broadcast_in_dim.3.place_ref), custom_call_target="tpu_custom_call" | custom-call | tf_op jit(solution)/shard_map/pallas_call | solution.py:387
  55.7 4.6 %all-to-all-start.2 = ((f32[16,128,128]{2,1,0:T(8,128)}), f32[16,128,128]{2,1,0:T(8,128)S(1)}, u32[]{:S(2)}, u32[]{:S(2)}) async-start(f32[16,128,128]{2,1,0:T(8,128)} %shard_map.122), calls=%async_computation.2 | async-start | bytes 2097152 | tf_op jit(solution)/shard_map/all_to_all | solution.py:511
  60.3 0.0 copy-done
  60.3 11.4 %shard_map.123 = (f32[512,2048]{1,0:T(8,128)}, f32[512,1024]{1,0:T(8,128)}, f32[512,1024]{1,0:T(8,128)S(1)}) custom-call(f32[1,16]{1,0:T(1,128)S(1)} %bitcast.9, bf16[512,128]{1,0:T(8,128)(2,1)} %refs_0_.1, bf16[512,128]{1,0:T(8,128)(2,1)} %refs_1_.1, s32[1,512]{1,0:T(1,128)} %bitcast.15, f32[16,512]{1,0:T(8,128)} %get-tuple-element.37.refs_3_, ...), custom_call_target="tpu_custom_call" | custom-call | tf_op jit(solution)/shard_map/pallas_call | solution.py:387
  71.8 2.2 %all-to-all-done.2.state_ref = f32[16,128,128]{2,1,0:T(8,128)S(1)} async-done(((f32[16,128,128]{2,1,0:T(8,128)}), f32[16,128,128]{2,1,0:T(8,128)S(1)}, u32[]{:S(2)}, u32[]{:S(2)}) %all-to-all-start.2) | async-done | bytes 1048608 | tf_op jit(solution)/shard_map/all_to_all | solution.py:511
  74.0 4.0 %shard_map.124 = (f32[512,2048]{1,0:T(8,128)S(1)}, f32[1,512]{1,0:T(1,128)S(1)}) custom-call(f32[16,128,128]{2,1,0:T(8,128)S(1)} %all-to-all-done.2.state_ref, f32[512,1024]{1,0:T(8,128)S(1)} %get-tuple-element.42.gain_near, bf16[512,128]{1,0:T(8,128)(2,1)S(1)} %get-tuple-element.43.read_ref, f32[512,2048]{1,0:T(8,128)} %get-tuple-element.44.base_far, ...), custom_call_target="tpu_custom_call" | custom-call | tf_op jit(solution)/shard_map/pallas_call | solution.py:387
  77.9 5.9 %collective-permute-start.4 = (f32[1,512]{1,0:T(1,128)S(1)}, f32[1,512]{1,0:T(1,128)S(1)}, u32[]{:S(2)}, u32[]{:S(2)}) collective-permute-start(f32[1,512]{1,0:T(1,128)S(1)} %get-tuple-element.47.mine_ref), channel_id=1, source_target_pairs={{0,129},{1,128},{128,1},{129,0},{2,131},{3,130},{130,3},{131,2},{4... | collective-permute-start | bytes 6152 | tf_op jit(solution)/shard_map/ppermute | solution.py:526
  83.9 1.1 %collective-permute-start.3 = (f32[1,512]{1,0:T(1,128)S(1)}, f32[1,512]{1,0:T(1,128)S(1)}, u32[]{:S(2)}, u32[]{:S(2)}) collective-permute-start(f32[1,512]{1,0:T(1,128)S(1)} %get-tuple-element.47.mine_ref), channel_id=1, source_target_pairs={{0,128},{1,129},{128,0},{129,1},{2,130},{3,131},{130,2},{131,3},{4... | collective-permute-start | bytes 6152 | tf_op jit(solution)/shard_map/ppermute | solution.py:526
  84.9 0.0 collective-permute-start.2
  84.9 0.2 collective-permute-done.4.cross_ref
  85.1 1.2 %collective-permute-done.3.side_ref = f32[1,512]{1,0:T(1,128)S(1)} collective-permute-done((f32[1,512]{1,0:T(1,128)S(1)}, f32[1,512]{1,0:T(1,128)S(1)}, u32[]{:S(2)}, u32[]{:S(2)}) %collective-permute-start.3) | collective-permute-done | bytes 2080 | tf_op jit(solution)/shard_map/ppermute | solution.py:526
  86.3 0.0 collective-permute-done.2.core_ref
  86.3 2.2 %shard_map.125 = bf16[512,2048]{1,0:T(8,128)(2,1)} custom-call(f32[512,2048]{1,0:T(8,128)S(1)} %get-tuple-element.46.gated_ref, f32[1,512]{1,0:T(1,128)S(1)} %get-tuple-element.47.mine_ref, f32[1,512]{1,0:T(1,128)S(1)} %collective-permute-done.2.core_ref, f32[1,512]{1,0:T(1,128)S(1)} %collective-permute-done.3.side_ref, ...), custom_call_target="tpu_custom_call" | custom-call | tf_op jit(solution)/shard_map/pallas_call | solution.py:387
  (2 shorter events, 0.0 us)
Async XLA Ops:
  3.2 4.3 %collective-permute-start = (f32[256,128]{1,0:T(8,128)S(1)}, f32[256,128]{1,0:T(8,128)S(1)}, u32[]{:S(2)}, u32[]{:S(2)}) collective-permute-start(f32[256,128]{1,0:T(8,128)S(1)} %get-tuple-element.28), channel_id=1, source_target_pairs={{0,1},{1,0},{2,3},{3,2},{4,5},{5,4},{6,7},{7,6},{8,9},{9,8},{10,11... | collective-permute-start | bytes 393224 | tf_op jit(solution)/shard_map/ppermute | solution.py:400
  7.6 4.8 %collective-permute-start.1 = (f32[256,128]{1,0:T(8,128)S(1)}, f32[256,128]{1,0:T(8,128)S(1)}, u32[]{:S(2)}, u32[]{:S(2)}) collective-permute-start(f32[256,128]{1,0:T(8,128)S(1)} %add.4.mine_ref), channel_id=1, source_target_pairs={{0,128},{128,0},{1,129},{129,1},{2,130},{130,2},{3,131},{131,3},{4... | collective-permute-start | bytes 393224 | tf_op jit(solution)/shard_map/ppermute | solution.py:400
  54.5 5.8 %copy-start = (f32[16]{0:T(128)S(1)}, f32[16]{0:T(128)}, u32[]{:S(2)}) copy-start(f32[16]{0:T(128)} %param.21) | copy-start | bytes 196
  55.7 18.2 %all-to-all-start.2 = ((f32[16,128,128]{2,1,0:T(8,128)}), f32[16,128,128]{2,1,0:T(8,128)S(1)}, u32[]{:S(2)}, u32[]{:S(2)}) async-start(f32[16,128,128]{2,1,0:T(8,128)} %shard_map.122), calls=%async_computation.2 | async-start | bytes 2097152 | tf_op jit(solution)/shard_map/all_to_all | solution.py:511
  77.9 7.2 %collective-permute-start.4 = (f32[1,512]{1,0:T(1,128)S(1)}, f32[1,512]{1,0:T(1,128)S(1)}, u32[]{:S(2)}, u32[]{:S(2)}) collective-permute-start(f32[1,512]{1,0:T(1,128)S(1)} %get-tuple-element.47.mine_ref), channel_id=1, source_target_pairs={{0,129},{1,128},{128,1},{129,0},{2,131},{3,130},{130,3},{131,2},{4... | collective-permute-start | bytes 6152 | tf_op jit(solution)/shard_map/ppermute | solution.py:526
  83.9 2.4 %collective-permute-start.3 = (f32[1,512]{1,0:T(1,128)S(1)}, f32[1,512]{1,0:T(1,128)S(1)}, u32[]{:S(2)}, u32[]{:S(2)}) collective-permute-start(f32[1,512]{1,0:T(1,128)S(1)} %get-tuple-element.47.mine_ref), channel_id=1, source_target_pairs={{0,128},{1,129},{128,0},{129,1},{2,130},{3,131},{130,2},{131,3},{4... | collective-permute-start | bytes 6152 | tf_op jit(solution)/shard_map/ppermute | solution.py:526
  84.9 1.4 %collective-permute-start.2 = (f32[1,512]{1,0:T(1,128)S(1)}, f32[1,512]{1,0:T(1,128)S(1)}, u32[]{:S(2)}, u32[]{:S(2)}) collective-permute-start(f32[1,512]{1,0:T(1,128)S(1)} %get-tuple-element.47.mine_ref), channel_id=1, source_target_pairs={{0,1},{1,0},{128,129},{129,128},{2,3},{3,2},{130,131},{131,130},{4... | collective-permute-start | bytes 6152 | tf_op jit(solution)/shard_map/ppermute | solution.py:526
